TPU v7x, 128 devices: a whole 4x4x4 slice. The times are simulated.
128 devices in a mesh: group: 64 (over z, y, x), kv: 2 (over core).
Axes of the slice: x: 4, y: 4, z: 4, core: 2. Of those that a mesh axis runs over, the one named last changes fastest.
Arguments:
- lengths: int32 [64], P('group'), may hold values from 2048 to 8192, as said below
- latents: bfloat16 [64, 8192, 160], P('group', 'kv'), may hold values from -6 to 6
- codes: bfloat16 [64, 8192, 1024], P('group', 'kv'), may hold values from -10 to 10
- scales: bfloat16 [64, 32, 8], P('group', 'kv'), may hold values from 0.5 to 4
- queries: bfloat16 [64, 8, 8192], P('group'), may hold values from -900 to 900
- new_keys: bfloat16 [64, 8, 1024], P('group'), may hold values from -8 to 8
- new_values: bfloat16 [64, 8, 1024], P('group'), may hold values from -12 to 12
- key_factor: bfloat16 [160, 1024], replicated, may hold values from -0.5 to 0.5
- out_weight: bfloat16 [8192, 8192], P('kv', 'group'), may hold values from -0.0625 to 0.0625
Outputs:
- layer_out: float32 [512, 8192], P('kv', 'group')
Inputs may be any that keep to these rules, and one draw needn't show every extreme that they name: `lengths`: one request has exactly 8192 cached tokens and one exactly 2048.
All inputs are finite; a program needn't handle non-finite values.
Results may differ from a plain program's by a relative error of at most 0.0087.
Values may be sent and summed in bfloat16 or wider, within the bound.
No kernel may reach another device: no remote copies, remote signals or barrier semaphores. Data moves between devices by JAX's collectives and lax.ppermute only.
A program may use at most 128 MiB of HBM per device.

v0:
```python
import jax
import jax.numpy as jnp
from jax import lax
from jax.sharding import PartitionSpec as P

HEADS = 64
KV_HEADS = 8
HEAD_DIM = 128
BLK = 256
CTX_DEV = 4096
Q_TOK = 8


ROPE_BASE = 500000.0
NEG_FILL = -1e30


def merged(shard, axis, combine):
    everything = jax.tree.map(lambda part: lax.all_gather(part, axis), shard)
    initial = jax.tree.map(lambda part: part[0], everything)

    def lap(k, so_far):
        return combine(so_far, jax.tree.map(lambda part: part[k], everything))

    return lax.fori_loop(1, lax.axis_size(axis), lap, initial)


def rotate(key_before_rotary, positions):
    half_dim = HEAD_DIM // 2
    frequency = ROPE_BASE ** (-(jnp.arange(half_dim, dtype=jnp.float32) * 2.0) / HEAD_DIM)
    angles = positions.astype(jnp.float32)[:, None] * frequency[None, :]
    cosine = jnp.cos(angles)[:, None, :]
    sine_val = jnp.sin(angles)[:, None, :]
    lower_half = key_before_rotary[..., :half_dim]
    upper_half = key_before_rotary[..., half_dim:]
    return jnp.concatenate(
        [lower_half * cosine - upper_half * sine_val, upper_half * cosine + lower_half * sine_val],
        axis=-1,
    )


def attend_block(
    carried, latent, code_rows, scale_row, query_matrix_rows, key_factor, start_pos, length
):
    peak_score, totals, numerator = carried
    key_before_rotary = jnp.dot(latent, key_factor, preferred_element_type=jnp.float32).reshape(
        BLK, KV_HEADS, HEAD_DIM
    )
    positions = start_pos + jnp.arange(BLK, dtype=jnp.int32)
    rotary_applied = rotate(key_before_rotary, positions).astype(jnp.bfloat16)
    scores = jnp.einsum(
        "onvs,xns->onvx", query_matrix_rows, rotary_applied, preferred_element_type=jnp.float32
    ) * HEAD_DIM ** (-0.5)
    valid_mask = (positions < length)[None, None, None, :]
    scores = jnp.where(valid_mask, scores, NEG_FILL)
    new_peak = jnp.maximum(peak_score, jnp.max(scores, axis=-1))
    shrink_by = jnp.exp(peak_score - new_peak)
    weights = jnp.where(valid_mask, jnp.exp(scores - new_peak[..., None]), 0.0)
    totals = totals * shrink_by + jnp.sum(weights, axis=-1)
    value_rows = code_rows.reshape(BLK, KV_HEADS, HEAD_DIM)
    block_part = jnp.einsum(
        "lahy,yaw->lahw",
        weights.astype(jnp.bfloat16),
        value_rows,
        preferred_element_type=jnp.float32,
    )
    numerator = (
        numerator * shrink_by[..., None]
        + block_part * scale_row.astype(jnp.float32)[None, :, None, None]
    )
    return (new_peak, totals, numerator)


def run_blocks(
    carried,
    latent,
    code_rows,
    scale_rows,
    query_matrix_rows,
    key_factor,
    block_count,
    base_pos,
    length,
):

    def advance(block_index, state_now):
        lat_block = lax.dynamic_slice_in_dim(latent, block_index * BLK, BLK, 0)
        code_block = lax.dynamic_slice_in_dim(code_rows, block_index * BLK, BLK, 0)
        scale_block = lax.dynamic_index_in_dim(scale_rows, block_index, 0, keepdims=False)
        return attend_block(
            state_now,
            lat_block,
            code_block,
            scale_block,
            query_matrix_rows,
            key_factor,
            base_pos + block_index * BLK,
            length,
        )

    return lax.fori_loop(0, block_count, advance, carried)


def live_blocks(length, owner_index):
    filled = jnp.clip(length - owner_index * CTX_DEV, 0, CTX_DEV)
    return (filled + BLK - 1) // BLK


def combine_triples(first_triple, second_triple):
    peak_a, total_a, numer_a = first_triple
    peak_b, total_b, numer_b = second_triple
    joint_peak = jnp.maximum(peak_a, peak_b)
    weight_a = jnp.exp(peak_a - joint_peak)
    weight_b = jnp.exp(peak_b - joint_peak)
    return (
        joint_peak,
        total_a * weight_a + total_b * weight_b,
        numer_a * weight_a[..., None] + numer_b * weight_b[..., None],
    )


def body(lengths, latents, codes, scales, queries, new_keys, new_values, key_factor, out_weight):
    kv_count = lax.axis_size("kv")
    kv_at = lax.axis_index("kv")
    groups = HEADS // KV_HEADS
    requests = latents.shape[0]
    heads_dev = HEADS // kv_count
    query_full_set = queries.reshape(requests, Q_TOK, KV_HEADS, groups, HEAD_DIM)
    order_mask = jnp.arange(Q_TOK)[None, :] <= jnp.arange(Q_TOK)[:, None]
    causal = jnp.logical_and(order_mask[:, None, None, :], kv_at == 0)
    query_matrix_rows = query_full_set[0]
    fresh_keys = new_keys[0].reshape(Q_TOK, KV_HEADS, HEAD_DIM)
    fresh_vals = new_values[0].reshape(Q_TOK, KV_HEADS, HEAD_DIM)
    fresh_scores = jnp.einsum(
        "tkgd,ukd->tkgu", query_matrix_rows, fresh_keys, preferred_element_type=jnp.float32
    ) * HEAD_DIM ** (-0.5)
    fresh_scores = jnp.where(causal, fresh_scores, NEG_FILL)
    start_peak = jnp.max(fresh_scores, axis=-1)
    fresh_weights = jnp.where(causal, jnp.exp(fresh_scores - start_peak[..., None]), 0.0)
    start_total = jnp.sum(fresh_weights, axis=-1)
    start_numer = jnp.einsum(
        "tkgu,ukd->tkgd",
        fresh_weights.astype(jnp.bfloat16),
        fresh_vals,
        preferred_element_type=jnp.float32,
    )
    state_now = (start_peak, start_total, start_numer)
    length = lengths[0]
    own_count = live_blocks(length, kv_at)
    state_now = run_blocks(
        state_now,
        latents[0],
        codes[0],
        scales[0],
        query_matrix_rows,
        key_factor,
        own_count,
        kv_at * CTX_DEV,
        length,
    )
    states = [state_now]
    peaks = jnp.stack([triple[0] for triple in states])
    totals = jnp.stack([triple[1] for triple in states])
    numerator = jnp.stack([triple[2] for triple in states])
    merged_peak, merged_total, merged_numer = merged(
        (peaks, totals, numerator), "kv", combine_triples
    )
    merged_total = merged_total.reshape(requests, Q_TOK, HEADS)
    merged_numer = merged_numer.reshape(requests, Q_TOK, HEADS, HEAD_DIM)
    totals_dev = lax.dynamic_slice_in_dim(merged_total, kv_at * heads_dev, heads_dev, 2)
    numer_dev = lax.dynamic_slice_in_dim(merged_numer, kv_at * heads_dev, heads_dev, 2)
    attended = (
        (numer_dev / totals_dev[..., None])
        .astype(jnp.bfloat16)
        .reshape(requests * Q_TOK, heads_dev * HEAD_DIM)
    )
    all_rows = lax.all_gather(attended, "group", axis=0, tiled=True)
    return lax.psum_scatter(
        jnp.dot(all_rows, out_weight, preferred_element_type=jnp.float32),
        "kv",
        scatter_dimension=0,
        tiled=True,
    )


def solution(mesh):
    placed = (
        P("group"),
        P("group", "kv", None),
        P("group", "kv", None),
        P("group", "kv", None),
        P("group", None, None),
        P("group", None, None),
        P("group", None, None),
        P(),
        P("kv", "group"),
    )
    return jax.shard_map(
        body, mesh=mesh, in_specs=placed, out_specs=P("kv", "group"), check_vma=False
    )
```

profile of v0, /device:TPU:1, one launch (start us, length us, event | category | flops | bytes accessed | tf_op | source)
XLA Modules:
  0.0 233.4 jit_solution(2071748687305617957)
XLA Ops:
  8.2 1.6 fusion.48
  11.7 11.5 %copy.37 = bf16[1,4096,1024]{1,2,0:T(8,128)(2,1)} copy(bf16[1,4096,1024]{2,1,0:T(8,128)(2,1)} %param.13) | data formatting | bytes 16777216 | tf_op args[2]
  23.3 2.4 %copy.36 = bf16[1,4096,160]{2,1,0:T(8,128)(2,1)} copy(bf16[1,4096,160]{1,2,0:T(8,128)(2,1)S(1)} %copy-done.1) | data formatting | bytes 2621440 | tf_op args[1]
  25.8 74.5 %while.2 = (s32[]{:T(128)}, f32[8,8,8]{2,0,1:T(8,128)S(1)}, f32[8,8,8]{2,0,1:T(8,128)S(1)}, f32[8,8,8,128]{3,2,0,1:T(8,128)S(1)}, s32[]{:T(128)}, /*index=5*/s32...) while((s32[]{:T(128)}, f32[8,8,8]{2,0,1:T(8,128)S(1)}, ...), condition=%wide.region_5.6_spmd, body=%wide.region_2.5_spmd.sunk | while | flops 154486992 | bytes 11898721 | solution.py:101
  29.3 1.4 fusion.75
  32.6 1.3 convolution_bitcast_fusion.3
  36.1 1.4 fusion.75
  39.3 1.3 convolution_bitcast_fusion.3
  42.9 1.4 fusion.75
  46.1 1.3 convolution_bitcast_fusion.3
  49.6 1.4 fusion.75
  56.4 1.4 fusion.75
  63.2 1.4 fusion.75
  70.0 1.4 fusion.75
  76.8 1.4 fusion.75
  83.5 1.4 fusion.75
  90.3 1.4 fusion.75
  97.1 1.4 fusion.75
  100.3 36.8 %all-gather.1 = f32[16,8,8]{2,0,1:T(8,128)S(1)} all-gather(f32[8,8,8]{2,0,1:T(8,128)S(1)} %get-tuple-element.95), channel_id=3, replica_groups=mesh['group'=64,'kv'=2] {'kv'}, dimensions={0}, use_global_device_ids=true | all-gather | bytes 6144 | tf_op jit(solution)/shard_map/all_gather | solution.py:19
  137.5 2.2 all-gather
  139.7 1.9 all-gather.2
  142.9 70.2 %all-gather.5.cloned.1.call-done = bf16[512,4096]{1,0:T(8,128)(2,1)} async-done(((bf16[8,4096]{1,0:T(8,128)(2,1)}), bf16[512,4096]{1,0:T(8,128)(2,1)}) %all-gather.5.cloned.1.call-update) | async-done | bytes 4194320 | tf_op jit(solution)/shard_map/all_gather | solution.py:177
  213.1 4.2 %fusion.49 = f32[512,128]{1,0:T(8,128)} fusion(bf16[512,4096]{1,0:T(8,128)(2,1)} %all-gather.5.cloned.1.call-done, bf16[4096,128]{1,0:T(8,128)(2,1)S(1)} %copy-done), kind=kOutput, calls=%fused_computation.79 | convolution fusion | flops 536870912 | bytes 5505024 | tf_op jit(solution)/shard_map/dot_general | solution.py:179
  217.3 9.3 %reduce-scatter.2.cloned.1.call-done = f32[256,128]{1,0:T(8,128)} async-done(((f32[512,128]{1,0:T(8,128)}), f32[256,128]{1,0:T(8,128)}) %reduce-scatter.2.cloned.1.call-update) | async-done | bytes 131088 | tf_op jit(solution)/shard_map/reduce_scatter | solution.py:178
  (198 shorter events, 58.1 us)
Async XLA Ops:
  6.5 206.5 %copy-start = (bf16[4096,128]{1,0:T(8,128)(2,1)S(1)}, bf16[4096,128]{1,0:T(8,128)(2,1)}, u32[]{:S(2)}) copy-start(bf16[4096,128]{1,0:T(8,128)(2,1)} %param.19) | copy-start | bytes 3145732
  6.5 206.5 %all-gather.5.cloned.1.call-start = ((), (), s32[]{:S(2)}) async-start(), calls=%async_computation.1 | async-start | bytes 4259840 | tf_op jit(solution)/shard_map/all_gather | solution.py:177
  11.7 11.5 %copy-start.1 = (bf16[1,4096,160]{1,2,0:T(8,128)(2,1)S(1)}, bf16[1,4096,160]{1,2,0:T(8,128)(2,1)}, u32[]{:S(2)}) copy-start(bf16[1,4096,160]{1,2,0:T(8,128)(2,1)} %param.12) | copy-start | bytes 3932164
  11.7 13.9 %copy-start.2 = (bf16[1,16,8]{1,2,0:T(8,128)(2,1)S(1)}, bf16[1,16,8]{1,2,0:T(8,128)(2,1)}, u32[]{:S(2)}) copy-start(bf16[1,16,8]{1,2,0:T(8,128)(2,1)} %param.14) | copy-start | bytes 772
  142.8 83.7 %reduce-scatter.2.cloned.1.call-start = ((), (), s32[]{:S(2)}) async-start(), calls=%async_computation.2 | async-start | bytes 393216 | tf_op jit(solution)/shard_map/reduce_scatter | solution.py:178
Sparse Core Ops, SparseCore 0:
  142.9 70.0 all-gather.4
  217.4 9.0 reduce-scatter.1
where the time goes:
time: 235 us; the launch traced here: 233 us
  waiting for transfers between devices  79.5 us (34%)
  matrix products  41 us (17%)
  blocking collectives  40.9 us (17%)
  local copies, waits for them, and re-layouts  34.9 us (15%)
  other arithmetic  21.4 us (9%)
  between operations  14.3 us (6%)
    all_gather x1, waiting for transfers between devices, body(): all_rows = lax.all_gather(attended, 'group', axis=0, tiled=True)  70.2 us
    all_gather x3, blocking collectives, merged(): everything = jax.tree.map(lambda part: lax.all_gather(part, axis), shard)  40.9 us
    dot_general x11, matrix products, attend_block(): jnp.einsum('onvs,xns->onvx', query_matrix_rows, rotary_applied, preferred...  15.6 us
    unnamed x10, local copies, waits for them, and re-layouts  15.5 us
    dot_general x11, matrix products, attend_block(): jnp.dot(latent, key_factor, preferred_element_type=jnp.float32)  14.7 us
    dynamic_slice x11, local copies, waits for them, and re-layouts, advance(): code_block = lax.dynamic_slice_in_dim(code_rows, block_index * BLK, BLK, 0)  11.9 us
    reduce_scatter x1, waiting for transfers between devices, body(): lax.psum_scatter(jnp.dot(all_rows, out_weight, preferred_element_type=jnp...  9.26 us
    lt x11, other arithmetic, attend_block(): valid_mask = (positions < length)[None, None, None, :]  7.18 us
  transfers between devices with their start and end apart: 2, of which 2 were waited for; matrix products, arithmetic and copies ran while one was open for 0% of the time, Pallas kernels for 0%

commit v1 on v0

v1 whole, which is shorter than its diff:
```python
import functools

import jax
import jax.numpy as jnp
import numpy as np
from jax import lax
from jax.experimental import pallas as pl
from jax.experimental.pallas import tpu as pltpu
from jax.sharding import PartitionSpec as P

HEADS = 64
KV_HEADS = 8
HEAD_DIM = 128
HALF = HEAD_DIM // 2
RANK = 160
BLK = 256
CTX_DEV = 4096
Q_TOK = 8
PAIRS = KV_HEADS // 2
ROWS = 2 * (HEADS // KV_HEADS) * Q_TOK
CHUNK = 512
N_CHUNKS = CTX_DEV // CHUNK
ROPE_BASE = 500000.0
NEG_FILL = -1e30
EXP2_SCALE = float(HEAD_DIM**-0.5 * np.log2(np.e))


def rotary_tables():
    freq = np.float32(ROPE_BASE) ** (-(np.arange(HALF, dtype=np.float32) * 2.0) / HEAD_DIM)
    freq = np.tile(freq.astype(np.float32), 2).astype(np.float64)[None, :]
    inner = np.arange(BLK, dtype=np.float64)[:, None] * freq
    outer = np.arange(0, 2 * CTX_DEV, BLK, dtype=np.float64)[:, None] * freq
    return [f(a).astype(np.float32) for a in (inner, outer) for f in (np.cos, np.sin)]


def swap_halves(x):
    return pltpu.roll(x, HALF, 1)


def low_lanes(shape):
    return lax.broadcasted_iota(jnp.int32, shape, 1) < HALF


def pair_columns(even, odd):
    low = low_lanes(even.shape)
    return (
        jnp.where(low, even, swap_halves(odd)),
        jnp.where(low, swap_halves(even), odd),
    )


def attend_kernel(
    length_ref, lat_hbm, code_hbm, scale_ref, q_ref, nk_ref, nv_ref, kf_ref,
    cos_in, sin_in, cos_out, sin_out,
    mine_ref, send_ref,
    lat_buf, code_buf, lat_sem, code_sem, qc, wp, scale_rows, peak, total, numer,
):
    f32, bf16 = jnp.float32, jnp.bfloat16
    kv_at = lax.axis_index("kv")
    valid = jnp.clip(length_ref[0] - kv_at * CTX_DEV, 0, CTX_DEV)
    chunks = lax.div(valid + (CHUNK - 1), CHUNK)

    def copies(c):
        rows = pl.ds(pl.multiple_of(c * CHUNK, CHUNK), CHUNK)
        return (
            pltpu.make_async_copy(lat_hbm.at[rows], lat_buf.at[rows], lat_sem.at[c]),
            pltpu.make_async_copy(code_hbm.at[rows], code_buf.at[rows], code_sem.at[c]),
        )

    @pl.loop(0, chunks)
    def _(c):
        for copy in copies(c):
            copy.start()

    scales = scale_ref[...].astype(f32)
    for k in range(KV_HEADS):
        scale_rows[k] = jnp.broadcast_to(scales[:, k : k + 1], (CTX_DEV // BLK, HEAD_DIM))

    row_tok = lax.rem(lax.broadcasted_iota(jnp.int32, (ROWS, HEAD_DIM), 0), Q_TOK)
    lane = lax.broadcasted_iota(jnp.int32, (ROWS, HEAD_DIM), 1)
    causal = jnp.logical_and(lane <= row_tok, kv_at == 0)
    queries = q_ref[...].astype(f32)
    kf = kf_ref[...].astype(f32)
    new_keys = nk_ref[...].astype(f32)
    new_values = nv_ref[...].astype(f32)
    pad = jnp.zeros((HEAD_DIM - Q_TOK, 2 * HEAD_DIM), f32)

    def head_rows(k):
        groups = HEADS // KV_HEADS
        return jnp.concatenate(
            [queries[:, (k * groups + g) * HEAD_DIM : (k * groups + g + 1) * HEAD_DIM] for g in range(groups)],
            axis=0,
        )

    def two_heads(x, j):
        return (
            x[:, 2 * j * HEAD_DIM : (2 * j + 1) * HEAD_DIM],
            x[:, (2 * j + 1) * HEAD_DIM : (2 * j + 2) * HEAD_DIM],
        )

    def own_blocks(x):
        return jnp.concatenate([x[: ROWS // 2, :HEAD_DIM], x[ROWS // 2 :, HEAD_DIM:]], axis=0)

    def scores(a, b):
        return lax.dot_general(a, b, (((1,), (1,)), ((), ())), preferred_element_type=f32)

    for j in range(PAIRS):
        even, odd = head_rows(2 * j), head_rows(2 * j + 1)
        low = low_lanes(even.shape)
        qc[j] = jnp.concatenate(
            [
                jnp.concatenate(
                    [jnp.where(low, even, 0.0), jnp.where(low, swap_halves(even), 0.0)], axis=1
                ),
                jnp.concatenate(
                    [jnp.where(low, 0.0, swap_halves(odd)), jnp.where(low, 0.0, odd)], axis=1
                ),
            ],
            axis=0,
        ).astype(bf16)
        wp[:, 2 * j * HEAD_DIM : (2 * j + 2) * HEAD_DIM] = jnp.concatenate(
            pair_columns(*two_heads(kf, j)), axis=1
        ).astype(bf16)

        fresh_keys = jnp.concatenate(pair_columns(*two_heads(new_keys, j)), axis=1)
        fresh_keys = jnp.concatenate([fresh_keys, pad], axis=0).astype(bf16)
        fresh_values = jnp.concatenate(
            [new_values[:, 2 * j * HEAD_DIM : (2 * j + 2) * HEAD_DIM], pad], axis=0
        ).astype(bf16)
        s = jnp.where(causal, scores(qc[j], fresh_keys), NEG_FILL)
        top = jnp.broadcast_to(jnp.max(s, axis=1, keepdims=True), s.shape)
        weights = jnp.where(causal, jnp.exp2((s - top) * EXP2_SCALE), 0.0)
        peak[j] = top
        total[j] = weights
        numer[j] = own_blocks(
            jnp.dot(weights.astype(bf16), fresh_values, preferred_element_type=f32)
        )

    @pl.loop(0, chunks)
    def _(c):
        for copy in copies(c):
            copy.wait()
        rows = pl.ds(pl.multiple_of(c * CHUNK, CHUNK), CHUNK)
        lat = lat_buf[rows, :]
        cosines, sines = [], []
        for b in range(CHUNK // BLK):
            block = kv_at * (CTX_DEV // BLK) + c * (CHUNK // BLK) + b
            cos_b, sin_b = cos_out[pl.ds(block, 1), :], sin_out[pl.ds(block, 1), :]
            cosines.append(cos_in[...] * cos_b - sin_in[...] * sin_b)
            sines.append(sin_in[...] * cos_b + cos_in[...] * sin_b)
        cos, sin = jnp.concatenate(cosines, axis=0), jnp.concatenate(sines, axis=0)
        position = c * CHUNK + lax.broadcasted_iota(jnp.int32, (ROWS, CHUNK), 1)
        live = position < valid
        for j in range(PAIRS):
            columns = slice(2 * j * HEAD_DIM, (2 * j + 2) * HEAD_DIM)
            pre = jnp.dot(lat, wp[:, columns], preferred_element_type=f32)
            lo, hi = pre[:, :HEAD_DIM], pre[:, HEAD_DIM:]
            keys = jnp.concatenate(
                [(lo * cos - hi * sin).astype(bf16), (hi * cos + lo * sin).astype(bf16)], axis=1
            )
            s = jnp.where(live, scores(qc[j], keys), NEG_FILL)
            old = peak[j]
            new = jnp.maximum(old, jnp.max(s, axis=1, keepdims=True))
            shrink = jnp.exp2((old - new) * EXP2_SCALE)
            weights = [
                jnp.exp2((s[:, i : i + HEAD_DIM] - new) * EXP2_SCALE) for i in range(0, CHUNK, HEAD_DIM)
            ]
            peak[j] = new
            total[j] = total[j] * shrink + functools.reduce(jnp.add, weights)
            rounded = [w.astype(bf16) for w in weights]
            result = numer[j] * shrink
            for b in range(CHUNK // BLK):
                per = BLK // HEAD_DIM
                w = jnp.concatenate(rounded[b * per : (b + 1) * per], axis=1)
                v = code_buf[pl.ds(pl.multiple_of(c * CHUNK + b * BLK, BLK), BLK), columns]
                part = own_blocks(jnp.dot(w, v, preferred_element_type=f32))
                block = pl.ds(c * (CHUNK // BLK) + b, 1)
                factor = jnp.concatenate(
                    [
                        jnp.broadcast_to(scale_rows[2 * j + i, block, :], (ROWS // 2, HEAD_DIM))
                        for i in range(2)
                    ],
                    axis=0,
                )
                result = result + part * factor
            numer[j] = result

    for j in range(PAIRS):
        summed = jnp.broadcast_to(jnp.sum(total[j], axis=1, keepdims=True), (ROWS, HEAD_DIM))
        total[j] = jnp.where(low_lanes(summed.shape), peak[j], summed)
    half = PAIRS // 2
    for i in range(half):
        at = slice(i * ROWS, (i + 1) * ROWS)
        for ref, first in ((mine_ref, kv_at * half), (send_ref, (1 - kv_at) * half)):
            ref[at, :HEAD_DIM] = numer[first + i]
            ref[at, HEAD_DIM:] = total[first + i]


def attend(length, latents, codes, scales, queries, new_keys, new_values, key_factor):
    f32, bf16 = jnp.float32, jnp.bfloat16
    vmem = pl.BlockSpec(memory_space=pltpu.VMEM)
    hbm = pl.BlockSpec(memory_space=pl.ANY)
    shape = jax.ShapeDtypeStruct((PAIRS // 2 * ROWS, 2 * HEAD_DIM), f32)
    macs = CTX_DEV * (RANK * KV_HEADS + 2 * PAIRS * ROWS * 2) * HEAD_DIM
    return pl.pallas_call(
        attend_kernel,
        out_shape=(shape, shape),
        in_specs=[pl.BlockSpec(memory_space=pltpu.SMEM), hbm, hbm] + [vmem] * 9,
        out_specs=(vmem, vmem),
        scratch_shapes=[
            pltpu.VMEM((CTX_DEV, RANK), bf16),
            pltpu.VMEM((CTX_DEV, KV_HEADS * HEAD_DIM), bf16),
            pltpu.SemaphoreType.DMA((N_CHUNKS,)),
            pltpu.SemaphoreType.DMA((N_CHUNKS,)),
            pltpu.VMEM((PAIRS, ROWS, 2 * HEAD_DIM), bf16),
            pltpu.VMEM((RANK, KV_HEADS * HEAD_DIM), bf16),
            pltpu.VMEM((KV_HEADS, CTX_DEV // BLK, HEAD_DIM), f32),
            pltpu.VMEM((PAIRS, ROWS, HEAD_DIM), f32),
            pltpu.VMEM((PAIRS, ROWS, HEAD_DIM), f32),
            pltpu.VMEM((PAIRS, ROWS, HEAD_DIM), f32),
        ],
        compiler_params=pltpu.CompilerParams(vmem_limit_bytes=40 * 2**20),
        cost_estimate=pl.CostEstimate(
            flops=2 * macs, bytes_accessed=12 * 2**20, transcendentals=CTX_DEV * HEADS * Q_TOK
        ),
        name="attend",
    )(length, latents, codes, scales, queries, new_keys, new_values, key_factor,
      *[jnp.asarray(t) for t in rotary_tables()])


def merge_kernel(a_ref, b_ref, out_ref):
    def parts(ref):
        both = ref[:, HEAD_DIM:]
        low, other = low_lanes(both.shape), swap_halves(both)
        return ref[:, :HEAD_DIM], jnp.where(low, both, other), jnp.where(low, other, both)

    numer_a, peak_a, total_a = parts(a_ref)
    numer_b, peak_b, total_b = parts(b_ref)
    peak = jnp.maximum(peak_a, peak_b)
    weight_a = jnp.exp2((peak_a - peak) * EXP2_SCALE)
    weight_b = jnp.exp2((peak_b - peak) * EXP2_SCALE)
    out = (numer_a * weight_a + numer_b * weight_b) / (total_a * weight_a + total_b * weight_b)
    out_ref[...] = jnp.concatenate(
        [out[i : i + Q_TOK] for i in range(0, out.shape[0], Q_TOK)], axis=1
    ).astype(out_ref.dtype)


def merge(mine, other):
    vmem = pl.BlockSpec(memory_space=pltpu.VMEM)
    return pl.pallas_call(
        merge_kernel,
        out_shape=jax.ShapeDtypeStruct((Q_TOK, HEADS // 2 * HEAD_DIM), jnp.bfloat16),
        in_specs=[vmem, vmem],
        out_specs=vmem,
        name="merge",
    )(mine, other)


def other_core(x):
    return lax.ppermute(x, "kv", [(0, 1), (1, 0)])


def body(lengths, latents, codes, scales, queries, new_keys, new_values, key_factor, out_weight):
    kv_at = lax.axis_index("kv")
    mine, send = attend(
        lengths, latents[0], codes[0], scales[0], queries[0], new_keys[0], new_values[0], key_factor
    )
    attended = merge(mine, other_core(send))
    all_rows = lax.all_gather(attended, "group", axis=0, tiled=True)
    out = jnp.dot(all_rows, out_weight, preferred_element_type=jnp.float32)
    half = out.shape[0] // 2
    keep = lax.dynamic_slice_in_dim(out, kv_at * half, half, 0)
    give = lax.dynamic_slice_in_dim(out, (1 - kv_at) * half, half, 0)
    return keep + other_core(give)


def solution(mesh):
    placed = (
        P("group"),
        P("group", "kv", None),
        P("group", "kv", None),
        P("group", "kv", None),
        P("group", None, None),
        P("group", None, None),
        P("group", None, None),
        P(),
        P("kv", "group"),
    )
    return jax.shard_map(
        body, mesh=mesh, in_specs=placed, out_specs=P("kv", "group"), check_vma=False
    )
```

time: 235 us -> 131 us (0.56)
  blocking collectives: 40.9 us -> 0 us
  matrix products: 41 us -> 3.44 us
  other arithmetic: 21.4 us -> 0.67 us
  local copies, waits for them, and re-layouts: 34.9 us -> 15.2 us
  starting transfers between devices: 0.04 us -> 19.3 us
  waiting for transfers between devices: 79.5 us -> 74.8 us
  Pallas kernels: 0 us -> 2.95 us
    all_gather x3 -> x0, blocking collectives: 40.9 us -> none  [merged(): everything = jax.tree.map(lambda part: lax.all_gather(part, axis), shard)]
    dot_general x36 -> x1, matrix products: 41 us -> 3.44 us  [body(): out = jnp.dot(all_rows, out_weight, preferred_element_type=jnp.float32)]
    ppermute x0 -> x2, starting transfers between devices: none -> 19.3 us  [other_core(): return lax.ppermute(x, 'kv', [(0, 1), (1, 0)])]
    dynamic_slice x16 -> x1, local copies, waits for them, and re-layouts: 12 us -> 0.02 us  [body(): give = lax.dynamic_slice_in_dim(out, (1 - kv_at) * half, half, 0)]
    reduce_scatter x1 -> x0, waiting for transfers between devices: 9.26 us -> none  [body(): lax.psum_scatter(jnp.dot(all_rows, out_weight, preferred_element_type=jnp...]
    lt x11 -> x0, other arithmetic: 7.18 us -> none  [attend_block(): valid_mask = (positions < length)[None, None, None, :]]
    cos x11 -> x0, other arithmetic: 5.86 us -> none  [rotate(): cosine = jnp.cos(angles)[:, None, :]]
    another operation x11 -> x0, other arithmetic: 4.51 us -> none
  transfers between devices with their start and end apart: 2 -> 3, of which waited for: 2 -> 3; matrix products, arithmetic and copies ran while one was open for 0% -> 0% of each run, Pallas kernels for 0% -> 0%
where the time goes in v1:
time: 131 us
  waiting for transfers between devices  74.8 us (57%)
  starting transfers between devices  19.3 us (15%)
  local copies, waits for them, and re-layouts  15.2 us (12%)
  between operations  14.2 us (11%)
  matrix products  3.44 us (3%)
  Pallas kernels  2.95 us (2%)
    all_gather x1, waiting for transfers between devices, body(): all_rows = lax.all_gather(attended, 'group', axis=0, tiled=True)  72.6 us
    ppermute x2, starting transfers between devices, other_core(): return lax.ppermute(x, 'kv', [(0, 1), (1, 0)])  19.3 us
    unnamed x25, local copies, waits for them, and re-layouts  14.4 us
    dot_general x1, matrix products, body(): out = jnp.dot(all_rows, out_weight, preferred_element_type=jnp.float32)  3.44 us
  transfers between devices with their start and end apart: 3, of which 3 were waited for; matrix products, arithmetic and copies ran while one was open for 0% of the time, Pallas kernels for 0%

profile of v1, /device:TPU:1, one launch (start us, length us, event | category | flops | bytes accessed | tf_op | source)
XLA Modules:
  0.0 130.5 jit_solution(8389849204822279480)
XLA Ops:
  6.5 0.0 copy-start
  7.3 3.1 %copy.14 = bf16[1,4096,160]{2,1,0:T(8,128)(2,1)S(1)} copy(bf16[1,4096,160]{1,2,0:T(8,128)(2,1)} %param.14) | data formatting | bytes 2621440 | tf_op args[1]
  10.4 0.8 copy.15.scale_ref
  11.1 3.4 %copy-done.2 = bf16[1,4096,1024]{2,1,0:T(8,128)(2,1)S(1)} copy-done((bf16[1,4096,1024]{2,1,0:T(8,128)(2,1)S(1)}, bf16[1,4096,1024]{2,1,0:T(8,128)(2,1)}, u32[]{:S(2)}) %copy-start.2) | copy-done | bytes 8388632
  14.5 1.0 copy-done.3
  15.5 0.9 copy-done.4
  16.4 0.7 copy-done.5
  17.1 0.7 copy-done.6
  17.8 0.9 copy-done.7
  18.8 0.9 copy-done.8
  19.7 0.7 copy-done.9
  20.4 0.7 copy-done.10
  21.1 1.1 attend.1
  22.2 0.7 copy-done.1
  22.9 17.7 %collective-permute-start = (f32[256,256]{1,0:T(8,128)S(1)}, f32[256,256]{1,0:T(8,128)S(1)}, u32[]{:S(2)}, u32[]{:S(2)}) collective-permute-start(f32[256,256]{1,0:T(8,128)S(1)} %get-tuple-element.8), channel_id=1, source_target_pairs={{0,1},{1,0},{2,3},{3,2},{4,5},{5,4},{6,7},{7,6},{8,9},{9,8},{10,11... | collective-permute-start | bytes 786440 | tf_op jit(solution)/shard_map/ppermute | solution.py:260
  40.6 1.2 collective-permute-done.b_ref
  41.7 0.7 copy-done.11
  42.4 1.8 %merge.1 = bf16[8,4096]{1,0:T(8,128)(2,1)} custom-call(f32[256,256]{1,0:T(8,128)} %copy-done.1, f32[256,256]{1,0:T(8,128)} %copy-done.11), custom_call_target="tpu_custom_call" | custom-call | tf_op jit(solution)/shard_map/merge/pallas_call | solution.py:250
  44.2 0.0 all-gather.2.cloned.1.call-update
  44.3 72.6 %all-gather.2.cloned.1.call-done = bf16[512,4096]{1,0:T(8,128)(2,1)} async-done(((bf16[8,4096]{1,0:T(8,128)(2,1)}), bf16[512,4096]{1,0:T(8,128)(2,1)}) %all-gather.2.cloned.1.call-update) | async-done | bytes 4194320 | tf_op jit(solution)/shard_map/all_gather | solution.py:269
  116.9 3.4 %fusion = f32[512,128]{1,0:T(8,128)S(1)} fusion(bf16[512,4096]{1,0:T(8,128)(2,1)} %all-gather.2.cloned.1.call-done, bf16[4096,128]{1,0:T(8,128)(2,1)S(1)} %copy-done), kind=kOutput, calls=%fused_computation.2 | convolution fusion | flops 536870912 | bytes 5505024 | tf_op jit(solution)/shard_map/dot_general | solution.py:270
  120.4 1.6 %collective-permute-start.1 = (f32[256,128]{1,0:T(8,128)S(1)}, f32[256,128]{1,0:T(8,128)S(1)}, u32[]{:S(2)}, u32[]{:S(2)}) collective-permute-start(f32[256,128]{1,0:T(8,128)S(1)} %constant_dynamic-slice_fusion), channel_id=1, source_target_pairs={{0,1},{1,0},{2,3},{3,2},{4,5},{5,4},{6,7},{7,6},{8,9},{9,8},{10,11... | collective-permute-start | bytes 393224 | tf_op jit(solution)/shard_map/ppermute | solution.py:260
  122.0 1.0 collective-permute-done.1
  123.0 0.7 dynamic-slice_add_fusion
  (14 shorter events, 0.0 us)
Async XLA Ops:
  6.5 110.3 %copy-start = (bf16[4096,128]{1,0:T(8,128)(2,1)S(1)}, bf16[4096,128]{1,0:T(8,128)(2,1)}, u32[]{:S(2)}) copy-start(bf16[4096,128]{1,0:T(8,128)(2,1)} %param.21) | copy-start | bytes 3145732
  6.5 110.3 %all-gather.2.cloned.1.call-start = ((), (), s32[]{:S(2)}) async-start(), calls=%async_computation | async-start | bytes 4259840 | tf_op jit(solution)/shard_map/all_gather | solution.py:269
  11.1 3.4 %copy-start.2 = (bf16[1,4096,1024]{2,1,0:T(8,128)(2,1)S(1)}, bf16[1,4096,1024]{2,1,0:T(8,128)(2,1)}, u32[]{:S(2)}) copy-start(bf16[1,4096,1024]{2,1,0:T(8,128)(2,1)} %param.15) | copy-start | bytes 25165828
  14.5 1.0 copy-start.3
  15.5 0.9 copy-start.4
  16.4 0.7 copy-start.5
  17.1 0.7 copy-start.6
  17.8 0.9 copy-start.7
  18.7 0.9 copy-start.8
  19.7 0.7 copy-start.9
  20.4 0.7 copy-start.10
  22.2 0.7 copy-start.1
  22.9 18.8 %collective-permute-start = (f32[256,256]{1,0:T(8,128)S(1)}, f32[256,256]{1,0:T(8,128)S(1)}, u32[]{:S(2)}, u32[]{:S(2)}) collective-permute-start(f32[256,256]{1,0:T(8,128)S(1)} %get-tuple-element.8), channel_id=1, source_target_pairs={{0,1},{1,0},{2,3},{3,2},{4,5},{5,4},{6,7},{7,6},{8,9},{9,8},{10,11... | collective-permute-start | bytes 786440 | tf_op jit(solution)/shard_map/ppermute | solution.py:260
  41.7 0.7 copy-start.11
  120.4 2.6 %collective-permute-start.1 = (f32[256,128]{1,0:T(8,128)S(1)}, f32[256,128]{1,0:T(8,128)S(1)}, u32[]{:S(2)}, u32[]{:S(2)}) collective-permute-start(f32[256,128]{1,0:T(8,128)S(1)} %constant_dynamic-slice_fusion), channel_id=1, source_target_pairs={{0,1},{1,0},{2,3},{3,2},{4,5},{5,4},{6,7},{7,6},{8,9},{9,8},{10,11... | collective-permute-start | bytes 393224 | tf_op jit(solution)/shard_map/ppermute | solution.py:260
Sparse Core Ops, SparseCore 0:
  44.4 72.4 all-gather.1

commit v2 on v1

v2 whole, which is shorter than its diff:
```python
import functools

import jax
import jax.numpy as jnp
import numpy as np
from jax import lax
from jax.experimental import pallas as pl
from jax.experimental.pallas import tpu as pltpu
from jax.sharding import PartitionSpec as P

HEADS = 64
KV_HEADS = 8
HEAD_DIM = 128
HALF = HEAD_DIM // 2
RANK = 160
BLK = 256
CTX_DEV = 4096
Q_TOK = 8
PAIRS = KV_HEADS // 2
ROWS = 2 * (HEADS // KV_HEADS) * Q_TOK
CHUNK = 2048
N_CHUNKS = CTX_DEV // CHUNK
ROPE_BASE = 500000.0
NEG_FILL = -1e30
EXP2_SCALE = float(HEAD_DIM**-0.5 * np.log2(np.e))


def rotary_table():
    freq = np.float32(ROPE_BASE) ** (-(np.arange(HALF, dtype=np.float32) * 2.0) / HEAD_DIM)
    angles = np.arange(2 * CTX_DEV, dtype=np.float32)[None, :] * freq.astype(np.float32)[:, None]
    angles = angles.reshape(HALF, 2, CTX_DEV).astype(np.float64)
    return np.stack([np.cos(angles), np.sin(angles)]).transpose(2, 0, 1, 3).astype(np.float32)


STRIP = 16


def strip_order():
    starts = [
        head * HEAD_DIM + half * HALF + m * STRIP
        for m in range(HALF // STRIP)
        for head in range(2)
        for half in range(2)
    ]
    return np.concatenate([np.arange(a, a + STRIP) for a in starts])


def swap_halves(x):
    return pltpu.roll(x, HALF, 1)


def low_lanes(shape):
    return lax.broadcasted_iota(jnp.int32, shape, 1) < HALF


def dot(a, b):
    return jnp.dot(a, b, preferred_element_type=jnp.float32)


def own_blocks(x):
    return jnp.concatenate([x[: ROWS // 2, :HEAD_DIM], x[ROWS // 2 :, HEAD_DIM:]], axis=0)


def attend_kernel(
    length_ref, lat_hbm, code_hbm, table_hbm, scale_hbm, q_hbm, nk_hbm, nv_hbm, kf_hbm,
    mine_ref, send_ref,
    lat_buf, code_buf, table_buf, scale_buf, q_buf, nk_buf, nv_buf, kf_buf,
    lat_sem, code_sem, table_sem, small_sem,
    qc, wt, scale_rows, peak, total, numer,
):
    f32, bf16 = jnp.float32, jnp.bfloat16
    kv_at = lax.axis_index("kv")
    valid = jnp.clip(length_ref[0] - kv_at * CTX_DEV, 0, CTX_DEV)
    chunks = lax.div(valid + (CHUNK - 1), CHUNK)

    small = [
        pltpu.make_async_copy(src, dst, small_sem.at[i])
        for i, (src, dst) in enumerate(
            ((kf_hbm, kf_buf), (q_hbm, q_buf), (nk_hbm, nk_buf), (nv_hbm, nv_buf), (scale_hbm, scale_buf))
        )
    ]
    for copy in small:
        copy.start()

    def copies(c):
        at = pl.ds(pl.multiple_of(c * CHUNK, CHUNK), CHUNK)
        return (
            pltpu.make_async_copy(lat_hbm.at[:, at], lat_buf.at[:, at], lat_sem.at[c]),
            pltpu.make_async_copy(table_hbm.at[kv_at, :, :, at], table_buf.at[:, :, at], table_sem.at[c]),
            pltpu.make_async_copy(code_hbm.at[at], code_buf.at[at], code_sem.at[c]),
        )

    @pl.loop(0, chunks)
    def _(c):
        for copy in copies(c):
            copy.start()

    for copy in small:
        copy.wait()
    scales = scale_buf[...].astype(f32)
    for b in range(CTX_DEV // BLK):
        scale_rows[b] = jnp.broadcast_to(scales[:, b : b + 1], (KV_HEADS, HEAD_DIM))
    row_tok = lax.rem(lax.broadcasted_iota(jnp.int32, (ROWS, HEAD_DIM), 0), Q_TOK)
    lane = lax.broadcasted_iota(jnp.int32, (ROWS, HEAD_DIM), 1)
    causal = jnp.logical_and(lane <= row_tok, kv_at == 0)
    queries = q_buf[...].astype(f32)
    new_keys = nk_buf[...].astype(f32)
    new_values = nv_buf[...].astype(f32)
    pad = jnp.zeros((HEAD_DIM - Q_TOK, 2 * HEAD_DIM), f32)
    groups = HEADS // KV_HEADS
    blank = jnp.zeros((ROWS // 2, HEAD_DIM), f32)

    def head_rows(k):
        return jnp.concatenate(
            [queries[:, (k * groups + g) * HEAD_DIM : (k * groups + g + 1) * HEAD_DIM] for g in range(groups)],
            axis=0,
        )

    order = strip_order()
    source = lax.broadcasted_iota(jnp.int32, (2 * HEAD_DIM, 2 * HEAD_DIM), 0)
    target = lax.broadcasted_iota(jnp.int32, (2 * HEAD_DIM, 2 * HEAD_DIM), 1)
    strip, inside = lax.div(target, STRIP), lax.rem(target, STRIP)
    wanted = (
        lax.rem(lax.div(strip, 2), 2) * HEAD_DIM + lax.rem(strip, 2) * HALF + lax.div(strip, 4) * STRIP + inside
    )
    arrange = jnp.where(source == wanted, 1.0, 0.0).astype(bf16)

    for j in range(PAIRS):
        columns = slice(2 * j * HEAD_DIM, (2 * j + 2) * HEAD_DIM)
        plain = jnp.concatenate(
            [
                jnp.concatenate([head_rows(2 * j), blank], axis=1),
                jnp.concatenate([blank, head_rows(2 * j + 1)], axis=1),
            ],
            axis=0,
        ).astype(bf16)
        qc[j] = dot(plain, arrange).astype(bf16)
        turned = kf_buf[:, columns].astype(f32).T
        wt[columns, :] = jnp.concatenate(
            [turned[a : a + STRIP] for a in order[::STRIP]], axis=0
        ).astype(bf16)
        fresh_keys = jnp.concatenate([new_keys[:, columns], pad], axis=0).astype(bf16)
        fresh_values = jnp.concatenate([new_values[:, columns], pad], axis=0).astype(bf16)
        s = lax.dot_general(plain, fresh_keys, (((1,), (1,)), ((), ())), preferred_element_type=f32)
        s = jnp.where(causal, s, NEG_FILL)
        top = jnp.broadcast_to(jnp.max(s, axis=1, keepdims=True), s.shape)
        weights = jnp.where(causal, jnp.exp2((s - top) * EXP2_SCALE), 0.0)
        peak[j] = top
        total[j] = weights
        numer[j] = own_blocks(dot(weights.astype(bf16), fresh_values))

    @pl.loop(0, chunks)
    def _(c):
        for copy in copies(c):
            copy.wait()
        at = pl.ds(pl.multiple_of(c * CHUNK, CHUNK), CHUNK)
        lat = lat_buf[:, at]
        position = c * CHUNK + lax.broadcasted_iota(jnp.int32, (1, CHUNK), 1)
        hide = jnp.where(position < valid, 0.0, NEG_FILL)
        def make_keys(j):
            columns = slice(2 * j * HEAD_DIM, (2 * j + 2) * HEAD_DIM)
            cos, sin = table_buf[0, :, at], table_buf[1, :, at]
            pre = dot(wt[columns, :], lat)
            keys = []
            for m in range(HALF // STRIP):
                here = slice(m * STRIP, (m + 1) * STRIP)
                for i in range(2):
                    at_lo = (4 * m + 2 * i) * STRIP
                    lo, hi = pre[at_lo : at_lo + STRIP], pre[at_lo + STRIP : at_lo + 2 * STRIP]
                    keys.append((lo * cos[here] - hi * sin[here]).astype(bf16))
                    keys.append((hi * cos[here] + lo * sin[here]).astype(bf16))
            return jnp.concatenate(keys, axis=0)

        def make_scores(j, keys):
            return dot(qc[j], keys) + hide

        def weigh(j, s):
            old = peak[j]
            new = jnp.maximum(old, jnp.max(s, axis=1, keepdims=True))
            shrink = jnp.exp2((old - new) * EXP2_SCALE)
            weights = [
                jnp.exp2((s[:, i : i + HEAD_DIM] - new) * EXP2_SCALE) for i in range(0, CHUNK, HEAD_DIM)
            ]
            peak[j] = new
            total[j] = total[j] * shrink + functools.reduce(jnp.add, weights)
            return shrink, [w.astype(bf16) for w in weights]

        def add_values(j, shrink, rounded):
            columns = slice(2 * j * HEAD_DIM, (2 * j + 2) * HEAD_DIM)
            result = numer[j] * shrink
            for b in range(CHUNK // BLK):
                per = BLK // HEAD_DIM
                w = jnp.concatenate(rounded[b * per : (b + 1) * per], axis=1)
                v = code_buf[pl.ds(pl.multiple_of(c * CHUNK + b * BLK, BLK), BLK), columns]
                part = own_blocks(dot(w, v))
                block = c * (CHUNK // BLK) + b
                factor = jnp.concatenate(
                    [
                        jnp.broadcast_to(scale_rows[block, 2 * j + i : 2 * j + i + 1, :], (ROWS // 2, HEAD_DIM))
                        for i in range(2)
                    ],
                    axis=0,
                )
                result = result + part * factor
            numer[j] = result

        all_keys = [make_keys(j) for j in range(PAIRS)]
        all_scores = [make_scores(j, all_keys[j]) for j in range(PAIRS)]
        weighed = [weigh(j, all_scores[j]) for j in range(PAIRS)]
        for j in range(PAIRS):
            add_values(j, *weighed[j])

    for j in range(PAIRS):
        summed = jnp.broadcast_to(jnp.sum(total[j], axis=1, keepdims=True), (ROWS, HEAD_DIM))
        total[j] = jnp.where(low_lanes(summed.shape), peak[j], summed)
    half = PAIRS // 2
    for i in range(half):
        at = slice(i * ROWS, (i + 1) * ROWS)
        for ref, first in ((mine_ref, kv_at * half), (send_ref, (1 - kv_at) * half)):
            ref[at, :HEAD_DIM] = numer[first + i]
            ref[at, HEAD_DIM:] = total[first + i]


def attend(length, latents, codes, scales, queries, new_keys, new_values, key_factor):
    f32, bf16 = jnp.float32, jnp.bfloat16
    vmem = pl.BlockSpec(memory_space=pltpu.VMEM)
    hbm = pl.BlockSpec(memory_space=pltpu.HBM)
    shape = jax.ShapeDtypeStruct((PAIRS // 2 * ROWS, 2 * HEAD_DIM), f32)
    macs = CTX_DEV * (RANK * KV_HEADS + 2 * PAIRS * ROWS * 2) * HEAD_DIM
    width = KV_HEADS * HEAD_DIM
    return pl.pallas_call(
        attend_kernel,
        out_shape=(shape, shape),
        in_specs=[pl.BlockSpec(memory_space=pltpu.SMEM)] + [hbm] * 8,
        out_specs=(vmem, vmem),
        scratch_shapes=[
            pltpu.VMEM((RANK, CTX_DEV), bf16),
            pltpu.VMEM((CTX_DEV, width), bf16),
            pltpu.VMEM((2, HALF, CTX_DEV), f32),
            pltpu.VMEM((KV_HEADS, CTX_DEV // BLK), bf16),
            pltpu.VMEM((Q_TOK, HEADS * HEAD_DIM), bf16),
            pltpu.VMEM((Q_TOK, width), bf16),
            pltpu.VMEM((Q_TOK, width), bf16),
            pltpu.VMEM((RANK, width), bf16),
            pltpu.SemaphoreType.DMA((N_CHUNKS,)),
            pltpu.SemaphoreType.DMA((N_CHUNKS,)),
            pltpu.SemaphoreType.DMA((N_CHUNKS,)),
            pltpu.SemaphoreType.DMA((5,)),
            pltpu.VMEM((PAIRS, ROWS, 2 * HEAD_DIM), bf16),
            pltpu.VMEM((width, RANK), bf16),
            pltpu.VMEM((CTX_DEV // BLK, KV_HEADS, HEAD_DIM), f32),
            pltpu.VMEM((PAIRS, ROWS, HEAD_DIM), f32),
            pltpu.VMEM((PAIRS, ROWS, HEAD_DIM), f32),
            pltpu.VMEM((PAIRS, ROWS, HEAD_DIM), f32),
        ],
        compiler_params=pltpu.CompilerParams(vmem_limit_bytes=60 * 2**20),
        cost_estimate=pl.CostEstimate(
            flops=2 * macs, bytes_accessed=12 * 2**20, transcendentals=CTX_DEV * HEADS * Q_TOK
        ),
        name="attend",
    )(length, latents.T, codes, jnp.asarray(rotary_table()), scales.T, queries, new_keys, new_values, key_factor)


def merge_kernel(a_ref, b_ref, out_ref):
    def parts(ref):
        both = ref[:, HEAD_DIM:]
        low, other = low_lanes(both.shape), swap_halves(both)
        return ref[:, :HEAD_DIM], jnp.where(low, both, other), jnp.where(low, other, both)

    numer_a, peak_a, total_a = parts(a_ref)
    numer_b, peak_b, total_b = parts(b_ref)
    peak = jnp.maximum(peak_a, peak_b)
    weight_a = jnp.exp2((peak_a - peak) * EXP2_SCALE)
    weight_b = jnp.exp2((peak_b - peak) * EXP2_SCALE)
    out = (numer_a * weight_a + numer_b * weight_b) / (total_a * weight_a + total_b * weight_b)
    out_ref[...] = jnp.concatenate(
        [out[i : i + Q_TOK] for i in range(0, out.shape[0], Q_TOK)], axis=1
    ).astype(out_ref.dtype)


def merge(mine, other):
    vmem = pl.BlockSpec(memory_space=pltpu.VMEM)
    return pl.pallas_call(
        merge_kernel,
        out_shape=jax.ShapeDtypeStruct((Q_TOK, HEADS // 2 * HEAD_DIM), jnp.bfloat16),
        in_specs=[vmem, vmem],
        out_specs=vmem,
        name="merge",
    )(mine, other)


def other_core(x):
    return lax.ppermute(x, "kv", [(0, 1), (1, 0)])


AXES = {"z": 16, "y": 4, "x": 1}
SIDE = 4
WEIGHT_AXIS = ("x", "y")
FIRST_AXIS = ("y", "z")
SECOND_AXIS = ("z", "x")
SHIFTS = (1, -1, 2)


def coordinate(chip, axis):
    return chip // AXES[axis] % SIDE


def shifted(x, axes, shift):
    moves = []
    for chip in range(SIDE**3):
        for core, axis in enumerate(axes):
            at = coordinate(chip, axis)
            target = chip + ((at + shift) % SIDE - at) * AXES[axis]
            moves.append((chip * 2 + core, target * 2 + core))
    return lax.ppermute(x, ("group", "kv"), moves)


def gathered(x, axes):
    return jnp.concatenate([x] + [shifted(x, axes, shift) for shift in SHIFTS], axis=0)


def assemble_kernel(p0_ref, p1_ref, p2_ref, p3_ref, keep_ref, give_ref, whole):
    chip, core = lax.axis_index("group"), lax.axis_index("kv")

    def axis_at(axes):
        return [lax.rem(lax.div(chip, AXES[axis]), SIDE) for axis in axes]

    def place(axes, core_at):
        return jnp.where(core_at == 0, *[jnp.int32(AXES[axis]) for axis in axes])

    weight, first, second = (
        jnp.where(core == 0, *axis_at(axes)) for axes in (WEIGHT_AXIS, FIRST_AXIS, SECOND_AXIS)
    )
    steps = (0,) + SHIFTS
    for ref, d in zip((p0_ref, p1_ref, p2_ref, p3_ref), steps):
        for i, e in enumerate(steps):
            for j, f in enumerate(steps):
                request = (
                    lax.rem(weight + (d + SIDE), SIDE) * place(WEIGHT_AXIS, core)
                    + lax.rem(first + (SIDE - f), SIDE) * place(FIRST_AXIS, core)
                    + lax.rem(second + (SIDE - e), SIDE) * place(SECOND_AXIS, core)
                )
                row = (i * SIDE + j) * Q_TOK
                whole[pl.ds(pl.multiple_of(request * Q_TOK, Q_TOK), Q_TOK), :] = ref[row : row + Q_TOK, :]
    half = whole.shape[0] // 2
    keep_ref[...] = whole[pl.ds(pl.multiple_of(core * half, half), half), :]
    give_ref[...] = whole[pl.ds(pl.multiple_of((1 - core) * half, half), half), :]


def assemble(pieces):
    vmem = pl.BlockSpec(memory_space=pltpu.VMEM)
    rows, columns = SIDE * pieces[0].shape[0], pieces[0].shape[1]
    shape = jax.ShapeDtypeStruct((rows // 2, columns), jnp.float32)
    return pl.pallas_call(
        assemble_kernel,
        out_shape=(shape, shape),
        in_specs=[vmem] * 4,
        out_specs=(vmem, vmem),
        scratch_shapes=[pltpu.VMEM((rows, columns), jnp.float32)],
        name="assemble",
    )(*pieces)


def body(lengths, latents, codes, scales, queries, new_keys, new_values, key_factor, out_weight):
    weights = [out_weight] + [shifted(out_weight, WEIGHT_AXIS, shift) for shift in SHIFTS]
    mine, send = attend(
        lengths, latents[0], codes[0], scales[0], queries[0], new_keys[0], new_values[0], key_factor
    )
    attended = merge(mine, other_core(send))
    rows = gathered(gathered(attended, FIRST_AXIS), SECOND_AXIS)
    results = [dot(rows, w) for w in weights]
    pieces = [results[0]] + [shifted(r, WEIGHT_AXIS, -shift) for r, shift in zip(results[1:], SHIFTS)]
    keep, give = assemble(pieces)
    return keep + other_core(give)


def solution(mesh):
    placed = (
        P("group"),
        P("group", "kv", None),
        P("group", "kv", None),
        P("group", "kv", None),
        P("group", None, None),
        P("group", None, None),
        P("group", None, None),
        P(),
        P("kv", "group"),
    )
    return jax.shard_map(
        body, mesh=mesh, in_specs=placed, out_specs=P("kv", "group"), check_vma=False
    )
```

time: 131 us -> 60.3 us (0.46)
  waiting for transfers between devices: 74.8 us -> 19.8 us
  between operations: 14.2 us -> 0.77 us
  local copies, waits for them, and re-layouts: 15.2 us -> 2.36 us
  Pallas kernels: 2.95 us -> 13.5 us
  other arithmetic: 0.67 us -> 2.43 us
    all_gather x1 -> x0, waiting for transfers between devices: 72.6 us -> none  [body(): all_rows = lax.all_gather(attended, 'group', axis=0, tiled=True)]
    ppermute x0 -> x12, waiting for transfers between devices: none -> 18.3 us  [shifted(): return lax.ppermute(x, ('group', 'kv'), moves)]
    ppermute x2, starting transfers between devices: 19.3 us -> 1.63 us  [other_core(): return lax.ppermute(x, 'kv', [(0, 1), (1, 0)])]
    ppermute x0 -> x12, starting transfers between devices: none -> 17.1 us  [shifted(): return lax.ppermute(x, ('group', 'kv'), moves)]
    unnamed x25 -> x16, local copies, waits for them, and re-layouts: 14.4 us -> 2.35 us
    pallas_call x1, Pallas kernels: 1.1 us -> 9.97 us  [attend(): pl.pallas_call(attend_kernel, out_shape=(shape, shape), in_specs=[pl.Bloc...]
    pallas_call x0 -> x1, Pallas kernels: none -> 1.73 us  [assemble(): pl.pallas_call(assemble_kernel, out_shape=(shape, shape), in_specs=[vmem]...]
    dot_general x1 -> x4, matrix products: 3.44 us -> 2.38 us  [dot(): return jnp.dot(a, b, preferred_element_type=jnp.float32)]
  transfers between devices with their start and end apart: 3 -> 14, of which waited for: 3 -> 6; matrix products, arithmetic and copies ran while one was open for 0% -> 7% of each run, Pallas kernels for 0% -> 3%
where the time goes in v2:
time: 60.3 us; the launch traced here: 60 us
  waiting for transfers between devices  19.8 us (33%)
  starting transfers between devices  18.7 us (31%)
  Pallas kernels  13.5 us (22%)
  other arithmetic  2.43 us (4%)
  matrix products  2.38 us (4%)
  local copies, waits for them, and re-layouts  2.36 us (4%)
  between operations  0.77 us (1%)
    ppermute x12, waiting for transfers between devices, shifted(): return lax.ppermute(x, ('group', 'kv'), moves)  18.3 us
    ppermute x12, starting transfers between devices, shifted(): return lax.ppermute(x, ('group', 'kv'), moves)  17.1 us
    pallas_call x1, Pallas kernels, attend(): pl.pallas_call(attend_kernel, out_shape=(shape, shape), in_specs=[pl.Bloc...  9.97 us
    dot_general x4, matrix products, dot(): return jnp.dot(a, b, preferred_element_type=jnp.float32)  2.38 us
    unnamed x16, local copies, waits for them, and re-layouts  2.35 us
    pallas_call x1, Pallas kernels, merge(): pl.pallas_call(merge_kernel, out_shape=jax.ShapeDtypeStruct((Q_TOK, HEADS...  1.85 us
    pallas_call x1, Pallas kernels, assemble(): pl.pallas_call(assemble_kernel, out_shape=(shape, shape), in_specs=[vmem]...  1.73 us
    ppermute x2, starting transfers between devices, other_core(): return lax.ppermute(x, 'kv', [(0, 1), (1, 0)])  1.63 us
  transfers between devices with their start and end apart: 14, of which 6 were waited for; matrix products, arithmetic and copies ran while one was open for 7% of the time, Pallas kernels for 3%

profile of v2, /device:TPU:1, one launch (start us, length us, event | category | flops | bytes accessed | tf_op | source)
XLA Modules:
  0.0 60.0 jit_solution(1716879107113586071)
XLA Ops:
  0.7 10.0 %attend.1 = (f32[256,256]{1,0:T(8,128)}, f32[256,256]{1,0:T(8,128)}) custom-call(s32[1]{0:T(128)S(6)} %copy.17.length_ref, bf16[160,4096]{1,0:T(8,128)(2,1)} %bitcast.19, bf16[4096,1024]{1,0:T(8,128)(2,1)} %bitcast.18, f32[2,2,64,4096]{3,2,1,0:T(8,128)} %constant.2.clone.table_hbm, bf16[8,16]{1,0:T(8,128)(2,1)} %bitcast.23, bf16[8,8192]{1,0:T(8,128)(2,1)} %bitcast.20, ...), custom_call_target="tpu_custom_call" | custom-call | flops 3489660928 | bytes 12582912 | tf_op jit(solution)/shard_map/attend/pallas_call | solution.py:231
  10.6 1.5 %collective-permute-start = (f32[256,256]{1,0:T(8,128)}, f32[256,256]{1,0:T(8,128)S(1)}, u32[]{:S(2)}, u32[]{:S(2)}) collective-permute-start(f32[256,256]{1,0:T(8,128)} %get-tuple-element.10), channel_id=1, source_target_pairs={{0,1},{1,0},{2,3},{3,2},{4,5},{5,4},{6,7},{7,6},{8,9},{9,8},{10,11... | collective-permute-start | bytes 786440 | tf_op jit(solution)/shard_map/ppermute | solution.py:293
  12.1 1.4 %collective-permute-start.7 = (bf16[4096,128]{1,0:T(8,128)(2,1)S(1)}, bf16[4096,128]{1,0:T(8,128)(2,1)S(1)}, u32[]{:S(2)}, u32[]{:S(2)}) collective-permute-start(bf16[4096,128]{1,0:T(8,128)(2,1)S(1)} %copy-done), channel_id=1, source_target_pairs={{0,2},{1,9},{2,4},{3,11},{4,6},{5,13},{6,0},{7,15},{8,10},{9,17},{... | collective-permute-start | bytes 3145736 | tf_op jit(solution)/shard_map/ppermute | solution.py:315
  13.5 1.4 %collective-permute-start.9 = (bf16[4096,128]{1,0:T(8,128)(2,1)S(1)}, bf16[4096,128]{1,0:T(8,128)(2,1)S(1)}, u32[]{:S(2)}, u32[]{:S(2)}) collective-permute-start(bf16[4096,128]{1,0:T(8,128)(2,1)S(1)} %copy-done), channel_id=1, source_target_pairs={{0,6},{1,25},{2,0},{3,27},{4,2},{5,29},{6,4},{7,31},{8,14},{9,1},{... | collective-permute-start | bytes 3145736 | tf_op jit(solution)/shard_map/ppermute | solution.py:315
  15.0 0.7 %copy-done.1 = f32[256,256]{1,0:T(8,128)} copy-done((f32[256,256]{1,0:T(8,128)}, f32[256,256]{1,0:T(8,128)S(1)}, u32[]{:S(2)}) %copy-start.1) | copy-done | bytes 262168
  15.7 1.8 %merge.1 = bf16[8,4096]{1,0:T(8,128)(2,1)} custom-call(f32[256,256]{1,0:T(8,128)} %get-tuple-element.9.a_ref, f32[256,256]{1,0:T(8,128)} %copy-done.1), custom_call_target="tpu_custom_call" | custom-call | tf_op jit(solution)/shard_map/merge/pallas_call | solution.py:283
  17.5 1.6 %collective-permute-start.1 = (bf16[8,4096]{1,0:T(8,128)(2,1)}, bf16[8,4096]{1,0:T(8,128)(2,1)S(1)}, u32[]{:S(2)}, u32[]{:S(2)}) collective-permute-start(bf16[8,4096]{1,0:T(8,128)(2,1)} %merge.1), channel_id=1, source_target_pairs={{0,8},{1,33},{2,10},{3,35},{4,12},{5,37},{6,14},{7,39},{8,16},{9,4... | collective-permute-start | bytes 196616 | tf_op jit(solution)/shard_map/ppermute | solution.py:315
  19.1 2.1 %collective-permute-start.2 = (bf16[8,4096]{1,0:T(8,128)(2,1)}, bf16[8,4096]{1,0:T(8,128)(2,1)S(1)}, u32[]{:S(2)}, u32[]{:S(2)}) collective-permute-start(bf16[8,4096]{1,0:T(8,128)(2,1)} %merge.1), channel_id=1, source_target_pairs={{0,24},{1,97},{2,26},{3,99},{4,28},{5,101},{6,30},{7,103},{8,0},{9... | collective-permute-start | bytes 196616 | tf_op jit(solution)/shard_map/ppermute | solution.py:315
  21.3 1.2 %collective-permute-start.3 = (bf16[8,4096]{1,0:T(8,128)(2,1)}, bf16[8,4096]{1,0:T(8,128)(2,1)S(1)}, u32[]{:S(2)}, u32[]{:S(2)}) collective-permute-start(bf16[8,4096]{1,0:T(8,128)(2,1)} %merge.1), channel_id=1, source_target_pairs={{0,16},{1,65},{2,18},{3,67},{4,20},{5,69},{6,22},{7,71},{8,24},{9,... | collective-permute-start | bytes 196616 | tf_op jit(solution)/shard_map/ppermute | solution.py:315
  22.5 0.9 %constant_dynamic-update-slice_fusion.6 = bf16[128,4096]{1,0:T(8,128)(2,1)S(1)} fusion(bf16[8,4096]{1,0:T(8,128)(2,1)} %merge.1), kind=kLoop, calls=%fused_computation.7 | loop fusion | bytes 131072
  23.4 1.7 %collective-permute-start.11 = (bf16[4096,128]{1,0:T(8,128)(2,1)S(1)}, bf16[4096,128]{1,0:T(8,128)(2,1)S(1)}, u32[]{:S(2)}, u32[]{:S(2)}) collective-permute-start(bf16[4096,128]{1,0:T(8,128)(2,1)S(1)} %copy-done), channel_id=1, source_target_pairs={{0,4},{1,17},{2,6},{3,19},{4,0},{5,21},{6,2},{7,23},{8,12},{9,25},... | collective-permute-start | bytes 3145736 | tf_op jit(solution)/shard_map/ppermute | solution.py:315
  25.1 1.3 %collective-permute-done.3 = bf16[8,4096]{1,0:T(8,128)(2,1)S(1)} collective-permute-done((bf16[8,4096]{1,0:T(8,128)(2,1)}, bf16[8,4096]{1,0:T(8,128)(2,1)S(1)}, u32[]{:S(2)}, u32[]{:S(2)}) %collective-permute-start.3) | collective-permute-done | bytes 65568 | tf_op jit(solution)/shard_map/ppermute | solution.py:315
  26.4 0.9 %pad_maximum_fusion = bf16[32,4096]{1,0:T(8,128)(2,1)S(1)} fusion(bf16[8,4096]{1,0:T(8,128)(2,1)S(1)} %collective-permute-done.3, bf16[8,4096]{1,0:T(8,128)(2,1)S(1)} %collective-permute-done.2, bf16[8,4096]{1,0:T(8,128)(2,1)S(1)} %collective-permute-done.1, bf16[8,4096]{1,0:T(8,128)(2,1)} %merge.1), kind=kLoop, calls=%fused_computation | loop fusion | flops 1048576 | bytes 524288 | tf_op jit(solution)/shard_map/concatenate | solution.py:319
  27.2 1.3 %collective-permute-start.4 = (bf16[32,4096]{1,0:T(8,128)(2,1)S(1)}, bf16[32,4096]{1,0:T(8,128)(2,1)S(1)}, u32[]{:S(2)}, u32[]{:S(2)}) collective-permute-start(bf16[32,4096]{1,0:T(8,128)(2,1)S(1)} %pad_maximum_fusion), channel_id=1, source_target_pairs={{0,32},{1,3},{2,34},{3,5},{4,36},{5,7},{6,38},{7,1},{8,40},{9,11},... | collective-permute-start | bytes 786440 | tf_op jit(solution)/shard_map/ppermute | solution.py:315
  28.5 1.5 %collective-permute-start.5 = (bf16[32,4096]{1,0:T(8,128)(2,1)S(1)}, bf16[32,4096]{1,0:T(8,128)(2,1)S(1)}, u32[]{:S(2)}, u32[]{:S(2)}) collective-permute-start(bf16[32,4096]{1,0:T(8,128)(2,1)S(1)} %pad_maximum_fusion), channel_id=1, source_target_pairs={{0,96},{1,7},{2,98},{3,1},{4,100},{5,3},{6,102},{7,5},{8,104},{9,1... | collective-permute-start | bytes 786440 | tf_op jit(solution)/shard_map/ppermute | solution.py:315
  30.0 7.9 %collective-permute-done.4 = bf16[32,4096]{1,0:T(8,128)(2,1)S(1)} collective-permute-done((bf16[32,4096]{1,0:T(8,128)(2,1)S(1)}, bf16[32,4096]{1,0:T(8,128)(2,1)S(1)}, u32[]{:S(2)}, u32[]{:S(2)}) %collective-permute-start.4) | collective-permute-done | bytes 262176 | tf_op jit(solution)/shard_map/ppermute | solution.py:315
  38.5 7.2 %collective-permute-done.6 = bf16[32,4096]{1,0:T(8,128)(2,1)S(1)} collective-permute-done((bf16[32,4096]{1,0:T(8,128)(2,1)S(1)}, bf16[32,4096]{1,0:T(8,128)(2,1)S(1)}, u32[]{:S(2)}, u32[]{:S(2)}) %collective-permute-start.6) | collective-permute-done | bytes 262176 | tf_op jit(solution)/shard_map/ppermute | solution.py:315
  46.2 2.6 %collective-permute-start.8 = (f32[128,128]{1,0:T(8,128)S(1)}, f32[128,128]{1,0:T(8,128)S(1)}, u32[]{:S(2)}, u32[]{:S(2)}) collective-permute-start(f32[128,128]{1,0:T(8,128)S(1)} %fusion.1), channel_id=1, source_target_pairs={{0,6},{1,25},{2,0},{3,27},{4,2},{5,29},{6,4},{7,31},{8,14},{9,1},{... | collective-permute-start | bytes 196616 | tf_op jit(solution)/shard_map/ppermute | solution.py:315
  49.7 1.7 %collective-permute-start.12 = (f32[128,128]{1,0:T(8,128)S(1)}, f32[128,128]{1,0:T(8,128)S(1)}, u32[]{:S(2)}, u32[]{:S(2)}) collective-permute-start(f32[128,128]{1,0:T(8,128)S(1)} %fusion.3), channel_id=1, source_target_pairs={{0,4},{1,17},{2,6},{3,19},{4,0},{5,21},{6,2},{7,23},{8,12},{9,25},... | collective-permute-start | bytes 196616 | tf_op jit(solution)/shard_map/ppermute | solution.py:315
  51.4 1.1 %fusion.p0_ref = f32[128,128]{1,0:T(8,128)} fusion(bf16[128,4096]{1,0:T(8,128)(2,1)S(1)} %constant_dynamic-update-slice_fusion, bf16[4096,128]{1,0:T(8,128)(2,1)S(1)} %copy-done), kind=kOutput, calls=%fused_computation.8 | convolution fusion | flops 134217728 | bytes 2162688 | tf_op jit(solution)/shard_map/dot_general | solution.py:57
  52.5 1.4 %collective-permute-done.10.p2_ref = f32[128,128]{1,0:T(8,128)S(1)} collective-permute-done((f32[128,128]{1,0:T(8,128)S(1)}, f32[128,128]{1,0:T(8,128)S(1)}, u32[]{:S(2)}, u32[]{:S(2)}) %collective-permute-start.10) | collective-permute-done | bytes 65568 | tf_op jit(solution)/shard_map/ppermute | solution.py:315
  55.1 1.7 %assemble.1 = (f32[256,128]{1,0:T(8,128)}, f32[256,128]{1,0:T(8,128)}) custom-call(f32[128,128]{1,0:T(8,128)} %fusion.p0_ref, f32[128,128]{1,0:T(8,128)} %copy-done.2, f32[128,128]{1,0:T(8,128)} %copy-done.3, f32[128,128]{1,0:T(8,128)} %copy-done.4), custom_call_target="tpu_custom_call" | custom-call | tf_op jit(solution)/shard_map/assemble/pallas_call | solution.py:354
  57.0 1.4 %collective-permute-done.13 = f32[256,128]{1,0:T(8,128)S(1)} collective-permute-done((f32[256,128]{1,0:T(8,128)}, f32[256,128]{1,0:T(8,128)S(1)}, u32[]{:S(2)}, u32[]{:S(2)}) %collective-permute-start.13) | collective-permute-done | bytes 131104 | tf_op jit(solution)/shard_map/ppermute | solution.py:293
  58.4 1.6 %add.3 = f32[256,128]{1,0:T(8,128)} add(f32[256,128]{1,0:T(8,128)} %get-tuple-element.11, f32[256,128]{1,0:T(8,128)S(1)} %collective-permute-done.13) | non-fusion elementwise | flops 32768 | bytes 393216 | tf_op jit(solution)/shard_map/add | solution.py:374
  (30 shorter events, 3.4 us)
Async XLA Ops:
  0.7 11.5 %copy-start = (bf16[4096,128]{1,0:T(8,128)(2,1)S(1)}, bf16[4096,128]{1,0:T(8,128)(2,1)}, u32[]{:S(2)}) copy-start(bf16[4096,128]{1,0:T(8,128)(2,1)} %param.18) | copy-start | bytes 3145732
  10.6 4.3 %collective-permute-start = (f32[256,256]{1,0:T(8,128)}, f32[256,256]{1,0:T(8,128)S(1)}, u32[]{:S(2)}, u32[]{:S(2)}) collective-permute-start(f32[256,256]{1,0:T(8,128)} %get-tuple-element.10), channel_id=1, source_target_pairs={{0,1},{1,0},{2,3},{3,2},{4,5},{5,4},{6,7},{7,6},{8,9},{9,8},{10,11... | collective-permute-start | bytes 786440 | tf_op jit(solution)/shard_map/ppermute | solution.py:293
  12.1 33.6 %collective-permute-start.7 = (bf16[4096,128]{1,0:T(8,128)(2,1)S(1)}, bf16[4096,128]{1,0:T(8,128)(2,1)S(1)}, u32[]{:S(2)}, u32[]{:S(2)}) collective-permute-start(bf16[4096,128]{1,0:T(8,128)(2,1)S(1)} %copy-done), channel_id=1, source_target_pairs={{0,2},{1,9},{2,4},{3,11},{4,6},{5,13},{6,0},{7,15},{8,10},{9,17},{... | collective-permute-start | bytes 3145736 | tf_op jit(solution)/shard_map/ppermute | solution.py:315
  13.5 35.2 %collective-permute-start.9 = (bf16[4096,128]{1,0:T(8,128)(2,1)S(1)}, bf16[4096,128]{1,0:T(8,128)(2,1)S(1)}, u32[]{:S(2)}, u32[]{:S(2)}) collective-permute-start(bf16[4096,128]{1,0:T(8,128)(2,1)S(1)} %copy-done), channel_id=1, source_target_pairs={{0,6},{1,25},{2,0},{3,27},{4,2},{5,29},{6,4},{7,31},{8,14},{9,1},{... | collective-permute-start | bytes 3145736 | tf_op jit(solution)/shard_map/ppermute | solution.py:315
  15.0 0.7 %copy-start.1 = (f32[256,256]{1,0:T(8,128)}, f32[256,256]{1,0:T(8,128)S(1)}, u32[]{:S(2)}) copy-start(f32[256,256]{1,0:T(8,128)S(1)} %collective-permute-done.b_ref) | copy-start | bytes 786436
  17.5 5.9 %collective-permute-start.1 = (bf16[8,4096]{1,0:T(8,128)(2,1)}, bf16[8,4096]{1,0:T(8,128)(2,1)S(1)}, u32[]{:S(2)}, u32[]{:S(2)}) collective-permute-start(bf16[8,4096]{1,0:T(8,128)(2,1)} %merge.1), channel_id=1, source_target_pairs={{0,8},{1,33},{2,10},{3,35},{4,12},{5,37},{6,14},{7,39},{8,16},{9,4... | collective-permute-start | bytes 196616 | tf_op jit(solution)/shard_map/ppermute | solution.py:315
  19.1 6.0 %collective-permute-start.2 = (bf16[8,4096]{1,0:T(8,128)(2,1)}, bf16[8,4096]{1,0:T(8,128)(2,1)S(1)}, u32[]{:S(2)}, u32[]{:S(2)}) collective-permute-start(bf16[8,4096]{1,0:T(8,128)(2,1)} %merge.1), channel_id=1, source_target_pairs={{0,24},{1,97},{2,26},{3,99},{4,28},{5,101},{6,30},{7,103},{8,0},{9... | collective-permute-start | bytes 196616 | tf_op jit(solution)/shard_map/ppermute | solution.py:315
  21.3 5.1 %collective-permute-start.3 = (bf16[8,4096]{1,0:T(8,128)(2,1)}, bf16[8,4096]{1,0:T(8,128)(2,1)S(1)}, u32[]{:S(2)}, u32[]{:S(2)}) collective-permute-start(bf16[8,4096]{1,0:T(8,128)(2,1)} %merge.1), channel_id=1, source_target_pairs={{0,16},{1,65},{2,18},{3,67},{4,20},{5,69},{6,22},{7,71},{8,24},{9,... | collective-permute-start | bytes 196616 | tf_op jit(solution)/shard_map/ppermute | solution.py:315
  23.4 25.9 %collective-permute-start.11 = (bf16[4096,128]{1,0:T(8,128)(2,1)S(1)}, bf16[4096,128]{1,0:T(8,128)(2,1)S(1)}, u32[]{:S(2)}, u32[]{:S(2)}) collective-permute-start(bf16[4096,128]{1,0:T(8,128)(2,1)S(1)} %copy-done), channel_id=1, source_target_pairs={{0,4},{1,17},{2,6},{3,19},{4,0},{5,21},{6,2},{7,23},{8,12},{9,25},... | collective-permute-start | bytes 3145736 | tf_op jit(solution)/shard_map/ppermute | solution.py:315
  27.2 10.7 %collective-permute-start.4 = (bf16[32,4096]{1,0:T(8,128)(2,1)S(1)}, bf16[32,4096]{1,0:T(8,128)(2,1)S(1)}, u32[]{:S(2)}, u32[]{:S(2)}) collective-permute-start(bf16[32,4096]{1,0:T(8,128)(2,1)S(1)} %pad_maximum_fusion), channel_id=1, source_target_pairs={{0,32},{1,3},{2,34},{3,5},{4,36},{5,7},{6,38},{7,1},{8,40},{9,11},... | collective-permute-start | bytes 786440 | tf_op jit(solution)/shard_map/ppermute | solution.py:315
  28.5 9.9 %collective-permute-start.5 = (bf16[32,4096]{1,0:T(8,128)(2,1)S(1)}, bf16[32,4096]{1,0:T(8,128)(2,1)S(1)}, u32[]{:S(2)}, u32[]{:S(2)}) collective-permute-start(bf16[32,4096]{1,0:T(8,128)(2,1)S(1)} %pad_maximum_fusion), channel_id=1, source_target_pairs={{0,96},{1,7},{2,98},{3,1},{4,100},{5,3},{6,102},{7,5},{8,104},{9,1... | collective-permute-start | bytes 786440 | tf_op jit(solution)/shard_map/ppermute | solution.py:315
  37.9 7.8 %collective-permute-start.6 = (bf16[32,4096]{1,0:T(8,128)(2,1)S(1)}, bf16[32,4096]{1,0:T(8,128)(2,1)S(1)}, u32[]{:S(2)}, u32[]{:S(2)}) collective-permute-start(bf16[32,4096]{1,0:T(8,128)(2,1)S(1)} %pad_maximum_fusion), channel_id=1, source_target_pairs={{0,64},{1,5},{2,66},{3,7},{4,68},{5,1},{6,70},{7,3},{8,72},{9,13},... | collective-permute-start | bytes 786440 | tf_op jit(solution)/shard_map/ppermute | solution.py:315
  46.2 6.3 %collective-permute-start.8 = (f32[128,128]{1,0:T(8,128)S(1)}, f32[128,128]{1,0:T(8,128)S(1)}, u32[]{:S(2)}, u32[]{:S(2)}) collective-permute-start(f32[128,128]{1,0:T(8,128)S(1)} %fusion.1), channel_id=1, source_target_pairs={{0,6},{1,25},{2,0},{3,27},{4,2},{5,29},{6,4},{7,31},{8,14},{9,1},{... | collective-permute-start | bytes 196616 | tf_op jit(solution)/shard_map/ppermute | solution.py:315
  49.2 4.7 %collective-permute-start.10 = (f32[128,128]{1,0:T(8,128)S(1)}, f32[128,128]{1,0:T(8,128)S(1)}, u32[]{:S(2)}, u32[]{:S(2)}) collective-permute-start(f32[128,128]{1,0:T(8,128)S(1)} %fusion.2), channel_id=1, source_target_pairs={{0,2},{1,9},{2,4},{3,11},{4,6},{5,13},{6,0},{7,15},{8,10},{9,17},{... | collective-permute-start | bytes 196616 | tf_op jit(solution)/shard_map/ppermute | solution.py:315
  49.7 4.7 %collective-permute-start.12 = (f32[128,128]{1,0:T(8,128)S(1)}, f32[128,128]{1,0:T(8,128)S(1)}, u32[]{:S(2)}, u32[]{:S(2)}) collective-permute-start(f32[128,128]{1,0:T(8,128)S(1)} %fusion.3), channel_id=1, source_target_pairs={{0,4},{1,17},{2,6},{3,19},{4,0},{5,21},{6,2},{7,23},{8,12},{9,25},... | collective-permute-start | bytes 196616 | tf_op jit(solution)/shard_map/ppermute | solution.py:315
  52.5 1.9 %copy-start.2 = (f32[128,128]{1,0:T(8,128)}, f32[128,128]{1,0:T(8,128)S(1)}, u32[]{:S(2)}) copy-start(f32[128,128]{1,0:T(8,128)S(1)} %collective-permute-done.8.p1_ref) | copy-start | bytes 196612
  53.9 0.6 %copy-start.3 = (f32[128,128]{1,0:T(8,128)}, f32[128,128]{1,0:T(8,128)S(1)}, u32[]{:S(2)}) copy-start(f32[128,128]{1,0:T(8,128)S(1)} %collective-permute-done.10.p2_ref) | copy-start | bytes 196612
  54.5 0.6 %copy-start.4 = (f32[128,128]{1,0:T(8,128)}, f32[128,128]{1,0:T(8,128)S(1)}, u32[]{:S(2)}) copy-start(f32[128,128]{1,0:T(8,128)S(1)} %collective-permute-done.12.p3_ref) | copy-start | bytes 196612
  56.9 1.6 %collective-permute-start.13 = (f32[256,128]{1,0:T(8,128)}, f32[256,128]{1,0:T(8,128)S(1)}, u32[]{:S(2)}, u32[]{:S(2)}) collective-permute-start(f32[256,128]{1,0:T(8,128)} %get-tuple-element.12), channel_id=1, source_target_pairs={{0,1},{1,0},{2,3},{3,2},{4,5},{5,4},{6,7},{7,6},{8,9},{9,8},{10,11... | collective-permute-start | bytes 393224 | tf_op jit(solution)/shard_map/ppermute | solution.py:293

commit v3 on v2

--- a/solution.py
+++ b/solution.py
@@ -43,14 +43,6 @@
         for half in range(2)
     ]
     return np.concatenate([np.arange(a, a + STRIP) for a in starts])
-
-
-def swap_halves(x):
-    return pltpu.roll(x, HALF, 1)
-
-
-def low_lanes(shape):
-    return lax.broadcasted_iota(jnp.int32, shape, 1) < HALF
 
 
 def dot(a, b):
@@ -211,21 +203,22 @@
             add_values(j, *weighed[j])
 
     for j in range(PAIRS):
-        summed = jnp.broadcast_to(jnp.sum(total[j], axis=1, keepdims=True), (ROWS, HEAD_DIM))
-        total[j] = jnp.where(low_lanes(summed.shape), peak[j], summed)
+        total[j] = jnp.broadcast_to(jnp.sum(total[j], axis=1, keepdims=True), (ROWS, HEAD_DIM))
     half = PAIRS // 2
-    for i in range(half):
-        at = slice(i * ROWS, (i + 1) * ROWS)
-        for ref, first in ((mine_ref, kv_at * half), (send_ref, (1 - kv_at) * half)):
-            ref[at, :HEAD_DIM] = numer[first + i]
-            ref[at, HEAD_DIM:] = total[first + i]
+    for ref, first in ((mine_ref, kv_at * half), (send_ref, (1 - kv_at) * half)):
+        for part, state in enumerate((numer, peak, total)):
+            for i in range(half):
+                whole = state[first + i]
+                for h in range(ROWS // Q_TOK):
+                    column = (i * (ROWS // Q_TOK) + h) * HEAD_DIM
+                    ref[part, :, column : column + HEAD_DIM] = whole[h * Q_TOK : (h + 1) * Q_TOK]
 
 
 def attend(length, latents, codes, scales, queries, new_keys, new_values, key_factor):
     f32, bf16 = jnp.float32, jnp.bfloat16
     vmem = pl.BlockSpec(memory_space=pltpu.VMEM)
     hbm = pl.BlockSpec(memory_space=pltpu.HBM)
-    shape = jax.ShapeDtypeStruct((PAIRS // 2 * ROWS, 2 * HEAD_DIM), f32)
+    shape = jax.ShapeDtypeStruct((3, Q_TOK, HEADS // 2 * HEAD_DIM), f32)
     macs = CTX_DEV * (RANK * KV_HEADS + 2 * PAIRS * ROWS * 2) * HEAD_DIM
     width = KV_HEADS * HEAD_DIM
     return pl.pallas_call(
@@ -253,40 +246,22 @@
             pltpu.VMEM((PAIRS, ROWS, HEAD_DIM), f32),
             pltpu.VMEM((PAIRS, ROWS, HEAD_DIM), f32),
         ],
-        compiler_params=pltpu.CompilerParams(vmem_limit_bytes=60 * 2**20),
+        compiler_params=pltpu.CompilerParams(vmem_limit_bytes=36 * 2**20),
         cost_estimate=pl.CostEstimate(
             flops=2 * macs, bytes_accessed=12 * 2**20, transcendentals=CTX_DEV * HEADS * Q_TOK
         ),
         name="attend",
-    )(length, latents.T, codes, jnp.asarray(rotary_table()), scales.T, queries, new_keys, new_values, key_factor)
-
-
-def merge_kernel(a_ref, b_ref, out_ref):
-    def parts(ref):
-        both = ref[:, HEAD_DIM:]
-        low, other = low_lanes(both.shape), swap_halves(both)
-        return ref[:, :HEAD_DIM], jnp.where(low, both, other), jnp.where(low, other, both)
-
-    numer_a, peak_a, total_a = parts(a_ref)
-    numer_b, peak_b, total_b = parts(b_ref)
-    peak = jnp.maximum(peak_a, peak_b)
-    weight_a = jnp.exp2((peak_a - peak) * EXP2_SCALE)
-    weight_b = jnp.exp2((peak_b - peak) * EXP2_SCALE)
-    out = (numer_a * weight_a + numer_b * weight_b) / (total_a * weight_a + total_b * weight_b)
-    out_ref[...] = jnp.concatenate(
-        [out[i : i + Q_TOK] for i in range(0, out.shape[0], Q_TOK)], axis=1
-    ).astype(out_ref.dtype)
-
-
-def merge(mine, other):
-    vmem = pl.BlockSpec(memory_space=pltpu.VMEM)
-    return pl.pallas_call(
-        merge_kernel,
-        out_shape=jax.ShapeDtypeStruct((Q_TOK, HEADS // 2 * HEAD_DIM), jnp.bfloat16),
-        in_specs=[vmem, vmem],
-        out_specs=vmem,
-        name="merge",
-    )(mine, other)
+    )(length, *[
+        pltpu.with_memory_space_constraint(x, pltpu.HBM)
+        for x in (latents.T, codes, jnp.asarray(rotary_table()), scales.T, queries, new_keys, new_values, key_factor)
+    ])
+
+
+def merge(a, b):
+    top = jnp.maximum(a[1], b[1])
+    weight_a, weight_b = (jnp.exp2((x[1] - top) * EXP2_SCALE) for x in (a, b))
+    numer = a[0] * weight_a + b[0] * weight_b
+    return (numer / (a[2] * weight_a + b[2] * weight_b)).astype(jnp.bfloat16)
 
 
 def other_core(x):
@@ -319,59 +294,64 @@
     return jnp.concatenate([x] + [shifted(x, axes, shift) for shift in SHIFTS], axis=0)
 
 
-def assemble_kernel(p0_ref, p1_ref, p2_ref, p3_ref, keep_ref, give_ref, whole):
+def assemble_kernel(*refs):
+    *pieces, out_ref, whole = refs
     chip, core = lax.axis_index("group"), lax.axis_index("kv")
-
-    def axis_at(axes):
-        return [lax.rem(lax.div(chip, AXES[axis]), SIDE) for axis in axes]
-
-    def place(axes, core_at):
-        return jnp.where(core_at == 0, *[jnp.int32(AXES[axis]) for axis in axes])
-
-    weight, first, second = (
-        jnp.where(core == 0, *axis_at(axes)) for axes in (WEIGHT_AXIS, FIRST_AXIS, SECOND_AXIS)
-    )
     steps = (0,) + SHIFTS
-    for ref, d in zip((p0_ref, p1_ref, p2_ref, p3_ref), steps):
-        for i, e in enumerate(steps):
-            for j, f in enumerate(steps):
-                request = (
-                    lax.rem(weight + (d + SIDE), SIDE) * place(WEIGHT_AXIS, core)
-                    + lax.rem(first + (SIDE - f), SIDE) * place(FIRST_AXIS, core)
-                    + lax.rem(second + (SIDE - e), SIDE) * place(SECOND_AXIS, core)
-                )
-                row = (i * SIDE + j) * Q_TOK
-                whole[pl.ds(pl.multiple_of(request * Q_TOK, Q_TOK), Q_TOK), :] = ref[row : row + Q_TOK, :]
-    half = whole.shape[0] // 2
-    keep_ref[...] = whole[pl.ds(pl.multiple_of(core * half, half), half), :]
-    give_ref[...] = whole[pl.ds(pl.multiple_of((1 - core) * half, half), half), :]
-
-
-def assemble(pieces):
+
+    def place(axes, at_core, shift):
+        value = jnp.int32(0)
+        for c, axis in enumerate(axes):
+            at = lax.rem(lax.div(chip, AXES[axis]) + (shift + SIDE), SIDE) * AXES[axis]
+            value = jnp.where(at_core == c, at, value)
+        return value
+
+    for at_core, refs in ((core, pieces[: len(steps)]), (1 - core, pieces[len(steps) :])):
+        for ref, d in zip(refs, steps):
+            for i, e in enumerate(steps):
+                for j, f in enumerate(steps):
+                    request = (
+                        place(WEIGHT_AXIS, at_core, d)
+                        + place(FIRST_AXIS, at_core, -f)
+                        + place(SECOND_AXIS, at_core, -e)
+                    )
+                    row = (i * SIDE + j) * Q_TOK
+                    at = pl.ds(pl.multiple_of(request * Q_TOK, Q_TOK), Q_TOK)
+                    block = ref[row : row + Q_TOK, :]
+                    whole[at, :] = block if at_core is core else whole[at, :] + block
+    half = out_ref.shape[0]
+    out_ref[...] = whole[pl.ds(pl.multiple_of(core * half, half), half), :]
+
+
+def assemble(own, other):
     vmem = pl.BlockSpec(memory_space=pltpu.VMEM)
-    rows, columns = SIDE * pieces[0].shape[0], pieces[0].shape[1]
-    shape = jax.ShapeDtypeStruct((rows // 2, columns), jnp.float32)
+    rows, columns = SIDE * own[0].shape[0], own[0].shape[1]
     return pl.pallas_call(
         assemble_kernel,
-        out_shape=(shape, shape),
-        in_specs=[vmem] * 4,
-        out_specs=(vmem, vmem),
+        out_shape=jax.ShapeDtypeStruct((rows // 2, columns), jnp.float32),
+        in_specs=[vmem] * 8,
+        out_specs=vmem,
         scratch_shapes=[pltpu.VMEM((rows, columns), jnp.float32)],
+        compiler_params=pltpu.CompilerParams(vmem_limit_bytes=4 * 2**20),
         name="assemble",
-    )(*pieces)
+    )(*own, *other)
 
 
 def body(lengths, latents, codes, scales, queries, new_keys, new_values, key_factor, out_weight):
-    weights = [out_weight] + [shifted(out_weight, WEIGHT_AXIS, shift) for shift in SHIFTS]
+    half = out_weight.shape[0] // 2
+    before, after = (shifted(out_weight, WEIGHT_AXIS, shift) for shift in SHIFTS[:2])
     mine, send = attend(
         lengths, latents[0], codes[0], scales[0], queries[0], new_keys[0], new_values[0], key_factor
     )
+    mine, before, after = lax.optimization_barrier((mine, before, after))
+    far = [shifted(before[:half], WEIGHT_AXIS, 1), shifted(after[half:], WEIGHT_AXIS, -1)]
     attended = merge(mine, other_core(send))
-    rows = gathered(gathered(attended, FIRST_AXIS), SECOND_AXIS)
-    results = [dot(rows, w) for w in weights]
+    rows = gathered(gathered(attended[None], FIRST_AXIS), SECOND_AXIS)
+    rows = rows.reshape(SIDE * SIDE * Q_TOK, HEADS // 2 * HEAD_DIM)
+    results = [dot(rows, w) for w in (out_weight, before, after)]
+    results.append(dot(rows[:, :half], far[0]) + dot(rows[:, half:], far[1]))
     pieces = [results[0]] + [shifted(r, WEIGHT_AXIS, -shift) for r, shift in zip(results[1:], SHIFTS)]
-    keep, give = assemble(pieces)
-    return keep + other_core(give)
+    return assemble(pieces, [other_core(p) for p in pieces])
 
 
 def solution(mesh):

time: 60.3 us -> 53.1 us (0.88)
  starting transfers between devices: 18.7 us -> 28.7 us
  Pallas kernels: 13.5 us -> 7.07 us
  waiting for transfers between devices: 19.8 us -> 14.3 us
  other arithmetic: 2.43 us -> 0.13 us
  local copies, waits for them, and re-layouts: 2.36 us -> 0.15 us
    ppermute x2 -> x5, starting transfers between devices: 1.63 us -> 9.65 us  [other_core(): return lax.ppermute(x, 'kv', [(0, 1), (1, 0)])]
    ppermute x12 -> x13, waiting for transfers between devices: 18.3 us -> 13.4 us  [shifted(): return lax.ppermute(x, ('group', 'kv'), moves)]
    pallas_call x1, Pallas kernels: 9.97 us -> 6.17 us  [attend(): pl.pallas_call(attend_kernel, out_shape=(shape, shape), in_specs=[pl.Bloc...]
    pallas_call x2 -> x1, Pallas kernels: 3.58 us -> 0.9 us  [assemble(): pl.pallas_call(assemble_kernel, out_shape=jax.ShapeDtypeStruct((rows // 2...]
    unnamed x16 -> x7, local copies, waits for them, and re-layouts: 2.35 us -> 0.06 us
    ppermute x12 -> x13, starting transfers between devices: 17.1 us -> 19 us  [shifted(): return lax.ppermute(x, ('group', 'kv'), moves)]
    add x1 -> x0, other arithmetic: 1.57 us -> none  [body(): return keep + other_core(give)]
    concatenate x1, other arithmetic: 0.86 us -> 0.04 us  [gathered(): jnp.concatenate([x] + [shifted(x, axes, shift) for shift in SHIFTS], axis=0)]
  transfers between devices with their start and end apart: 14 -> 18, of which waited for: 6 -> 6; matrix products, arithmetic and copies ran while one was open for 7% -> 4% of each run, Pallas kernels for 3% -> 12%
where the time goes in v3:
time: 53.1 us; the launch traced here: 53 us
  starting transfers between devices  28.7 us (54%)
  waiting for transfers between devices  14.3 us (27%)
  Pallas kernels  7.07 us (13%)
  matrix products  1.88 us (4%)
  between operations  0.79 us (1%)
    ppermute x13, starting transfers between devices, shifted(): return lax.ppermute(x, ('group', 'kv'), moves)  19 us
    ppermute x13, waiting for transfers between devices, shifted(): return lax.ppermute(x, ('group', 'kv'), moves)  13.4 us
    ppermute x5, starting transfers between devices, other_core(): return lax.ppermute(x, 'kv', [(0, 1), (1, 0)])  9.65 us
    pallas_call x1, Pallas kernels, attend(): pl.pallas_call(attend_kernel, out_shape=(shape, shape), in_specs=[pl.Bloc...  6.17 us
    dot_general x5, matrix products, dot(): return jnp.dot(a, b, preferred_element_type=jnp.float32)  1.88 us
  transfers between devices with their start and end apart: 18, of which 6 were waited for; matrix products, arithmetic and copies ran while one was open for 4% of the time, Pallas kernels for 12%

profile of v3, /device:TPU:1, one launch (start us, length us, event | category | flops | bytes accessed | tf_op | source)
XLA Modules:
  0.0 53.0 jit_solution(3437603073998384360)
XLA Ops:
  0.0 2.1 %collective-permute-start = (bf16[4096,128]{1,0:T(8,128)(2,1)}, bf16[4096,128]{1,0:T(8,128)(2,1)S(1)}, u32[]{:S(2)}, u32[]{:S(2)}) collective-permute-start(bf16[4096,128]{1,0:T(8,128)(2,1)} %param.18), channel_id=1, source_target_pairs={{0,2},{1,9},{2,4},{3,11},{4,6},{5,13},{6,0},{7,15},{8,10},{9,17},{... | collective-permute-start | bytes 3145736 | tf_op jit(solution)/shard_map/ppermute | solution.py:290
  2.1 1.4 %collective-permute-start.1 = (bf16[4096,128]{1,0:T(8,128)(2,1)}, bf16[4096,128]{1,0:T(8,128)(2,1)S(1)}, u32[]{:S(2)}, u32[]{:S(2)}) collective-permute-start(bf16[4096,128]{1,0:T(8,128)(2,1)} %param.18), channel_id=1, source_target_pairs={{0,6},{1,25},{2,0},{3,27},{4,2},{5,29},{6,4},{7,31},{8,14},{9,1},{... | collective-permute-start | bytes 3145736 | tf_op jit(solution)/shard_map/ppermute | solution.py:290
  4.2 6.2 %attend.1 = (f32[3,8,4096]{2,1,0:T(8,128)S(1)}, f32[3,8,4096]{2,1,0:T(8,128)S(1)}) custom-call(s32[1]{0:T(128)S(6)} %copy.17.length_ref, bf16[160,4096]{1,0:T(8,128)(2,1)} %bitcast.25, bf16[4096,1024]{1,0:T(8,128)(2,1)} %bitcast.24, f32[2,2,64,4096]{3,2,1,0:T(8,128)} %constant.7.clone.table_hbm, bf16[8,16]{1,0:T(8,128)(2,1)} %bitcast.29, ...), custom_call_target="tpu_custom_call" | custom-call | flops 3489660928 | bytes 12582912 | tf_op jit(solution)/shard_map/attend/pallas_call | solution.py:224
  10.4 4.1 %collective-permute-start.2 = (f32[3,8,4096]{2,1,0:T(8,128)S(1)}, f32[3,8,4096]{2,1,0:T(8,128)S(1)}, u32[]{:S(2)}, u32[]{:S(2)}) collective-permute-start(f32[3,8,4096]{2,1,0:T(8,128)S(1)} %get-tuple-element.12), channel_id=1, source_target_pairs={{0,1},{1,0},{2,3},{3,2},{4,5},{5,4},{6,7},{7,6},{8,9},{9,8},{10,11... | collective-permute-start | bytes 1179656 | tf_op jit(solution)/shard_map/ppermute | solution.py:268
  14.5 1.7 %collective-permute-done = bf16[4096,128]{1,0:T(8,128)(2,1)S(1)} collective-permute-done((bf16[4096,128]{1,0:T(8,128)(2,1)}, bf16[4096,128]{1,0:T(8,128)(2,1)S(1)}, u32[]{:S(2)}, u32[]{:S(2)}) %collective-permute-start) | collective-permute-done | bytes 1048608 | tf_op jit(solution)/shard_map/ppermute | solution.py:290
  16.4 1.7 %collective-permute-start.3 = (bf16[1,8,4096]{2,1,0:T(8,128)(2,1)S(1)}, bf16[1,8,4096]{2,1,0:T(8,128)(2,1)S(1)}, u32[]{:S(2)}, u32[]{:S(2)}) collective-permute-start(bf16[1,8,4096]{2,1,0:T(8,128)(2,1)S(1)} %get-tuple-element.16), channel_id=1, source_target_pairs={{0,8},{1,33},{2,10},{3,35},{4,12},{5,37},{6,14},{7,39},{8,16},{9,4... | collective-permute-start | bytes 196616 | tf_op jit(solution)/shard_map/ppermute | solution.py:290
  18.1 2.2 %collective-permute-start.4 = (bf16[1,8,4096]{2,1,0:T(8,128)(2,1)S(1)}, bf16[1,8,4096]{2,1,0:T(8,128)(2,1)S(1)}, u32[]{:S(2)}, u32[]{:S(2)}) collective-permute-start(bf16[1,8,4096]{2,1,0:T(8,128)(2,1)S(1)} %get-tuple-element.16), channel_id=1, source_target_pairs={{0,24},{1,97},{2,26},{3,99},{4,28},{5,101},{6,30},{7,103},{8,0},{9... | collective-permute-start | bytes 196616 | tf_op jit(solution)/shard_map/ppermute | solution.py:290
  20.3 1.2 %collective-permute-start.5 = (bf16[1,8,4096]{2,1,0:T(8,128)(2,1)S(1)}, bf16[1,8,4096]{2,1,0:T(8,128)(2,1)S(1)}, u32[]{:S(2)}, u32[]{:S(2)}) collective-permute-start(bf16[1,8,4096]{2,1,0:T(8,128)(2,1)S(1)} %get-tuple-element.16), channel_id=1, source_target_pairs={{0,16},{1,65},{2,18},{3,67},{4,20},{5,69},{6,22},{7,71},{8,24},{9,... | collective-permute-start | bytes 196616 | tf_op jit(solution)/shard_map/ppermute | solution.py:290
  21.6 2.7 %collective-permute-start.12 = (bf16[2048,128]{1,0:T(8,128)(2,1)S(1)}, bf16[2048,128]{1,0:T(8,128)(2,1)S(1)}, u32[]{:S(2)}, u32[]{:S(2)}) collective-permute-start(bf16[2048,128]{1,0:T(8,128)(2,1)S(1)} %slice.41), channel_id=1, source_target_pairs={{0,6},{1,25},{2,0},{3,27},{4,2},{5,29},{6,4},{7,31},{8,14},{9,1},{... | collective-permute-start | bytes 1572872 | tf_op jit(solution)/shard_map/ppermute | solution.py:290
  24.4 0.5 collective-permute-done.5
  25.0 1.3 %collective-permute-start.6 = (bf16[4,8,4096]{2,1,0:T(8,128)(2,1)S(1)}, bf16[4,8,4096]{2,1,0:T(8,128)(2,1)S(1)}, u32[]{:S(2)}, u32[]{:S(2)}) collective-permute-start(bf16[4,8,4096]{2,1,0:T(8,128)(2,1)S(1)} %pad_maximum_fusion), channel_id=1, source_target_pairs={{0,32},{1,3},{2,34},{3,5},{4,36},{5,7},{6,38},{7,1},{8,40},{9,11},... | collective-permute-start | bytes 786440 | tf_op jit(solution)/shard_map/ppermute | solution.py:290
  26.2 1.5 %collective-permute-start.7 = (bf16[4,8,4096]{2,1,0:T(8,128)(2,1)S(1)}, bf16[4,8,4096]{2,1,0:T(8,128)(2,1)S(1)}, u32[]{:S(2)}, u32[]{:S(2)}) collective-permute-start(bf16[4,8,4096]{2,1,0:T(8,128)(2,1)S(1)} %pad_maximum_fusion), channel_id=1, source_target_pairs={{0,96},{1,7},{2,98},{3,1},{4,100},{5,3},{6,102},{7,5},{8,104},{9,1... | collective-permute-start | bytes 786440 | tf_op jit(solution)/shard_map/ppermute | solution.py:290
  27.7 1.5 %collective-permute-start.8 = (bf16[4,8,4096]{2,1,0:T(8,128)(2,1)S(1)}, bf16[4,8,4096]{2,1,0:T(8,128)(2,1)S(1)}, u32[]{:S(2)}, u32[]{:S(2)}) collective-permute-start(bf16[4,8,4096]{2,1,0:T(8,128)(2,1)S(1)} %pad_maximum_fusion), channel_id=1, source_target_pairs={{0,64},{1,5},{2,66},{3,7},{4,68},{5,1},{6,70},{7,3},{8,72},{9,13},... | collective-permute-start | bytes 786440 | tf_op jit(solution)/shard_map/ppermute | solution.py:290
  29.3 3.2 %collective-permute-done.6 = bf16[4,8,4096]{2,1,0:T(8,128)(2,1)S(1)} collective-permute-done((bf16[4,8,4096]{2,1,0:T(8,128)(2,1)S(1)}, bf16[4,8,4096]{2,1,0:T(8,128)(2,1)S(1)}, u32[]{:S(2)}, u32[]{:S(2)}) %collective-permute-start.6) | collective-permute-done | bytes 262176 | tf_op jit(solution)/shard_map/ppermute | solution.py:290
  32.5 2.1 %collective-permute-done.7 = bf16[4,8,4096]{2,1,0:T(8,128)(2,1)S(1)} collective-permute-done((bf16[4,8,4096]{2,1,0:T(8,128)(2,1)S(1)}, bf16[4,8,4096]{2,1,0:T(8,128)(2,1)S(1)}, u32[]{:S(2)}, u32[]{:S(2)}) %collective-permute-start.7) | collective-permute-done | bytes 262176 | tf_op jit(solution)/shard_map/ppermute | solution.py:290
  34.6 5.8 %collective-permute-done.8 = bf16[4,8,4096]{2,1,0:T(8,128)(2,1)S(1)} collective-permute-done((bf16[4,8,4096]{2,1,0:T(8,128)(2,1)S(1)}, bf16[4,8,4096]{2,1,0:T(8,128)(2,1)S(1)}, u32[]{:S(2)}, u32[]{:S(2)}) %collective-permute-start.8) | collective-permute-done | bytes 262176 | tf_op jit(solution)/shard_map/ppermute | solution.py:290
  40.5 0.4 fusion.13
  40.9 1.2 %collective-permute-start.9 = (f32[128,128]{1,0:T(8,128)S(1)}, f32[128,128]{1,0:T(8,128)S(1)}, u32[]{:S(2)}, u32[]{:S(2)}) collective-permute-start(f32[128,128]{1,0:T(8,128)S(1)} %fusion.13), channel_id=1, source_target_pairs={{0,6},{1,25},{2,0},{3,27},{4,2},{5,29},{6,4},{7,31},{8,14},{9,1},{... | collective-permute-start | bytes 196616 | tf_op jit(solution)/shard_map/ppermute | solution.py:290
  43.6 1.7 %collective-permute-start.13 = (f32[128,128]{1,0:T(8,128)S(1)}, f32[128,128]{1,0:T(8,128)S(1)}, u32[]{:S(2)}, u32[]{:S(2)}) collective-permute-start(f32[128,128]{1,0:T(8,128)S(1)} %convolution_add_fusion), channel_id=1, source_target_pairs={{0,4},{1,17},{2,6},{3,19},{4,0},{5,21},{6,2},{7,23},{8,12},{9,25},... | collective-permute-start | bytes 196616 | tf_op jit(solution)/shard_map/ppermute | solution.py:290
  45.7 2.1 %collective-permute-start.14 = (f32[128,128]{1,0:T(8,128)S(1)}, f32[128,128]{1,0:T(8,128)S(1)}, u32[]{:S(2)}, u32[]{:S(2)}) collective-permute-start(f32[128,128]{1,0:T(8,128)S(1)} %fusion.15.refs_0_), channel_id=1, source_target_pairs={{0,1},{1,0},{2,3},{3,2},{4,5},{5,4},{6,7},{7,6},{8,9},{9,8},{10,11... | collective-permute-start | bytes 196616 | tf_op jit(solution)/shard_map/ppermute | solution.py:268
  47.8 2.4 %collective-permute-start.16 = (f32[128,128]{1,0:T(8,128)S(1)}, f32[128,128]{1,0:T(8,128)S(1)}, u32[]{:S(2)}, u32[]{:S(2)}) collective-permute-start(f32[128,128]{1,0:T(8,128)S(1)} %collective-permute-done.10.refs_2_), channel_id=1, source_target_pairs={{0,1},{1,0},{2,3},{3,2},{4,5},{5,4},{6,7},{7,6},{8,9},{9,8},{10,11... | collective-permute-start | bytes 196616 | tf_op jit(solution)/shard_map/ppermute | solution.py:268
  50.2 1.0 %collective-permute-start.17 = (f32[128,128]{1,0:T(8,128)S(1)}, f32[128,128]{1,0:T(8,128)S(1)}, u32[]{:S(2)}, u32[]{:S(2)}) collective-permute-start(f32[128,128]{1,0:T(8,128)S(1)} %collective-permute-done.13.refs_3_), channel_id=1, source_target_pairs={{0,1},{1,0},{2,3},{3,2},{4,5},{5,4},{6,7},{7,6},{8,9},{9,8},{10,11... | collective-permute-start | bytes 196616 | tf_op jit(solution)/shard_map/ppermute | solution.py:268
  51.2 0.9 %collective-permute-done.17.refs_7_ = f32[128,128]{1,0:T(8,128)S(1)} collective-permute-done((f32[128,128]{1,0:T(8,128)S(1)}, f32[128,128]{1,0:T(8,128)S(1)}, u32[]{:S(2)}, u32[]{:S(2)}) %collective-permute-start.17) | collective-permute-done | bytes 65568 | tf_op jit(solution)/shard_map/ppermute | solution.py:268
  52.1 0.9 %assemble.1 = f32[256,128]{1,0:T(8,128)} custom-call(f32[128,128]{1,0:T(8,128)S(1)} %fusion.15.refs_0_, f32[128,128]{1,0:T(8,128)S(1)} %collective-permute-done.9.refs_1_, f32[128,128]{1,0:T(8,128)S(1)} %collective-permute-done.10.refs_2_, f32[128,128]{1,0:T(8,128)S(1)} %collective-permute-done.13.refs_3_, f32[128,128]{1,0:T(8,128)S(1)} %collective-permute-done.14.refs_4_, ...), custom_call_target="tpu_custom_call" | custom-call | tf_op jit(solution)/shard_map/assemble/pallas_call | solution.py:329
  (31 shorter events, 2.4 us)
Async XLA Ops:
  0.0 16.3 %collective-permute-start = (bf16[4096,128]{1,0:T(8,128)(2,1)}, bf16[4096,128]{1,0:T(8,128)(2,1)S(1)}, u32[]{:S(2)}, u32[]{:S(2)}) collective-permute-start(bf16[4096,128]{1,0:T(8,128)(2,1)} %param.18), channel_id=1, source_target_pairs={{0,2},{1,9},{2,4},{3,11},{4,6},{5,13},{6,0},{7,15},{8,10},{9,17},{... | collective-permute-start | bytes 3145736 | tf_op jit(solution)/shard_map/ppermute | solution.py:290
  2.1 14.2 %collective-permute-start.1 = (bf16[4096,128]{1,0:T(8,128)(2,1)}, bf16[4096,128]{1,0:T(8,128)(2,1)S(1)}, u32[]{:S(2)}, u32[]{:S(2)}) collective-permute-start(bf16[4096,128]{1,0:T(8,128)(2,1)} %param.18), channel_id=1, source_target_pairs={{0,6},{1,25},{2,0},{3,27},{4,2},{5,29},{6,4},{7,31},{8,14},{9,1},{... | collective-permute-start | bytes 3145736 | tf_op jit(solution)/shard_map/ppermute | solution.py:290
  10.4 5.9 %collective-permute-start.2 = (f32[3,8,4096]{2,1,0:T(8,128)S(1)}, f32[3,8,4096]{2,1,0:T(8,128)S(1)}, u32[]{:S(2)}, u32[]{:S(2)}) collective-permute-start(f32[3,8,4096]{2,1,0:T(8,128)S(1)} %get-tuple-element.12), channel_id=1, source_target_pairs={{0,1},{1,0},{2,3},{3,2},{4,5},{5,4},{6,7},{7,6},{8,9},{9,8},{10,11... | collective-permute-start | bytes 1179656 | tf_op jit(solution)/shard_map/ppermute | solution.py:268
  16.4 8.0 %collective-permute-start.3 = (bf16[1,8,4096]{2,1,0:T(8,128)(2,1)S(1)}, bf16[1,8,4096]{2,1,0:T(8,128)(2,1)S(1)}, u32[]{:S(2)}, u32[]{:S(2)}) collective-permute-start(bf16[1,8,4096]{2,1,0:T(8,128)(2,1)S(1)} %get-tuple-element.16), channel_id=1, source_target_pairs={{0,8},{1,33},{2,10},{3,35},{4,12},{5,37},{6,14},{7,39},{8,16},{9,4... | collective-permute-start | bytes 196616 | tf_op jit(solution)/shard_map/ppermute | solution.py:290
  18.1 6.3 %collective-permute-start.4 = (bf16[1,8,4096]{2,1,0:T(8,128)(2,1)S(1)}, bf16[1,8,4096]{2,1,0:T(8,128)(2,1)S(1)}, u32[]{:S(2)}, u32[]{:S(2)}) collective-permute-start(bf16[1,8,4096]{2,1,0:T(8,128)(2,1)S(1)} %get-tuple-element.16), channel_id=1, source_target_pairs={{0,24},{1,97},{2,26},{3,99},{4,28},{5,101},{6,30},{7,103},{8,0},{9... | collective-permute-start | bytes 196616 | tf_op jit(solution)/shard_map/ppermute | solution.py:290
  20.3 4.6 %collective-permute-start.5 = (bf16[1,8,4096]{2,1,0:T(8,128)(2,1)S(1)}, bf16[1,8,4096]{2,1,0:T(8,128)(2,1)S(1)}, u32[]{:S(2)}, u32[]{:S(2)}) collective-permute-start(bf16[1,8,4096]{2,1,0:T(8,128)(2,1)S(1)} %get-tuple-element.16), channel_id=1, source_target_pairs={{0,16},{1,65},{2,18},{3,67},{4,20},{5,69},{6,22},{7,71},{8,24},{9,... | collective-permute-start | bytes 196616 | tf_op jit(solution)/shard_map/ppermute | solution.py:290
  21.6 21.4 %collective-permute-start.12 = (bf16[2048,128]{1,0:T(8,128)(2,1)S(1)}, bf16[2048,128]{1,0:T(8,128)(2,1)S(1)}, u32[]{:S(2)}, u32[]{:S(2)}) collective-permute-start(bf16[2048,128]{1,0:T(8,128)(2,1)S(1)} %slice.41), channel_id=1, source_target_pairs={{0,6},{1,25},{2,0},{3,27},{4,2},{5,29},{6,4},{7,31},{8,14},{9,1},{... | collective-permute-start | bytes 1572872 | tf_op jit(solution)/shard_map/ppermute | solution.py:290
  24.3 19.0 %collective-permute-start.11 = (bf16[2048,128]{1,0:T(8,128)(2,1)S(1)}, bf16[2048,128]{1,0:T(8,128)(2,1)S(1)}, u32[]{:S(2)}, u32[]{:S(2)}) collective-permute-start(bf16[2048,128]{1,0:T(8,128)(2,1)S(1)} %slice.39), channel_id=1, source_target_pairs={{0,2},{1,9},{2,4},{3,11},{4,6},{5,13},{6,0},{7,15},{8,10},{9,17},{... | collective-permute-start | bytes 1572872 | tf_op jit(solution)/shard_map/ppermute | solution.py:290
  25.0 7.5 %collective-permute-start.6 = (bf16[4,8,4096]{2,1,0:T(8,128)(2,1)S(1)}, bf16[4,8,4096]{2,1,0:T(8,128)(2,1)S(1)}, u32[]{:S(2)}, u32[]{:S(2)}) collective-permute-start(bf16[4,8,4096]{2,1,0:T(8,128)(2,1)S(1)} %pad_maximum_fusion), channel_id=1, source_target_pairs={{0,32},{1,3},{2,34},{3,5},{4,36},{5,7},{6,38},{7,1},{8,40},{9,11},... | collective-permute-start | bytes 786440 | tf_op jit(solution)/shard_map/ppermute | solution.py:290
  26.2 8.4 %collective-permute-start.7 = (bf16[4,8,4096]{2,1,0:T(8,128)(2,1)S(1)}, bf16[4,8,4096]{2,1,0:T(8,128)(2,1)S(1)}, u32[]{:S(2)}, u32[]{:S(2)}) collective-permute-start(bf16[4,8,4096]{2,1,0:T(8,128)(2,1)S(1)} %pad_maximum_fusion), channel_id=1, source_target_pairs={{0,96},{1,7},{2,98},{3,1},{4,100},{5,3},{6,102},{7,5},{8,104},{9,1... | collective-permute-start | bytes 786440 | tf_op jit(solution)/shard_map/ppermute | solution.py:290
  27.7 12.8 %collective-permute-start.8 = (bf16[4,8,4096]{2,1,0:T(8,128)(2,1)S(1)}, bf16[4,8,4096]{2,1,0:T(8,128)(2,1)S(1)}, u32[]{:S(2)}, u32[]{:S(2)}) collective-permute-start(bf16[4,8,4096]{2,1,0:T(8,128)(2,1)S(1)} %pad_maximum_fusion), channel_id=1, source_target_pairs={{0,64},{1,5},{2,66},{3,7},{4,68},{5,1},{6,70},{7,3},{8,72},{9,13},... | collective-permute-start | bytes 786440 | tf_op jit(solution)/shard_map/ppermute | solution.py:290
  29.2 16.0 %copy-start = (bf16[4096,128]{1,0:T(8,128)(2,1)S(1)}, bf16[4096,128]{1,0:T(8,128)(2,1)}, u32[]{:S(2)}) copy-start(bf16[4096,128]{1,0:T(8,128)(2,1)} %param.18) | copy-start | bytes 3145732
  40.9 6.8 %collective-permute-start.9 = (f32[128,128]{1,0:T(8,128)S(1)}, f32[128,128]{1,0:T(8,128)S(1)}, u32[]{:S(2)}, u32[]{:S(2)}) collective-permute-start(f32[128,128]{1,0:T(8,128)S(1)} %fusion.13), channel_id=1, source_target_pairs={{0,6},{1,25},{2,0},{3,27},{4,2},{5,29},{6,4},{7,31},{8,14},{9,1},{... | collective-permute-start | bytes 196616 | tf_op jit(solution)/shard_map/ppermute | solution.py:290
  42.6 5.3 %collective-permute-start.10 = (f32[128,128]{1,0:T(8,128)S(1)}, f32[128,128]{1,0:T(8,128)S(1)}, u32[]{:S(2)}, u32[]{:S(2)}) collective-permute-start(f32[128,128]{1,0:T(8,128)S(1)} %fusion.11), channel_id=1, source_target_pairs={{0,2},{1,9},{2,4},{3,11},{4,6},{5,13},{6,0},{7,15},{8,10},{9,17},{... | collective-permute-start | bytes 196616 | tf_op jit(solution)/shard_map/ppermute | solution.py:290
  43.6 6.6 %collective-permute-start.13 = (f32[128,128]{1,0:T(8,128)S(1)}, f32[128,128]{1,0:T(8,128)S(1)}, u32[]{:S(2)}, u32[]{:S(2)}) collective-permute-start(f32[128,128]{1,0:T(8,128)S(1)} %convolution_add_fusion), channel_id=1, source_target_pairs={{0,4},{1,17},{2,6},{3,19},{4,0},{5,21},{6,2},{7,23},{8,12},{9,25},... | collective-permute-start | bytes 196616 | tf_op jit(solution)/shard_map/ppermute | solution.py:290
  45.7 5.5 %collective-permute-start.14 = (f32[128,128]{1,0:T(8,128)S(1)}, f32[128,128]{1,0:T(8,128)S(1)}, u32[]{:S(2)}, u32[]{:S(2)}) collective-permute-start(f32[128,128]{1,0:T(8,128)S(1)} %fusion.15.refs_0_), channel_id=1, source_target_pairs={{0,1},{1,0},{2,3},{3,2},{4,5},{5,4},{6,7},{7,6},{8,9},{9,8},{10,11... | collective-permute-start | bytes 196616 | tf_op jit(solution)/shard_map/ppermute | solution.py:268
  47.7 3.5 %collective-permute-start.15 = (f32[128,128]{1,0:T(8,128)S(1)}, f32[128,128]{1,0:T(8,128)S(1)}, u32[]{:S(2)}, u32[]{:S(2)}) collective-permute-start(f32[128,128]{1,0:T(8,128)S(1)} %collective-permute-done.9.refs_1_), channel_id=1, source_target_pairs={{0,1},{1,0},{2,3},{3,2},{4,5},{5,4},{6,7},{7,6},{8,9},{9,8},{10,11... | collective-permute-start | bytes 196616 | tf_op jit(solution)/shard_map/ppermute | solution.py:268
  47.8 3.4 %collective-permute-start.16 = (f32[128,128]{1,0:T(8,128)S(1)}, f32[128,128]{1,0:T(8,128)S(1)}, u32[]{:S(2)}, u32[]{:S(2)}) collective-permute-start(f32[128,128]{1,0:T(8,128)S(1)} %collective-permute-done.10.refs_2_), channel_id=1, source_target_pairs={{0,1},{1,0},{2,3},{3,2},{4,5},{5,4},{6,7},{7,6},{8,9},{9,8},{10,11... | collective-permute-start | bytes 196616 | tf_op jit(solution)/shard_map/ppermute | solution.py:268
  50.2 1.9 %collective-permute-start.17 = (f32[128,128]{1,0:T(8,128)S(1)}, f32[128,128]{1,0:T(8,128)S(1)}, u32[]{:S(2)}, u32[]{:S(2)}) collective-permute-start(f32[128,128]{1,0:T(8,128)S(1)} %collective-permute-done.13.refs_3_), channel_id=1, source_target_pairs={{0,1},{1,0},{2,3},{3,2},{4,5},{5,4},{6,7},{7,6},{8,9},{9,8},{10,11... | collective-permute-start | bytes 196616 | tf_op jit(solution)/shard_map/ppermute | solution.py:268

commit v4 on v3

--- a/solution.py
+++ b/solution.py
@@ -58,7 +58,7 @@
     mine_ref, send_ref,
     lat_buf, code_buf, table_buf, scale_buf, q_buf, nk_buf, nv_buf, kf_buf,
     lat_sem, code_sem, table_sem, small_sem,
-    qc, wt, scale_rows, peak, total, numer,
+    qc, wt, scale_rows, peak, total, numer, scores,
 ):
     f32, bf16 = jnp.float32, jnp.bfloat16
     kv_at = lax.axis_index("kv")
@@ -74,18 +74,26 @@
     for copy in small:
         copy.start()
 
-    def copies(c):
-        at = pl.ds(pl.multiple_of(c * CHUNK, CHUNK), CHUNK)
+    def at(c):
+        return pl.ds(pl.multiple_of(c * CHUNK, CHUNK), CHUNK)
+
+    def key_copies(c):
         return (
-            pltpu.make_async_copy(lat_hbm.at[:, at], lat_buf.at[:, at], lat_sem.at[c]),
-            pltpu.make_async_copy(table_hbm.at[kv_at, :, :, at], table_buf.at[:, :, at], table_sem.at[c]),
-            pltpu.make_async_copy(code_hbm.at[at], code_buf.at[at], code_sem.at[c]),
+            pltpu.make_async_copy(lat_hbm.at[:, at(c)], lat_buf.at[:, at(c)], lat_sem.at[c]),
+            pltpu.make_async_copy(table_hbm.at[kv_at, :, :, at(c)], table_buf.at[:, :, at(c)], table_sem.at[c]),
         )
+
+    def code_copy(c):
+        return pltpu.make_async_copy(code_hbm.at[at(c)], code_buf.at[at(c)], code_sem.at[c])
 
     @pl.loop(0, chunks)
     def _(c):
-        for copy in copies(c):
+        for copy in key_copies(c):
             copy.start()
+
+    @pl.loop(0, chunks)
+    def _(c):
+        code_copy(c).start()
 
     for copy in small:
         copy.wait()
@@ -141,17 +149,14 @@
         total[j] = weights
         numer[j] = own_blocks(dot(weights.astype(bf16), fresh_values))
 
-    @pl.loop(0, chunks)
-    def _(c):
-        for copy in copies(c):
+    def make_keys(c):
+        for copy in key_copies(c):
             copy.wait()
-        at = pl.ds(pl.multiple_of(c * CHUNK, CHUNK), CHUNK)
-        lat = lat_buf[:, at]
-        position = c * CHUNK + lax.broadcasted_iota(jnp.int32, (1, CHUNK), 1)
-        hide = jnp.where(position < valid, 0.0, NEG_FILL)
-        def make_keys(j):
+        lat = lat_buf[:, at(c)]
+        every = []
+        for j in range(PAIRS):
             columns = slice(2 * j * HEAD_DIM, (2 * j + 2) * HEAD_DIM)
-            cos, sin = table_buf[0, :, at], table_buf[1, :, at]
+            cos, sin = table_buf[0, :, at(c)], table_buf[1, :, at(c)]
             pre = dot(wt[columns, :], lat)
             keys = []
             for m in range(HALF // STRIP):
@@ -161,46 +166,65 @@
                     lo, hi = pre[at_lo : at_lo + STRIP], pre[at_lo + STRIP : at_lo + 2 * STRIP]
                     keys.append((lo * cos[here] - hi * sin[here]).astype(bf16))
                     keys.append((hi * cos[here] + lo * sin[here]).astype(bf16))
-            return jnp.concatenate(keys, axis=0)
-
-        def make_scores(j, keys):
-            return dot(qc[j], keys) + hide
-
-        def weigh(j, s):
-            old = peak[j]
-            new = jnp.maximum(old, jnp.max(s, axis=1, keepdims=True))
-            shrink = jnp.exp2((old - new) * EXP2_SCALE)
-            weights = [
-                jnp.exp2((s[:, i : i + HEAD_DIM] - new) * EXP2_SCALE) for i in range(0, CHUNK, HEAD_DIM)
-            ]
-            peak[j] = new
-            total[j] = total[j] * shrink + functools.reduce(jnp.add, weights)
-            return shrink, [w.astype(bf16) for w in weights]
-
-        def add_values(j, shrink, rounded):
-            columns = slice(2 * j * HEAD_DIM, (2 * j + 2) * HEAD_DIM)
-            result = numer[j] * shrink
-            for b in range(CHUNK // BLK):
-                per = BLK // HEAD_DIM
-                w = jnp.concatenate(rounded[b * per : (b + 1) * per], axis=1)
-                v = code_buf[pl.ds(pl.multiple_of(c * CHUNK + b * BLK, BLK), BLK), columns]
-                part = own_blocks(dot(w, v))
-                block = c * (CHUNK // BLK) + b
-                factor = jnp.concatenate(
-                    [
-                        jnp.broadcast_to(scale_rows[block, 2 * j + i : 2 * j + i + 1, :], (ROWS // 2, HEAD_DIM))
-                        for i in range(2)
-                    ],
-                    axis=0,
-                )
-                result = result + part * factor
-            numer[j] = result
-
-        all_keys = [make_keys(j) for j in range(PAIRS)]
-        all_scores = [make_scores(j, all_keys[j]) for j in range(PAIRS)]
-        weighed = [weigh(j, all_scores[j]) for j in range(PAIRS)]
+            every.append(jnp.concatenate(keys, axis=0))
+        return every
+
+    def make_scores(c, keys):
+        position = c * CHUNK + lax.broadcasted_iota(jnp.int32, (1, CHUNK), 1)
+        hide = jnp.where(position < valid, 0.0, NEG_FILL)
         for j in range(PAIRS):
-            add_values(j, *weighed[j])
+            scores[j] = dot(qc[j], keys[j]) + hide
+
+    def weigh(j):
+        s = scores[j]
+        old = peak[j]
+        new = jnp.maximum(old, jnp.max(s, axis=1, keepdims=True))
+        shrink = jnp.exp2((old - new) * EXP2_SCALE)
+        weights = [
+            jnp.exp2((s[:, i : i + HEAD_DIM] - new) * EXP2_SCALE) for i in range(0, CHUNK, HEAD_DIM)
+        ]
+        peak[j] = new
+        total[j] = total[j] * shrink + functools.reduce(jnp.add, weights)
+        return shrink, [w.astype(bf16) for w in weights]
+
+    def add_values(c, j, shrink, rounded):
+        columns = slice(2 * j * HEAD_DIM, (2 * j + 2) * HEAD_DIM)
+        result = numer[j] * shrink
+        for b in range(CHUNK // BLK):
+            per = BLK // HEAD_DIM
+            w = jnp.concatenate(rounded[b * per : (b + 1) * per], axis=1)
+            v = code_buf[pl.ds(pl.multiple_of(c * CHUNK + b * BLK, BLK), BLK), columns]
+            part = own_blocks(dot(w, v))
+            block = c * (CHUNK // BLK) + b
+            factor = jnp.concatenate(
+                [
+                    jnp.broadcast_to(scale_rows[block, 2 * j + i : 2 * j + i + 1, :], (ROWS // 2, HEAD_DIM))
+                    for i in range(2)
+                ],
+                axis=0,
+            )
+            result = result + part * factor
+        numer[j] = result
+
+    @pl.when(chunks > 0)
+    def _():
+        make_scores(0, make_keys(0))
+
+    @pl.loop(0, chunks - 1)
+    def _(c):
+        code_copy(c).wait()
+        keys = make_keys(c + 1)
+        weighed = [weigh(j) for j in range(PAIRS)]
+        make_scores(c + 1, keys)
+        for j in range(PAIRS):
+            add_values(c, j, *weighed[j])
+
+    @pl.when(chunks > 0)
+    def _():
+        code_copy(chunks - 1).wait()
+        weighed = [weigh(j) for j in range(PAIRS)]
+        for j in range(PAIRS):
+            add_values(chunks - 1, j, *weighed[j])
 
     for j in range(PAIRS):
         total[j] = jnp.broadcast_to(jnp.sum(total[j], axis=1, keepdims=True), (ROWS, HEAD_DIM))
@@ -245,6 +269,7 @@
             pltpu.VMEM((PAIRS, ROWS, HEAD_DIM), f32),
             pltpu.VMEM((PAIRS, ROWS, HEAD_DIM), f32),
             pltpu.VMEM((PAIRS, ROWS, HEAD_DIM), f32),
+            pltpu.VMEM((PAIRS, ROWS, CHUNK), f32),
         ],
         compiler_params=pltpu.CompilerParams(vmem_limit_bytes=36 * 2**20),
         cost_estimate=pl.CostEstimate(
@@ -274,6 +299,7 @@
 FIRST_AXIS = ("y", "z")
 SECOND_AXIS = ("z", "x")
 SHIFTS = (1, -1, 2)
+FIRST_SHIFTS = (2, 1, -1)
 
 
 def coordinate(chip, axis):
@@ -309,7 +335,7 @@
     for at_core, refs in ((core, pieces[: len(steps)]), (1 - core, pieces[len(steps) :])):
         for ref, d in zip(refs, steps):
             for i, e in enumerate(steps):
-                for j, f in enumerate(steps):
+                for j, f in enumerate((0,) + FIRST_SHIFTS):
                     request = (
                         place(WEIGHT_AXIS, at_core, d)
                         + place(FIRST_AXIS, at_core, -f)
@@ -338,18 +364,25 @@
 
 
 def body(lengths, latents, codes, scales, queries, new_keys, new_values, key_factor, out_weight):
-    half = out_weight.shape[0] // 2
+    cut = out_weight.shape[0] // 16
     before, after = (shifted(out_weight, WEIGHT_AXIS, shift) for shift in SHIFTS[:2])
     mine, send = attend(
         lengths, latents[0], codes[0], scales[0], queries[0], new_keys[0], new_values[0], key_factor
     )
-    mine, before, after = lax.optimization_barrier((mine, before, after))
-    far = [shifted(before[:half], WEIGHT_AXIS, 1), shifted(after[half:], WEIGHT_AXIS, -1)]
-    attended = merge(mine, other_core(send))
-    rows = gathered(gathered(attended[None], FIRST_AXIS), SECOND_AXIS)
+    attended = merge(mine, [other_core(part) for part in send])
+    before, after = lax.optimization_barrier((before, after))
+    half = out_weight.shape[0] // 2
+    far = [
+        shifted(before[:cut], WEIGHT_AXIS, 1),
+        shifted(before[cut:half], WEIGHT_AXIS, 1),
+        shifted(after[half:], WEIGHT_AXIS, -1),
+    ]
+    blocks = [attended[None]] + [shifted(attended[None], FIRST_AXIS, shift) for shift in FIRST_SHIFTS]
+    blocks[1], far[0] = lax.optimization_barrier((blocks[1], far[0]))
+    rows = gathered(jnp.concatenate(blocks, axis=0), SECOND_AXIS)
     rows = rows.reshape(SIDE * SIDE * Q_TOK, HEADS // 2 * HEAD_DIM)
     results = [dot(rows, w) for w in (out_weight, before, after)]
-    results.append(dot(rows[:, :half], far[0]) + dot(rows[:, half:], far[1]))
+    results.append(dot(rows[:, :cut], far[0]) + dot(rows[:, cut:half], far[1]) + dot(rows[:, half:], far[2]))
     pieces = [results[0]] + [shifted(r, WEIGHT_AXIS, -shift) for r, shift in zip(results[1:], SHIFTS)]
     return assemble(pieces, [other_core(p) for p in pieces])
 

time: 53.1 us -> 51.4 us (0.968)
  starting transfers between devices: 28.7 us -> 32.5 us
  Pallas kernels: 7.07 us -> 3.35 us
  waiting for transfers between devices: 14.3 us -> 12.8 us
    pallas_call x1, Pallas kernels: 6.17 us -> 2.45 us  [attend(): pl.pallas_call(attend_kernel, out_shape=(shape, shape), in_specs=[pl.Bloc...]
    ppermute x13 -> x14, starting transfers between devices: 19 us -> 22.6 us  [shifted(): return lax.ppermute(x, ('group', 'kv'), moves)]
    ppermute x13 -> x14, waiting for transfers between devices: 13.4 us -> 10.9 us  [shifted(): return lax.ppermute(x, ('group', 'kv'), moves)]
    ppermute x5 -> x7, waiting for transfers between devices: 0.9 us -> 1.92 us  [other_core(): return lax.ppermute(x, 'kv', [(0, 1), (1, 0)])]
    ppermute x5 -> x7, starting transfers between devices: 9.65 us -> 9.91 us  [other_core(): return lax.ppermute(x, 'kv', [(0, 1), (1, 0)])]
    dot_general x5 -> x6, matrix products: 1.88 us -> 2.01 us  [dot(): return jnp.dot(a, b, preferred_element_type=jnp.float32)]
  transfers between devices with their start and end apart: 18 -> 21, of which waited for: 6 -> 8; matrix products, arithmetic and copies ran while one was open for 4% -> 4% of each run, Pallas kernels for 12% -> 5%
where the time goes in v4:
time: 51.4 us; the launch traced here: 51.8 us
  starting transfers between devices  32.5 us (63%)
  waiting for transfers between devices  12.8 us (25%)
  Pallas kernels  3.35 us (7%)
  matrix products  2.01 us (4%)
  between operations  0.82 us (2%)
    ppermute x14, starting transfers between devices, shifted(): return lax.ppermute(x, ('group', 'kv'), moves)  22.6 us
    ppermute x14, waiting for transfers between devices, shifted(): return lax.ppermute(x, ('group', 'kv'), moves)  10.9 us
    ppermute x7, starting transfers between devices, other_core(): return lax.ppermute(x, 'kv', [(0, 1), (1, 0)])  9.91 us
    pallas_call x1, Pallas kernels, attend(): pl.pallas_call(attend_kernel, out_shape=(shape, shape), in_specs=[pl.Bloc...  2.45 us
    dot_general x6, matrix products, dot(): return jnp.dot(a, b, preferred_element_type=jnp.float32)  2.01 us
    ppermute x7, waiting for transfers between devices, other_core(): return lax.ppermute(x, 'kv', [(0, 1), (1, 0)])  1.92 us
  transfers between devices with their start and end apart: 21, of which 8 were waited for; matrix products, arithmetic and copies ran while one was open for 4% of the time, Pallas kernels for 5%

profile of v4, /device:TPU:1, one launch (start us, length us, event | category | flops | bytes accessed | tf_op | source)
XLA Modules:
  0.0 51.8 jit_solution(4131072314676665644)
XLA Ops:
  0.0 2.1 %collective-permute-start.4 = (bf16[4096,128]{1,0:T(8,128)(2,1)}, bf16[4096,128]{1,0:T(8,128)(2,1)S(1)}, u32[]{:S(2)}, u32[]{:S(2)}) collective-permute-start(bf16[4096,128]{1,0:T(8,128)(2,1)} %param.18), channel_id=1, source_target_pairs={{0,2},{1,9},{2,4},{3,11},{4,6},{5,13},{6,0},{7,15},{8,10},{9,17},{... | collective-permute-start | bytes 3145736 | tf_op jit(solution)/shard_map/ppermute | solution.py:316
  2.1 1.4 %collective-permute-start.5 = (bf16[4096,128]{1,0:T(8,128)(2,1)}, bf16[4096,128]{1,0:T(8,128)(2,1)S(1)}, u32[]{:S(2)}, u32[]{:S(2)}) collective-permute-start(bf16[4096,128]{1,0:T(8,128)(2,1)} %param.18), channel_id=1, source_target_pairs={{0,6},{1,25},{2,0},{3,27},{4,2},{5,29},{6,4},{7,31},{8,14},{9,1},{... | collective-permute-start | bytes 3145736 | tf_op jit(solution)/shard_map/ppermute | solution.py:316
  4.2 2.4 %attend.1 = (f32[3,8,4096]{2,1,0:T(8,128)S(1)}, f32[3,8,4096]{2,1,0:T(8,128)S(1)}) custom-call(s32[1]{0:T(128)S(6)} %copy.17.length_ref, bf16[160,4096]{1,0:T(8,128)(2,1)} %bitcast.66, bf16[4096,1024]{1,0:T(8,128)(2,1)} %bitcast.65, f32[2,2,64,4096]{3,2,1,0:T(8,128)} %constant.7.clone.table_hbm, bf16[8,16]{1,0:T(8,128)(2,1)} %bitcast.70, ...), custom_call_target="tpu_custom_call" | custom-call | flops 3489660928 | bytes 12582912 | tf_op jit(solution)/shard_map/attend/pallas_call | solution.py:248
  6.7 4.4 %collective-permute-start.2 = (f32[8,4096]{1,0:T(8,128)S(1)}, f32[8,4096]{1,0:T(8,128)S(1)}, u32[]{:S(2)}, u32[]{:S(2)}) collective-permute-start(f32[8,4096]{1,0:T(8,128)S(1)} %get-tuple-element.20), channel_id=1, source_target_pairs={{0,1},{1,0},{2,3},{3,2},{4,5},{5,4},{6,7},{7,6},{8,9},{9,8},{10,11... | collective-permute-start | bytes 393224 | tf_op jit(solution)/shard_map/ppermute | solution.py:293
  11.6 0.5 collective-permute-done.2
  12.7 7.0 %collective-permute-start.3 = (bf16[1,8,4096]{2,1,0:T(8,128)(2,1)S(1)}, bf16[1,8,4096]{2,1,0:T(8,128)(2,1)S(1)}, u32[]{:S(2)}, u32[]{:S(2)}) collective-permute-start(bf16[1,8,4096]{2,1,0:T(8,128)(2,1)S(1)} %get-tuple-element.18), channel_id=1, source_target_pairs={{0,16},{1,65},{2,18},{3,67},{4,20},{5,69},{6,22},{7,71},{8,24},{9,... | collective-permute-start | bytes 196616 | tf_op jit(solution)/shard_map/ppermute | solution.py:316
  19.7 1.4 %collective-permute-start.6 = (bf16[256,128]{1,0:T(8,128)(2,1)S(1)}, bf16[256,128]{1,0:T(8,128)(2,1)S(1)}, u32[]{:S(2)}, u32[]{:S(2)}) collective-permute-start(bf16[256,128]{1,0:T(8,128)(2,1)S(1)} %slice.31), channel_id=1, source_target_pairs={{0,2},{1,9},{2,4},{3,11},{4,6},{5,13},{6,0},{7,15},{8,10},{9,17},{... | collective-permute-start | bytes 196616 | tf_op jit(solution)/shard_map/ppermute | solution.py:316
  21.1 0.7 %collective-permute-start.7 = (bf16[1,8,4096]{2,1,0:T(8,128)(2,1)S(1)}, bf16[1,8,4096]{2,1,0:T(8,128)(2,1)S(1)}, u32[]{:S(2)}, u32[]{:S(2)}) collective-permute-start(bf16[1,8,4096]{2,1,0:T(8,128)(2,1)S(1)} %get-tuple-element.18), channel_id=1, source_target_pairs={{0,8},{1,33},{2,10},{3,35},{4,12},{5,37},{6,14},{7,39},{8,16},{9,4... | collective-permute-start | bytes 196616 | tf_op jit(solution)/shard_map/ppermute | solution.py:316
  21.8 1.9 %collective-permute-start.8 = (bf16[1,8,4096]{2,1,0:T(8,128)(2,1)S(1)}, bf16[1,8,4096]{2,1,0:T(8,128)(2,1)S(1)}, u32[]{:S(2)}, u32[]{:S(2)}) collective-permute-start(bf16[1,8,4096]{2,1,0:T(8,128)(2,1)S(1)} %get-tuple-element.18), channel_id=1, source_target_pairs={{0,24},{1,97},{2,26},{3,99},{4,28},{5,101},{6,30},{7,103},{8,0},{9... | collective-permute-start | bytes 196616 | tf_op jit(solution)/shard_map/ppermute | solution.py:316
  23.8 1.6 %collective-permute-start.15 = (bf16[2048,128]{1,0:T(8,128)(2,1)S(1)}, bf16[2048,128]{1,0:T(8,128)(2,1)S(1)}, u32[]{:S(2)}, u32[]{:S(2)}) collective-permute-start(bf16[2048,128]{1,0:T(8,128)(2,1)S(1)} %slice.36), channel_id=1, source_target_pairs={{0,6},{1,25},{2,0},{3,27},{4,2},{5,29},{6,4},{7,31},{8,14},{9,1},{... | collective-permute-start | bytes 1572872 | tf_op jit(solution)/shard_map/ppermute | solution.py:316
  25.8 2.4 %collective-permute-start.10 = (bf16[4,8,4096]{2,1,0:T(8,128)(2,1)S(1)}, bf16[4,8,4096]{2,1,0:T(8,128)(2,1)S(1)}, u32[]{:S(2)}, u32[]{:S(2)}) collective-permute-start(bf16[4,8,4096]{2,1,0:T(8,128)(2,1)S(1)} %pad_maximum_fusion), channel_id=1, source_target_pairs={{0,96},{1,7},{2,98},{3,1},{4,100},{5,3},{6,102},{7,5},{8,104},{9,1... | collective-permute-start | bytes 786440 | tf_op jit(solution)/shard_map/ppermute | solution.py:316
  28.2 0.6 %collective-permute-start.11 = (bf16[4,8,4096]{2,1,0:T(8,128)(2,1)S(1)}, bf16[4,8,4096]{2,1,0:T(8,128)(2,1)S(1)}, u32[]{:S(2)}, u32[]{:S(2)}) collective-permute-start(bf16[4,8,4096]{2,1,0:T(8,128)(2,1)S(1)} %pad_maximum_fusion), channel_id=1, source_target_pairs={{0,64},{1,5},{2,66},{3,7},{4,68},{5,1},{6,70},{7,3},{8,72},{9,13},... | collective-permute-start | bytes 786440 | tf_op jit(solution)/shard_map/ppermute | solution.py:316
  28.8 5.0 %collective-permute-done.9 = bf16[4,8,4096]{2,1,0:T(8,128)(2,1)S(1)} collective-permute-done((bf16[4,8,4096]{2,1,0:T(8,128)(2,1)S(1)}, bf16[4,8,4096]{2,1,0:T(8,128)(2,1)S(1)}, u32[]{:S(2)}, u32[]{:S(2)}) %collective-permute-start.9) | collective-permute-done | bytes 262176 | tf_op jit(solution)/shard_map/ppermute | solution.py:316
  33.9 3.2 %collective-permute-done.10 = bf16[4,8,4096]{2,1,0:T(8,128)(2,1)S(1)} collective-permute-done((bf16[4,8,4096]{2,1,0:T(8,128)(2,1)S(1)}, bf16[4,8,4096]{2,1,0:T(8,128)(2,1)S(1)}, u32[]{:S(2)}, u32[]{:S(2)}) %collective-permute-start.10) | collective-permute-done | bytes 262176 | tf_op jit(solution)/shard_map/ppermute | solution.py:316
  37.1 2.5 %collective-permute-done.11 = bf16[4,8,4096]{2,1,0:T(8,128)(2,1)S(1)} collective-permute-done((bf16[4,8,4096]{2,1,0:T(8,128)(2,1)S(1)}, bf16[4,8,4096]{2,1,0:T(8,128)(2,1)S(1)}, u32[]{:S(2)}, u32[]{:S(2)}) %collective-permute-start.11) | collective-permute-done | bytes 262176 | tf_op jit(solution)/shard_map/ppermute | solution.py:316
  39.6 0.4 fusion.17
  40.1 1.5 %collective-permute-start.12 = (f32[128,128]{1,0:T(8,128)S(1)}, f32[128,128]{1,0:T(8,128)S(1)}, u32[]{:S(2)}, u32[]{:S(2)}) collective-permute-start(f32[128,128]{1,0:T(8,128)S(1)} %fusion.17), channel_id=1, source_target_pairs={{0,6},{1,25},{2,0},{3,27},{4,2},{5,29},{6,4},{7,31},{8,14},{9,1},{... | collective-permute-start | bytes 196616 | tf_op jit(solution)/shard_map/ppermute | solution.py:316
  41.6 0.4 fusion.15
  42.9 1.6 %collective-permute-start.16 = (f32[128,128]{1,0:T(8,128)S(1)}, f32[128,128]{1,0:T(8,128)S(1)}, u32[]{:S(2)}, u32[]{:S(2)}) collective-permute-start(f32[128,128]{1,0:T(8,128)S(1)} %fusion), channel_id=1, source_target_pairs={{0,4},{1,17},{2,6},{3,19},{4,0},{5,21},{6,2},{7,23},{8,12},{9,25},... | collective-permute-start | bytes 196616 | tf_op jit(solution)/shard_map/ppermute | solution.py:316
  44.9 1.4 %collective-permute-start.17 = (f32[128,128]{1,0:T(8,128)S(1)}, f32[128,128]{1,0:T(8,128)S(1)}, u32[]{:S(2)}, u32[]{:S(2)}) collective-permute-start(f32[128,128]{1,0:T(8,128)S(1)} %fusion.19.refs_0_), channel_id=1, source_target_pairs={{0,1},{1,0},{2,3},{3,2},{4,5},{5,4},{6,7},{7,6},{8,9},{9,8},{10,11... | collective-permute-start | bytes 196616 | tf_op jit(solution)/shard_map/ppermute | solution.py:293
  46.4 2.4 %collective-permute-start.19 = (f32[128,128]{1,0:T(8,128)S(1)}, f32[128,128]{1,0:T(8,128)S(1)}, u32[]{:S(2)}, u32[]{:S(2)}) collective-permute-start(f32[128,128]{1,0:T(8,128)S(1)} %collective-permute-done.13.refs_2_), channel_id=1, source_target_pairs={{0,1},{1,0},{2,3},{3,2},{4,5},{5,4},{6,7},{7,6},{8,9},{9,8},{10,11... | collective-permute-start | bytes 196616 | tf_op jit(solution)/shard_map/ppermute | solution.py:293
  48.9 1.1 %collective-permute-start.20 = (f32[128,128]{1,0:T(8,128)S(1)}, f32[128,128]{1,0:T(8,128)S(1)}, u32[]{:S(2)}, u32[]{:S(2)}) collective-permute-start(f32[128,128]{1,0:T(8,128)S(1)} %collective-permute-done.16.refs_3_), channel_id=1, source_target_pairs={{0,1},{1,0},{2,3},{3,2},{4,5},{5,4},{6,7},{7,6},{8,9},{9,8},{10,11... | collective-permute-start | bytes 196616 | tf_op jit(solution)/shard_map/ppermute | solution.py:293
  50.0 0.9 %collective-permute-done.20.refs_7_ = f32[128,128]{1,0:T(8,128)S(1)} collective-permute-done((f32[128,128]{1,0:T(8,128)S(1)}, f32[128,128]{1,0:T(8,128)S(1)}, u32[]{:S(2)}, u32[]{:S(2)}) %collective-permute-start.20) | collective-permute-done | bytes 65568 | tf_op jit(solution)/shard_map/ppermute | solution.py:293
  50.9 0.9 %assemble.1 = f32[256,128]{1,0:T(8,128)} custom-call(f32[128,128]{1,0:T(8,128)S(1)} %fusion.19.refs_0_, f32[128,128]{1,0:T(8,128)S(1)} %collective-permute-done.12.refs_1_, f32[128,128]{1,0:T(8,128)S(1)} %collective-permute-done.13.refs_2_, f32[128,128]{1,0:T(8,128)S(1)} %collective-permute-done.16.refs_3_, f32[128,128]{1,0:T(8,128)S(1)} %collective-permute-done.17.refs_4_, ...), custom_call_target="tpu_custom_call" | custom-call | tf_op jit(solution)/shard_map/assemble/pallas_call | solution.py:355
  (40 shorter events, 3.1 us)
Async XLA Ops:
  0.0 19.7 %collective-permute-start.4 = (bf16[4096,128]{1,0:T(8,128)(2,1)}, bf16[4096,128]{1,0:T(8,128)(2,1)S(1)}, u32[]{:S(2)}, u32[]{:S(2)}) collective-permute-start(bf16[4096,128]{1,0:T(8,128)(2,1)} %param.18), channel_id=1, source_target_pairs={{0,2},{1,9},{2,4},{3,11},{4,6},{5,13},{6,0},{7,15},{8,10},{9,17},{... | collective-permute-start | bytes 3145736 | tf_op jit(solution)/shard_map/ppermute | solution.py:316
  2.1 17.6 %collective-permute-start.5 = (bf16[4096,128]{1,0:T(8,128)(2,1)}, bf16[4096,128]{1,0:T(8,128)(2,1)S(1)}, u32[]{:S(2)}, u32[]{:S(2)}) collective-permute-start(bf16[4096,128]{1,0:T(8,128)(2,1)} %param.18), channel_id=1, source_target_pairs={{0,6},{1,25},{2,0},{3,27},{4,2},{5,29},{6,4},{7,31},{8,14},{9,1},{... | collective-permute-start | bytes 3145736 | tf_op jit(solution)/shard_map/ppermute | solution.py:316
  6.7 5.4 %collective-permute-start.2 = (f32[8,4096]{1,0:T(8,128)S(1)}, f32[8,4096]{1,0:T(8,128)S(1)}, u32[]{:S(2)}, u32[]{:S(2)}) collective-permute-start(f32[8,4096]{1,0:T(8,128)S(1)} %get-tuple-element.20), channel_id=1, source_target_pairs={{0,1},{1,0},{2,3},{3,2},{4,5},{5,4},{6,7},{7,6},{8,9},{9,8},{10,11... | collective-permute-start | bytes 393224 | tf_op jit(solution)/shard_map/ppermute | solution.py:293
  11.1 1.3 %collective-permute-start.1 = (f32[8,4096]{1,0:T(8,128)S(1)}, f32[8,4096]{1,0:T(8,128)S(1)}, u32[]{:S(2)}, u32[]{:S(2)}) collective-permute-start(f32[8,4096]{1,0:T(8,128)S(1)} %get-tuple-element.21), channel_id=1, source_target_pairs={{0,1},{1,0},{2,3},{3,2},{4,5},{5,4},{6,7},{7,6},{8,9},{9,8},{10,11... | collective-permute-start | bytes 393224 | tf_op jit(solution)/shard_map/ppermute | solution.py:293
  11.2 1.4 %collective-permute-start = (f32[8,4096]{1,0:T(8,128)S(1)}, f32[8,4096]{1,0:T(8,128)S(1)}, u32[]{:S(2)}, u32[]{:S(2)}) collective-permute-start(f32[8,4096]{1,0:T(8,128)S(1)} %get-tuple-element.19), channel_id=1, source_target_pairs={{0,1},{1,0},{2,3},{3,2},{4,5},{5,4},{6,7},{7,6},{8,9},{9,8},{10,11... | collective-permute-start | bytes 393224 | tf_op jit(solution)/shard_map/ppermute | solution.py:293
  12.7 12.7 %collective-permute-start.3 = (bf16[1,8,4096]{2,1,0:T(8,128)(2,1)S(1)}, bf16[1,8,4096]{2,1,0:T(8,128)(2,1)S(1)}, u32[]{:S(2)}, u32[]{:S(2)}) collective-permute-start(bf16[1,8,4096]{2,1,0:T(8,128)(2,1)S(1)} %get-tuple-element.18), channel_id=1, source_target_pairs={{0,16},{1,65},{2,18},{3,67},{4,20},{5,69},{6,22},{7,71},{8,24},{9,... | collective-permute-start | bytes 196616 | tf_op jit(solution)/shard_map/ppermute | solution.py:316
  19.7 5.7 %collective-permute-start.6 = (bf16[256,128]{1,0:T(8,128)(2,1)S(1)}, bf16[256,128]{1,0:T(8,128)(2,1)S(1)}, u32[]{:S(2)}, u32[]{:S(2)}) collective-permute-start(bf16[256,128]{1,0:T(8,128)(2,1)S(1)} %slice.31), channel_id=1, source_target_pairs={{0,2},{1,9},{2,4},{3,11},{4,6},{5,13},{6,0},{7,15},{8,10},{9,17},{... | collective-permute-start | bytes 196616 | tf_op jit(solution)/shard_map/ppermute | solution.py:316
  21.1 4.4 %collective-permute-start.7 = (bf16[1,8,4096]{2,1,0:T(8,128)(2,1)S(1)}, bf16[1,8,4096]{2,1,0:T(8,128)(2,1)S(1)}, u32[]{:S(2)}, u32[]{:S(2)}) collective-permute-start(bf16[1,8,4096]{2,1,0:T(8,128)(2,1)S(1)} %get-tuple-element.18), channel_id=1, source_target_pairs={{0,8},{1,33},{2,10},{3,35},{4,12},{5,37},{6,14},{7,39},{8,16},{9,4... | collective-permute-start | bytes 196616 | tf_op jit(solution)/shard_map/ppermute | solution.py:316
  21.8 3.6 %collective-permute-start.8 = (bf16[1,8,4096]{2,1,0:T(8,128)(2,1)S(1)}, bf16[1,8,4096]{2,1,0:T(8,128)(2,1)S(1)}, u32[]{:S(2)}, u32[]{:S(2)}) collective-permute-start(bf16[1,8,4096]{2,1,0:T(8,128)(2,1)S(1)} %get-tuple-element.18), channel_id=1, source_target_pairs={{0,24},{1,97},{2,26},{3,99},{4,28},{5,101},{6,30},{7,103},{8,0},{9... | collective-permute-start | bytes 196616 | tf_op jit(solution)/shard_map/ppermute | solution.py:316
  23.8 18.6 %collective-permute-start.15 = (bf16[2048,128]{1,0:T(8,128)(2,1)S(1)}, bf16[2048,128]{1,0:T(8,128)(2,1)S(1)}, u32[]{:S(2)}, u32[]{:S(2)}) collective-permute-start(bf16[2048,128]{1,0:T(8,128)(2,1)S(1)} %slice.36), channel_id=1, source_target_pairs={{0,6},{1,25},{2,0},{3,27},{4,2},{5,29},{6,4},{7,31},{8,14},{9,1},{... | collective-permute-start | bytes 1572872 | tf_op jit(solution)/shard_map/ppermute | solution.py:316
  25.4 16.7 %collective-permute-start.14 = (bf16[1792,128]{1,0:T(8,128)(2,1)S(1)}, bf16[1792,128]{1,0:T(8,128)(2,1)S(1)}, u32[]{:S(2)}, u32[]{:S(2)}) collective-permute-start(bf16[1792,128]{1,0:T(8,128)(2,1)S(1)} %slice.34), channel_id=1, source_target_pairs={{0,2},{1,9},{2,4},{3,11},{4,6},{5,13},{6,0},{7,15},{8,10},{9,17},{... | collective-permute-start | bytes 1376264 | tf_op jit(solution)/shard_map/ppermute | solution.py:316
  25.5 8.3 %collective-permute-start.9 = (bf16[4,8,4096]{2,1,0:T(8,128)(2,1)S(1)}, bf16[4,8,4096]{2,1,0:T(8,128)(2,1)S(1)}, u32[]{:S(2)}, u32[]{:S(2)}) collective-permute-start(bf16[4,8,4096]{2,1,0:T(8,128)(2,1)S(1)} %pad_maximum_fusion), channel_id=1, source_target_pairs={{0,32},{1,3},{2,34},{3,5},{4,36},{5,7},{6,38},{7,1},{8,40},{9,11},... | collective-permute-start | bytes 786440 | tf_op jit(solution)/shard_map/ppermute | solution.py:316
  25.8 11.3 %collective-permute-start.10 = (bf16[4,8,4096]{2,1,0:T(8,128)(2,1)S(1)}, bf16[4,8,4096]{2,1,0:T(8,128)(2,1)S(1)}, u32[]{:S(2)}, u32[]{:S(2)}) collective-permute-start(bf16[4,8,4096]{2,1,0:T(8,128)(2,1)S(1)} %pad_maximum_fusion), channel_id=1, source_target_pairs={{0,96},{1,7},{2,98},{3,1},{4,100},{5,3},{6,102},{7,5},{8,104},{9,1... | collective-permute-start | bytes 786440 | tf_op jit(solution)/shard_map/ppermute | solution.py:316
  28.2 11.4 %collective-permute-start.11 = (bf16[4,8,4096]{2,1,0:T(8,128)(2,1)S(1)}, bf16[4,8,4096]{2,1,0:T(8,128)(2,1)S(1)}, u32[]{:S(2)}, u32[]{:S(2)}) collective-permute-start(bf16[4,8,4096]{2,1,0:T(8,128)(2,1)S(1)} %pad_maximum_fusion), channel_id=1, source_target_pairs={{0,64},{1,5},{2,66},{3,7},{4,68},{5,1},{6,70},{7,3},{8,72},{9,13},... | collective-permute-start | bytes 786440 | tf_op jit(solution)/shard_map/ppermute | solution.py:316
  28.8 15.6 %copy-start = (bf16[4096,128]{1,0:T(8,128)(2,1)S(1)}, bf16[4096,128]{1,0:T(8,128)(2,1)}, u32[]{:S(2)}) copy-start(bf16[4096,128]{1,0:T(8,128)(2,1)} %param.18) | copy-start | bytes 3145732
  40.1 6.1 %collective-permute-start.12 = (f32[128,128]{1,0:T(8,128)S(1)}, f32[128,128]{1,0:T(8,128)S(1)}, u32[]{:S(2)}, u32[]{:S(2)}) collective-permute-start(f32[128,128]{1,0:T(8,128)S(1)} %fusion.17), channel_id=1, source_target_pairs={{0,6},{1,25},{2,0},{3,27},{4,2},{5,29},{6,4},{7,31},{8,14},{9,1},{... | collective-permute-start | bytes 196616 | tf_op jit(solution)/shard_map/ppermute | solution.py:316
  42.0 4.4 %collective-permute-start.13 = (f32[128,128]{1,0:T(8,128)S(1)}, f32[128,128]{1,0:T(8,128)S(1)}, u32[]{:S(2)}, u32[]{:S(2)}) collective-permute-start(f32[128,128]{1,0:T(8,128)S(1)} %fusion.15), channel_id=1, source_target_pairs={{0,2},{1,9},{2,4},{3,11},{4,6},{5,13},{6,0},{7,15},{8,10},{9,17},{... | collective-permute-start | bytes 196616 | tf_op jit(solution)/shard_map/ppermute | solution.py:316
  42.9 6.0 %collective-permute-start.16 = (f32[128,128]{1,0:T(8,128)S(1)}, f32[128,128]{1,0:T(8,128)S(1)}, u32[]{:S(2)}, u32[]{:S(2)}) collective-permute-start(f32[128,128]{1,0:T(8,128)S(1)} %fusion), channel_id=1, source_target_pairs={{0,4},{1,17},{2,6},{3,19},{4,0},{5,21},{6,2},{7,23},{8,12},{9,25},... | collective-permute-start | bytes 196616 | tf_op jit(solution)/shard_map/ppermute | solution.py:316
  44.9 5.1 %collective-permute-start.17 = (f32[128,128]{1,0:T(8,128)S(1)}, f32[128,128]{1,0:T(8,128)S(1)}, u32[]{:S(2)}, u32[]{:S(2)}) collective-permute-start(f32[128,128]{1,0:T(8,128)S(1)} %fusion.19.refs_0_), channel_id=1, source_target_pairs={{0,1},{1,0},{2,3},{3,2},{4,5},{5,4},{6,7},{7,6},{8,9},{9,8},{10,11... | collective-permute-start | bytes 196616 | tf_op jit(solution)/shard_map/ppermute | solution.py:293
  46.2 3.8 %collective-permute-start.18 = (f32[128,128]{1,0:T(8,128)S(1)}, f32[128,128]{1,0:T(8,128)S(1)}, u32[]{:S(2)}, u32[]{:S(2)}) collective-permute-start(f32[128,128]{1,0:T(8,128)S(1)} %collective-permute-done.12.refs_1_), channel_id=1, source_target_pairs={{0,1},{1,0},{2,3},{3,2},{4,5},{5,4},{6,7},{7,6},{8,9},{9,8},{10,11... | collective-permute-start | bytes 196616 | tf_op jit(solution)/shard_map/ppermute | solution.py:293
  46.4 3.6 %collective-permute-start.19 = (f32[128,128]{1,0:T(8,128)S(1)}, f32[128,128]{1,0:T(8,128)S(1)}, u32[]{:S(2)}, u32[]{:S(2)}) collective-permute-start(f32[128,128]{1,0:T(8,128)S(1)} %collective-permute-done.13.refs_2_), channel_id=1, source_target_pairs={{0,1},{1,0},{2,3},{3,2},{4,5},{5,4},{6,7},{7,6},{8,9},{9,8},{10,11... | collective-permute-start | bytes 196616 | tf_op jit(solution)/shard_map/ppermute | solution.py:293
  48.9 2.0 %collective-permute-start.20 = (f32[128,128]{1,0:T(8,128)S(1)}, f32[128,128]{1,0:T(8,128)S(1)}, u32[]{:S(2)}, u32[]{:S(2)}) collective-permute-start(f32[128,128]{1,0:T(8,128)S(1)} %collective-permute-done.16.refs_3_), channel_id=1, source_target_pairs={{0,1},{1,0},{2,3},{3,2},{4,5},{5,4},{6,7},{7,6},{8,9},{9,8},{10,11... | collective-permute-start | bytes 196616 | tf_op jit(solution)/shard_map/ppermute | solution.py:293

commit v5 on v4

--- a/solution.py
+++ b/solution.py
@@ -299,7 +299,7 @@
 FIRST_AXIS = ("y", "z")
 SECOND_AXIS = ("z", "x")
 SHIFTS = (1, -1, 2)
-FIRST_SHIFTS = (2, 1, -1)
+FIRST_SHIFTS = SECOND_SHIFTS = OUT_SHIFTS = (2, 1, -1)
 
 
 def coordinate(chip, axis):
@@ -323,7 +323,6 @@
 def assemble_kernel(*refs):
     *pieces, out_ref, whole = refs
     chip, core = lax.axis_index("group"), lax.axis_index("kv")
-    steps = (0,) + SHIFTS
 
     def place(axes, at_core, shift):
         value = jnp.int32(0)
@@ -332,9 +331,9 @@
             value = jnp.where(at_core == c, at, value)
         return value
 
-    for at_core, refs in ((core, pieces[: len(steps)]), (1 - core, pieces[len(steps) :])):
-        for ref, d in zip(refs, steps):
-            for i, e in enumerate(steps):
+    for at_core, refs in ((core, pieces[:SIDE]), (1 - core, pieces[SIDE:])):
+        for ref, d in zip(refs, (0,) + OUT_SHIFTS):
+            for i, e in enumerate((0,) + SECOND_SHIFTS):
                 for j, f in enumerate((0,) + FIRST_SHIFTS):
                     request = (
                         place(WEIGHT_AXIS, at_core, d)
@@ -379,11 +378,13 @@
     ]
     blocks = [attended[None]] + [shifted(attended[None], FIRST_AXIS, shift) for shift in FIRST_SHIFTS]
     blocks[1], far[0] = lax.optimization_barrier((blocks[1], far[0]))
-    rows = gathered(jnp.concatenate(blocks, axis=0), SECOND_AXIS)
+    near = jnp.concatenate(blocks, axis=0)
+    rows = jnp.concatenate([near] + [shifted(near, SECOND_AXIS, shift) for shift in SECOND_SHIFTS], axis=0)
     rows = rows.reshape(SIDE * SIDE * Q_TOK, HEADS // 2 * HEAD_DIM)
-    results = [dot(rows, w) for w in (out_weight, before, after)]
-    results.append(dot(rows[:, :cut], far[0]) + dot(rows[:, cut:half], far[1]) + dot(rows[:, half:], far[2]))
-    pieces = [results[0]] + [shifted(r, WEIGHT_AXIS, -shift) for r, shift in zip(results[1:], SHIFTS)]
+    distant = dot(rows[:, :cut], far[0]) + dot(rows[:, cut:half], far[1]) + dot(rows[:, half:], far[2])
+    distant = shifted(distant, WEIGHT_AXIS, -2)
+    pieces = [shifted(dot(rows, w), WEIGHT_AXIS, -shift) for w, shift in zip((before, after), SHIFTS)]
+    pieces = [dot(rows, out_weight), distant, *pieces]
     return assemble(pieces, [other_core(p) for p in pieces])
 
 

time: 51.4 us -> 51.3 us (level)
  Pallas kernels: 3.35 us -> 6.57 us
  starting transfers between devices: 32.5 us -> 30.2 us
  waiting for transfers between devices: 12.8 us -> 11.3 us
    pallas_call x1, Pallas kernels: 2.45 us -> 5.67 us  [attend(): pl.pallas_call(attend_kernel, out_shape=(shape, shape), in_specs=[pl.Bloc...]
    ppermute x14, waiting for transfers between devices: 10.9 us -> 9.34 us  [shifted(): return lax.ppermute(x, ('group', 'kv'), moves)]
    ppermute x14, starting transfers between devices: 22.6 us -> 21.3 us  [shifted(): return lax.ppermute(x, ('group', 'kv'), moves)]
    ppermute x7, starting transfers between devices: 9.91 us -> 8.96 us  [other_core(): return lax.ppermute(x, 'kv', [(0, 1), (1, 0)])]
  transfers between devices with their start and end apart: 21 -> 21, of which waited for: 8 -> 7; matrix products, arithmetic and copies ran while one was open for 4% -> 5% of each run, Pallas kernels for 5% -> 11%
where the time goes in v5:
time: 51.3 us; the launch traced here: 51.2 us
  starting transfers between devices  30.2 us (59%)
  waiting for transfers between devices  11.3 us (22%)
  Pallas kernels  6.57 us (13%)
  matrix products  2.01 us (4%)
  between operations  0.84 us (2%)
    ppermute x14, starting transfers between devices, shifted(): return lax.ppermute(x, ('group', 'kv'), moves)  21.3 us
    ppermute x14, waiting for transfers between devices, shifted(): return lax.ppermute(x, ('group', 'kv'), moves)  9.34 us
    ppermute x7, starting transfers between devices, other_core(): return lax.ppermute(x, 'kv', [(0, 1), (1, 0)])  8.96 us
    pallas_call x1, Pallas kernels, attend(): pl.pallas_call(attend_kernel, out_shape=(shape, shape), in_specs=[pl.Bloc...  5.67 us
    dot_general x6, matrix products, dot(): return jnp.dot(a, b, preferred_element_type=jnp.float32)  2.01 us
    ppermute x7, waiting for transfers between devices, other_core(): return lax.ppermute(x, 'kv', [(0, 1), (1, 0)])  1.92 us
  transfers between devices with their start and end apart: 21, of which 7 were waited for; matrix products, arithmetic and copies ran while one was open for 5% of the time, Pallas kernels for 11%

profile of v5, /device:TPU:1, one launch (start us, length us, event | category | flops | bytes accessed | tf_op | source)
XLA Modules:
  0.0 51.2 jit_solution(9348904529843073221)
XLA Ops:
  0.0 2.1 %collective-permute-start.4 = (bf16[4096,128]{1,0:T(8,128)(2,1)}, bf16[4096,128]{1,0:T(8,128)(2,1)S(1)}, u32[]{:S(2)}, u32[]{:S(2)}) collective-permute-start(bf16[4096,128]{1,0:T(8,128)(2,1)} %param.18), channel_id=1, source_target_pairs={{0,2},{1,9},{2,4},{3,11},{4,6},{5,13},{6,0},{7,15},{8,10},{9,17},{... | collective-permute-start | bytes 3145736 | tf_op jit(solution)/shard_map/ppermute | solution.py:316
  2.1 1.4 %collective-permute-start.5 = (bf16[4096,128]{1,0:T(8,128)(2,1)}, bf16[4096,128]{1,0:T(8,128)(2,1)S(1)}, u32[]{:S(2)}, u32[]{:S(2)}) collective-permute-start(bf16[4096,128]{1,0:T(8,128)(2,1)} %param.18), channel_id=1, source_target_pairs={{0,6},{1,25},{2,0},{3,27},{4,2},{5,29},{6,4},{7,31},{8,14},{9,1},{... | collective-permute-start | bytes 3145736 | tf_op jit(solution)/shard_map/ppermute | solution.py:316
  4.2 5.7 %attend.1 = (f32[3,8,4096]{2,1,0:T(8,128)S(1)}, f32[3,8,4096]{2,1,0:T(8,128)S(1)}) custom-call(s32[1]{0:T(128)S(6)} %copy.17.length_ref, bf16[160,4096]{1,0:T(8,128)(2,1)} %bitcast.66, bf16[4096,1024]{1,0:T(8,128)(2,1)} %bitcast.65, f32[2,2,64,4096]{3,2,1,0:T(8,128)} %constant.7.clone.table_hbm, bf16[8,16]{1,0:T(8,128)(2,1)} %bitcast.70, ...), custom_call_target="tpu_custom_call" | custom-call | flops 3489660928 | bytes 12582912 | tf_op jit(solution)/shard_map/attend/pallas_call | solution.py:248
  9.9 4.4 %collective-permute-start.2 = (f32[8,4096]{1,0:T(8,128)S(1)}, f32[8,4096]{1,0:T(8,128)S(1)}, u32[]{:S(2)}, u32[]{:S(2)}) collective-permute-start(f32[8,4096]{1,0:T(8,128)S(1)} %get-tuple-element.20), channel_id=1, source_target_pairs={{0,1},{1,0},{2,3},{3,2},{4,5},{5,4},{6,7},{7,6},{8,9},{9,8},{10,11... | collective-permute-start | bytes 393224 | tf_op jit(solution)/shard_map/ppermute | solution.py:293
  14.8 0.5 collective-permute-done.2
  15.9 3.8 %collective-permute-start.3 = (bf16[1,8,4096]{2,1,0:T(8,128)(2,1)S(1)}, bf16[1,8,4096]{2,1,0:T(8,128)(2,1)S(1)}, u32[]{:S(2)}, u32[]{:S(2)}) collective-permute-start(bf16[1,8,4096]{2,1,0:T(8,128)(2,1)S(1)} %get-tuple-element.18), channel_id=1, source_target_pairs={{0,16},{1,65},{2,18},{3,67},{4,20},{5,69},{6,22},{7,71},{8,24},{9,... | collective-permute-start | bytes 196616 | tf_op jit(solution)/shard_map/ppermute | solution.py:316
  19.7 1.4 %collective-permute-start.6 = (bf16[256,128]{1,0:T(8,128)(2,1)S(1)}, bf16[256,128]{1,0:T(8,128)(2,1)S(1)}, u32[]{:S(2)}, u32[]{:S(2)}) collective-permute-start(bf16[256,128]{1,0:T(8,128)(2,1)S(1)} %slice.31), channel_id=1, source_target_pairs={{0,2},{1,9},{2,4},{3,11},{4,6},{5,13},{6,0},{7,15},{8,10},{9,17},{... | collective-permute-start | bytes 196616 | tf_op jit(solution)/shard_map/ppermute | solution.py:316
  21.1 0.7 %collective-permute-start.7 = (bf16[1,8,4096]{2,1,0:T(8,128)(2,1)S(1)}, bf16[1,8,4096]{2,1,0:T(8,128)(2,1)S(1)}, u32[]{:S(2)}, u32[]{:S(2)}) collective-permute-start(bf16[1,8,4096]{2,1,0:T(8,128)(2,1)S(1)} %get-tuple-element.18), channel_id=1, source_target_pairs={{0,8},{1,33},{2,10},{3,35},{4,12},{5,37},{6,14},{7,39},{8,16},{9,4... | collective-permute-start | bytes 196616 | tf_op jit(solution)/shard_map/ppermute | solution.py:316
  21.8 1.9 %collective-permute-start.8 = (bf16[1,8,4096]{2,1,0:T(8,128)(2,1)S(1)}, bf16[1,8,4096]{2,1,0:T(8,128)(2,1)S(1)}, u32[]{:S(2)}, u32[]{:S(2)}) collective-permute-start(bf16[1,8,4096]{2,1,0:T(8,128)(2,1)S(1)} %get-tuple-element.18), channel_id=1, source_target_pairs={{0,24},{1,97},{2,26},{3,99},{4,28},{5,101},{6,30},{7,103},{8,0},{9... | collective-permute-start | bytes 196616 | tf_op jit(solution)/shard_map/ppermute | solution.py:316
  23.8 1.6 %collective-permute-start.13 = (bf16[2048,128]{1,0:T(8,128)(2,1)S(1)}, bf16[2048,128]{1,0:T(8,128)(2,1)S(1)}, u32[]{:S(2)}, u32[]{:S(2)}) collective-permute-start(bf16[2048,128]{1,0:T(8,128)(2,1)S(1)} %slice.36), channel_id=1, source_target_pairs={{0,6},{1,25},{2,0},{3,27},{4,2},{5,29},{6,4},{7,31},{8,14},{9,1},{... | collective-permute-start | bytes 1572872 | tf_op jit(solution)/shard_map/ppermute | solution.py:316
  25.5 1.9 %collective-permute-start.9 = (bf16[4,8,4096]{2,1,0:T(8,128)(2,1)S(1)}, bf16[4,8,4096]{2,1,0:T(8,128)(2,1)S(1)}, u32[]{:S(2)}, u32[]{:S(2)}) collective-permute-start(bf16[4,8,4096]{2,1,0:T(8,128)(2,1)S(1)} %pad_maximum_fusion), channel_id=1, source_target_pairs={{0,64},{1,5},{2,66},{3,7},{4,68},{5,1},{6,70},{7,3},{8,72},{9,13},... | collective-permute-start | bytes 786440 | tf_op jit(solution)/shard_map/ppermute | solution.py:316
  27.4 2.6 %collective-permute-start.11 = (bf16[4,8,4096]{2,1,0:T(8,128)(2,1)S(1)}, bf16[4,8,4096]{2,1,0:T(8,128)(2,1)S(1)}, u32[]{:S(2)}, u32[]{:S(2)}) collective-permute-start(bf16[4,8,4096]{2,1,0:T(8,128)(2,1)S(1)} %pad_maximum_fusion), channel_id=1, source_target_pairs={{0,96},{1,7},{2,98},{3,1},{4,100},{5,3},{6,102},{7,5},{8,104},{9,1... | collective-permute-start | bytes 786440 | tf_op jit(solution)/shard_map/ppermute | solution.py:316
  30.1 5.0 %collective-permute-done.9 = bf16[4,8,4096]{2,1,0:T(8,128)(2,1)S(1)} collective-permute-done((bf16[4,8,4096]{2,1,0:T(8,128)(2,1)S(1)}, bf16[4,8,4096]{2,1,0:T(8,128)(2,1)S(1)}, u32[]{:S(2)}, u32[]{:S(2)}) %collective-permute-start.9) | collective-permute-done | bytes 262176 | tf_op jit(solution)/shard_map/ppermute | solution.py:316
  35.1 3.9 %collective-permute-done.10 = bf16[4,8,4096]{2,1,0:T(8,128)(2,1)S(1)} collective-permute-done((bf16[4,8,4096]{2,1,0:T(8,128)(2,1)S(1)}, bf16[4,8,4096]{2,1,0:T(8,128)(2,1)S(1)}, u32[]{:S(2)}, u32[]{:S(2)}) %collective-permute-start.10) | collective-permute-done | bytes 262176 | tf_op jit(solution)/shard_map/ppermute | solution.py:316
  39.0 0.4 fusion.17
  39.4 1.9 %collective-permute-start.15 = (f32[128,128]{1,0:T(8,128)S(1)}, f32[128,128]{1,0:T(8,128)S(1)}, u32[]{:S(2)}, u32[]{:S(2)}) collective-permute-start(f32[128,128]{1,0:T(8,128)S(1)} %fusion.17), channel_id=1, source_target_pairs={{0,6},{1,25},{2,0},{3,27},{4,2},{5,29},{6,4},{7,31},{8,14},{9,1},{... | collective-permute-start | bytes 196616 | tf_op jit(solution)/shard_map/ppermute | solution.py:316
  41.4 0.4 fusion.15
  42.6 1.8 %collective-permute-start.14 = (f32[128,128]{1,0:T(8,128)S(1)}, f32[128,128]{1,0:T(8,128)S(1)}, u32[]{:S(2)}, u32[]{:S(2)}) collective-permute-start(f32[128,128]{1,0:T(8,128)S(1)} %fusion), channel_id=1, source_target_pairs={{0,4},{1,17},{2,6},{3,19},{4,0},{5,21},{6,2},{7,23},{8,12},{9,25},... | collective-permute-start | bytes 196616 | tf_op jit(solution)/shard_map/ppermute | solution.py:316
  44.8 0.8 %collective-permute-start.17 = (f32[128,128]{1,0:T(8,128)S(1)}, f32[128,128]{1,0:T(8,128)S(1)}, u32[]{:S(2)}, u32[]{:S(2)}) collective-permute-start(f32[128,128]{1,0:T(8,128)S(1)} %fusion.19.refs_0_), channel_id=1, source_target_pairs={{0,1},{1,0},{2,3},{3,2},{4,5},{5,4},{6,7},{7,6},{8,9},{9,8},{10,11... | collective-permute-start | bytes 196616 | tf_op jit(solution)/shard_map/ppermute | solution.py:293
  45.7 0.5 collective-permute-done.16.refs_3_
  46.2 2.1 %collective-permute-start.20 = (f32[128,128]{1,0:T(8,128)S(1)}, f32[128,128]{1,0:T(8,128)S(1)}, u32[]{:S(2)}, u32[]{:S(2)}) collective-permute-start(f32[128,128]{1,0:T(8,128)S(1)} %collective-permute-done.16.refs_3_), channel_id=1, source_target_pairs={{0,1},{1,0},{2,3},{3,2},{4,5},{5,4},{6,7},{7,6},{8,9},{9,8},{10,11... | collective-permute-start | bytes 196616 | tf_op jit(solution)/shard_map/ppermute | solution.py:293
  48.3 1.1 %collective-permute-start.18 = (f32[128,128]{1,0:T(8,128)S(1)}, f32[128,128]{1,0:T(8,128)S(1)}, u32[]{:S(2)}, u32[]{:S(2)}) collective-permute-start(f32[128,128]{1,0:T(8,128)S(1)} %collective-permute-done.14.refs_1_), channel_id=1, source_target_pairs={{0,1},{1,0},{2,3},{3,2},{4,5},{5,4},{6,7},{7,6},{8,9},{9,8},{10,11... | collective-permute-start | bytes 196616 | tf_op jit(solution)/shard_map/ppermute | solution.py:293
  49.4 0.9 %collective-permute-done.18.refs_5_ = f32[128,128]{1,0:T(8,128)S(1)} collective-permute-done((f32[128,128]{1,0:T(8,128)S(1)}, f32[128,128]{1,0:T(8,128)S(1)}, u32[]{:S(2)}, u32[]{:S(2)}) %collective-permute-start.18) | collective-permute-done | bytes 65568 | tf_op jit(solution)/shard_map/ppermute | solution.py:293
  50.3 0.9 %assemble.1 = f32[256,128]{1,0:T(8,128)} custom-call(f32[128,128]{1,0:T(8,128)S(1)} %fusion.19.refs_0_, f32[128,128]{1,0:T(8,128)S(1)} %collective-permute-done.14.refs_1_, f32[128,128]{1,0:T(8,128)S(1)} %collective-permute-done.15.refs_2_, f32[128,128]{1,0:T(8,128)S(1)} %collective-permute-done.16.refs_3_, f32[128,128]{1,0:T(8,128)S(1)} %collective-permute-done.17.refs_4_, ...), custom_call_target="tpu_custom_call" | custom-call | tf_op jit(solution)/shard_map/assemble/pallas_call | solution.py:354
  (40 shorter events, 2.8 us)
Async XLA Ops:
  0.0 19.7 %collective-permute-start.4 = (bf16[4096,128]{1,0:T(8,128)(2,1)}, bf16[4096,128]{1,0:T(8,128)(2,1)S(1)}, u32[]{:S(2)}, u32[]{:S(2)}) collective-permute-start(bf16[4096,128]{1,0:T(8,128)(2,1)} %param.18), channel_id=1, source_target_pairs={{0,2},{1,9},{2,4},{3,11},{4,6},{5,13},{6,0},{7,15},{8,10},{9,17},{... | collective-permute-start | bytes 3145736 | tf_op jit(solution)/shard_map/ppermute | solution.py:316
  2.1 17.6 %collective-permute-start.5 = (bf16[4096,128]{1,0:T(8,128)(2,1)}, bf16[4096,128]{1,0:T(8,128)(2,1)S(1)}, u32[]{:S(2)}, u32[]{:S(2)}) collective-permute-start(bf16[4096,128]{1,0:T(8,128)(2,1)} %param.18), channel_id=1, source_target_pairs={{0,6},{1,25},{2,0},{3,27},{4,2},{5,29},{6,4},{7,31},{8,14},{9,1},{... | collective-permute-start | bytes 3145736 | tf_op jit(solution)/shard_map/ppermute | solution.py:316
  9.9 5.3 %collective-permute-start.2 = (f32[8,4096]{1,0:T(8,128)S(1)}, f32[8,4096]{1,0:T(8,128)S(1)}, u32[]{:S(2)}, u32[]{:S(2)}) collective-permute-start(f32[8,4096]{1,0:T(8,128)S(1)} %get-tuple-element.20), channel_id=1, source_target_pairs={{0,1},{1,0},{2,3},{3,2},{4,5},{5,4},{6,7},{7,6},{8,9},{9,8},{10,11... | collective-permute-start | bytes 393224 | tf_op jit(solution)/shard_map/ppermute | solution.py:293
  14.3 1.3 %collective-permute-start.1 = (f32[8,4096]{1,0:T(8,128)S(1)}, f32[8,4096]{1,0:T(8,128)S(1)}, u32[]{:S(2)}, u32[]{:S(2)}) collective-permute-start(f32[8,4096]{1,0:T(8,128)S(1)} %get-tuple-element.21), channel_id=1, source_target_pairs={{0,1},{1,0},{2,3},{3,2},{4,5},{5,4},{6,7},{7,6},{8,9},{9,8},{10,11... | collective-permute-start | bytes 393224 | tf_op jit(solution)/shard_map/ppermute | solution.py:293
  14.4 1.4 %collective-permute-start = (f32[8,4096]{1,0:T(8,128)S(1)}, f32[8,4096]{1,0:T(8,128)S(1)}, u32[]{:S(2)}, u32[]{:S(2)}) collective-permute-start(f32[8,4096]{1,0:T(8,128)S(1)} %get-tuple-element.19), channel_id=1, source_target_pairs={{0,1},{1,0},{2,3},{3,2},{4,5},{5,4},{6,7},{7,6},{8,9},{9,8},{10,11... | collective-permute-start | bytes 393224 | tf_op jit(solution)/shard_map/ppermute | solution.py:293
  15.9 9.5 %collective-permute-start.3 = (bf16[1,8,4096]{2,1,0:T(8,128)(2,1)S(1)}, bf16[1,8,4096]{2,1,0:T(8,128)(2,1)S(1)}, u32[]{:S(2)}, u32[]{:S(2)}) collective-permute-start(bf16[1,8,4096]{2,1,0:T(8,128)(2,1)S(1)} %get-tuple-element.18), channel_id=1, source_target_pairs={{0,16},{1,65},{2,18},{3,67},{4,20},{5,69},{6,22},{7,71},{8,24},{9,... | collective-permute-start | bytes 196616 | tf_op jit(solution)/shard_map/ppermute | solution.py:316
  19.7 5.7 %collective-permute-start.6 = (bf16[256,128]{1,0:T(8,128)(2,1)S(1)}, bf16[256,128]{1,0:T(8,128)(2,1)S(1)}, u32[]{:S(2)}, u32[]{:S(2)}) collective-permute-start(bf16[256,128]{1,0:T(8,128)(2,1)S(1)} %slice.31), channel_id=1, source_target_pairs={{0,2},{1,9},{2,4},{3,11},{4,6},{5,13},{6,0},{7,15},{8,10},{9,17},{... | collective-permute-start | bytes 196616 | tf_op jit(solution)/shard_map/ppermute | solution.py:316
  21.1 4.4 %collective-permute-start.7 = (bf16[1,8,4096]{2,1,0:T(8,128)(2,1)S(1)}, bf16[1,8,4096]{2,1,0:T(8,128)(2,1)S(1)}, u32[]{:S(2)}, u32[]{:S(2)}) collective-permute-start(bf16[1,8,4096]{2,1,0:T(8,128)(2,1)S(1)} %get-tuple-element.18), channel_id=1, source_target_pairs={{0,8},{1,33},{2,10},{3,35},{4,12},{5,37},{6,14},{7,39},{8,16},{9,4... | collective-permute-start | bytes 196616 | tf_op jit(solution)/shard_map/ppermute | solution.py:316
  21.8 3.6 %collective-permute-start.8 = (bf16[1,8,4096]{2,1,0:T(8,128)(2,1)S(1)}, bf16[1,8,4096]{2,1,0:T(8,128)(2,1)S(1)}, u32[]{:S(2)}, u32[]{:S(2)}) collective-permute-start(bf16[1,8,4096]{2,1,0:T(8,128)(2,1)S(1)} %get-tuple-element.18), channel_id=1, source_target_pairs={{0,24},{1,97},{2,26},{3,99},{4,28},{5,101},{6,30},{7,103},{8,0},{9... | collective-permute-start | bytes 196616 | tf_op jit(solution)/shard_map/ppermute | solution.py:316
  23.8 18.4 %collective-permute-start.13 = (bf16[2048,128]{1,0:T(8,128)(2,1)S(1)}, bf16[2048,128]{1,0:T(8,128)(2,1)S(1)}, u32[]{:S(2)}, u32[]{:S(2)}) collective-permute-start(bf16[2048,128]{1,0:T(8,128)(2,1)S(1)} %slice.36), channel_id=1, source_target_pairs={{0,6},{1,25},{2,0},{3,27},{4,2},{5,29},{6,4},{7,31},{8,14},{9,1},{... | collective-permute-start | bytes 1572872 | tf_op jit(solution)/shard_map/ppermute | solution.py:316
  25.4 16.5 %collective-permute-start.12 = (bf16[1792,128]{1,0:T(8,128)(2,1)S(1)}, bf16[1792,128]{1,0:T(8,128)(2,1)S(1)}, u32[]{:S(2)}, u32[]{:S(2)}) collective-permute-start(bf16[1792,128]{1,0:T(8,128)(2,1)S(1)} %slice.34), channel_id=1, source_target_pairs={{0,2},{1,9},{2,4},{3,11},{4,6},{5,13},{6,0},{7,15},{8,10},{9,17},{... | collective-permute-start | bytes 1376264 | tf_op jit(solution)/shard_map/ppermute | solution.py:316
  25.5 9.5 %collective-permute-start.9 = (bf16[4,8,4096]{2,1,0:T(8,128)(2,1)S(1)}, bf16[4,8,4096]{2,1,0:T(8,128)(2,1)S(1)}, u32[]{:S(2)}, u32[]{:S(2)}) collective-permute-start(bf16[4,8,4096]{2,1,0:T(8,128)(2,1)S(1)} %pad_maximum_fusion), channel_id=1, source_target_pairs={{0,64},{1,5},{2,66},{3,7},{4,68},{5,1},{6,70},{7,3},{8,72},{9,13},... | collective-permute-start | bytes 786440 | tf_op jit(solution)/shard_map/ppermute | solution.py:316
  27.3 11.6 %collective-permute-start.10 = (bf16[4,8,4096]{2,1,0:T(8,128)(2,1)S(1)}, bf16[4,8,4096]{2,1,0:T(8,128)(2,1)S(1)}, u32[]{:S(2)}, u32[]{:S(2)}) collective-permute-start(bf16[4,8,4096]{2,1,0:T(8,128)(2,1)S(1)} %pad_maximum_fusion), channel_id=1, source_target_pairs={{0,32},{1,3},{2,34},{3,5},{4,36},{5,7},{6,38},{7,1},{8,40},{9,11},... | collective-permute-start | bytes 786440 | tf_op jit(solution)/shard_map/ppermute | solution.py:316
  27.4 11.5 %collective-permute-start.11 = (bf16[4,8,4096]{2,1,0:T(8,128)(2,1)S(1)}, bf16[4,8,4096]{2,1,0:T(8,128)(2,1)S(1)}, u32[]{:S(2)}, u32[]{:S(2)}) collective-permute-start(bf16[4,8,4096]{2,1,0:T(8,128)(2,1)S(1)} %pad_maximum_fusion), channel_id=1, source_target_pairs={{0,96},{1,7},{2,98},{3,1},{4,100},{5,3},{6,102},{7,5},{8,104},{9,1... | collective-permute-start | bytes 786440 | tf_op jit(solution)/shard_map/ppermute | solution.py:316
  30.1 14.3 %copy-start = (bf16[4096,128]{1,0:T(8,128)(2,1)S(1)}, bf16[4096,128]{1,0:T(8,128)(2,1)}, u32[]{:S(2)}) copy-start(bf16[4096,128]{1,0:T(8,128)(2,1)} %param.18) | copy-start | bytes 3145732
  39.4 6.2 %collective-permute-start.15 = (f32[128,128]{1,0:T(8,128)S(1)}, f32[128,128]{1,0:T(8,128)S(1)}, u32[]{:S(2)}, u32[]{:S(2)}) collective-permute-start(f32[128,128]{1,0:T(8,128)S(1)} %fusion.17), channel_id=1, source_target_pairs={{0,6},{1,25},{2,0},{3,27},{4,2},{5,29},{6,4},{7,31},{8,14},{9,1},{... | collective-permute-start | bytes 196616 | tf_op jit(solution)/shard_map/ppermute | solution.py:316
  41.8 4.4 %collective-permute-start.16 = (f32[128,128]{1,0:T(8,128)S(1)}, f32[128,128]{1,0:T(8,128)S(1)}, u32[]{:S(2)}, u32[]{:S(2)}) collective-permute-start(f32[128,128]{1,0:T(8,128)S(1)} %fusion.15), channel_id=1, source_target_pairs={{0,2},{1,9},{2,4},{3,11},{4,6},{5,13},{6,0},{7,15},{8,10},{9,17},{... | collective-permute-start | bytes 196616 | tf_op jit(solution)/shard_map/ppermute | solution.py:316
  42.6 5.6 %collective-permute-start.14 = (f32[128,128]{1,0:T(8,128)S(1)}, f32[128,128]{1,0:T(8,128)S(1)}, u32[]{:S(2)}, u32[]{:S(2)}) collective-permute-start(f32[128,128]{1,0:T(8,128)S(1)} %fusion), channel_id=1, source_target_pairs={{0,4},{1,17},{2,6},{3,19},{4,0},{5,21},{6,2},{7,23},{8,12},{9,25},... | collective-permute-start | bytes 196616 | tf_op jit(solution)/shard_map/ppermute | solution.py:316
  44.8 4.6 %collective-permute-start.17 = (f32[128,128]{1,0:T(8,128)S(1)}, f32[128,128]{1,0:T(8,128)S(1)}, u32[]{:S(2)}, u32[]{:S(2)}) collective-permute-start(f32[128,128]{1,0:T(8,128)S(1)} %fusion.19.refs_0_), channel_id=1, source_target_pairs={{0,1},{1,0},{2,3},{3,2},{4,5},{5,4},{6,7},{7,6},{8,9},{9,8},{10,11... | collective-permute-start | bytes 196616 | tf_op jit(solution)/shard_map/ppermute | solution.py:293
  45.6 3.8 %collective-permute-start.19 = (f32[128,128]{1,0:T(8,128)S(1)}, f32[128,128]{1,0:T(8,128)S(1)}, u32[]{:S(2)}, u32[]{:S(2)}) collective-permute-start(f32[128,128]{1,0:T(8,128)S(1)} %collective-permute-done.15.refs_2_), channel_id=1, source_target_pairs={{0,1},{1,0},{2,3},{3,2},{4,5},{5,4},{6,7},{7,6},{8,9},{9,8},{10,11... | collective-permute-start | bytes 196616 | tf_op jit(solution)/shard_map/ppermute | solution.py:293
  46.2 3.2 %collective-permute-start.20 = (f32[128,128]{1,0:T(8,128)S(1)}, f32[128,128]{1,0:T(8,128)S(1)}, u32[]{:S(2)}, u32[]{:S(2)}) collective-permute-start(f32[128,128]{1,0:T(8,128)S(1)} %collective-permute-done.16.refs_3_), channel_id=1, source_target_pairs={{0,1},{1,0},{2,3},{3,2},{4,5},{5,4},{6,7},{7,6},{8,9},{9,8},{10,11... | collective-permute-start | bytes 196616 | tf_op jit(solution)/shard_map/ppermute | solution.py:293
  48.3 2.0 %collective-permute-start.18 = (f32[128,128]{1,0:T(8,128)S(1)}, f32[128,128]{1,0:T(8,128)S(1)}, u32[]{:S(2)}, u32[]{:S(2)}) collective-permute-start(f32[128,128]{1,0:T(8,128)S(1)} %collective-permute-done.14.refs_1_), channel_id=1, source_target_pairs={{0,1},{1,0},{2,3},{3,2},{4,5},{5,4},{6,7},{7,6},{8,9},{9,8},{10,11... | collective-permute-start | bytes 196616 | tf_op jit(solution)/shard_map/ppermute | solution.py:293

commit v6 on v5

--- a/solution.py
+++ b/solution.py
@@ -295,9 +295,9 @@
 
 AXES = {"z": 16, "y": 4, "x": 1}
 SIDE = 4
-WEIGHT_AXIS = ("x", "y")
-FIRST_AXIS = ("y", "z")
-SECOND_AXIS = ("z", "x")
+WEIGHT_AXIS = ("y", "z")
+FIRST_AXIS = ("z", "x")
+SECOND_AXIS = ("x", "y")
 SHIFTS = (1, -1, 2)
 FIRST_SHIFTS = SECOND_SHIFTS = OUT_SHIFTS = (2, 1, -1)
 

time: 51.3 us -> 50.7 us (0.988)
  starting transfers between devices: 30.2 us -> 28.3 us
  waiting for transfers between devices: 11.3 us -> 12.6 us
    ppermute x7, starting transfers between devices: 8.96 us -> 5.22 us  [other_core(): return lax.ppermute(x, 'kv', [(0, 1), (1, 0)])]
    ppermute x14, starting transfers between devices: 21.3 us -> 23.1 us  [shifted(): return lax.ppermute(x, ('group', 'kv'), moves)]
    ppermute x14, waiting for transfers between devices: 9.34 us -> 10.7 us  [shifted(): return lax.ppermute(x, ('group', 'kv'), moves)]
  transfers between devices with their start and end apart: 21 -> 21, of which waited for: 7 -> 8; matrix products, arithmetic and copies ran while one was open for 5% -> 5% of each run, Pallas kernels for 11% -> 11%
where the time goes in v6:
time: 50.7 us; the launch traced here: 50.6 us
  starting transfers between devices  28.3 us (56%)
  waiting for transfers between devices  12.6 us (25%)
  Pallas kernels  6.57 us (13%)
  matrix products  2.01 us (4%)
  between operations  0.85 us (2%)
    ppermute x14, starting transfers between devices, shifted(): return lax.ppermute(x, ('group', 'kv'), moves)  23.1 us
    ppermute x14, waiting for transfers between devices, shifted(): return lax.ppermute(x, ('group', 'kv'), moves)  10.7 us
    pallas_call x1, Pallas kernels, attend(): pl.pallas_call(attend_kernel, out_shape=(shape, shape), in_specs=[pl.Bloc...  5.66 us
    ppermute x7, starting transfers between devices, other_core(): return lax.ppermute(x, 'kv', [(0, 1), (1, 0)])  5.22 us
    dot_general x6, matrix products, dot(): return jnp.dot(a, b, preferred_element_type=jnp.float32)  2.01 us
    ppermute x7, waiting for transfers between devices, other_core(): return lax.ppermute(x, 'kv', [(0, 1), (1, 0)])  1.92 us
  transfers between devices with their start and end apart: 21, of which 8 were waited for; matrix products, arithmetic and copies ran while one was open for 5% of the time, Pallas kernels for 11%

profile of v6, /device:TPU:1, one launch (start us, length us, event | category | flops | bytes accessed | tf_op | source)
XLA Modules:
  0.0 50.6 jit_solution(18213313351254395971)
XLA Ops:
  0.0 2.5 %collective-permute-start.4 = (bf16[4096,128]{1,0:T(8,128)(2,1)}, bf16[4096,128]{1,0:T(8,128)(2,1)S(1)}, u32[]{:S(2)}, u32[]{:S(2)}) collective-permute-start(bf16[4096,128]{1,0:T(8,128)(2,1)} %param.18), channel_id=1, source_target_pairs={{0,8},{1,33},{2,10},{3,35},{4,12},{5,37},{6,14},{7,39},{8,16},{9,4... | collective-permute-start | bytes 3145736 | tf_op jit(solution)/shard_map/ppermute | solution.py:316
  2.5 2.1 %collective-permute-start.5 = (bf16[4096,128]{1,0:T(8,128)(2,1)}, bf16[4096,128]{1,0:T(8,128)(2,1)S(1)}, u32[]{:S(2)}, u32[]{:S(2)}) collective-permute-start(bf16[4096,128]{1,0:T(8,128)(2,1)} %param.18), channel_id=1, source_target_pairs={{0,24},{1,97},{2,26},{3,99},{4,28},{5,101},{6,30},{7,103},{8,0},{9... | collective-permute-start | bytes 3145736 | tf_op jit(solution)/shard_map/ppermute | solution.py:316
  5.2 5.7 %attend.1 = (f32[3,8,4096]{2,1,0:T(8,128)S(1)}, f32[3,8,4096]{2,1,0:T(8,128)S(1)}) custom-call(s32[1]{0:T(128)S(6)} %copy.17.length_ref, bf16[160,4096]{1,0:T(8,128)(2,1)} %bitcast.66, bf16[4096,1024]{1,0:T(8,128)(2,1)} %bitcast.65, f32[2,2,64,4096]{3,2,1,0:T(8,128)} %constant.7.clone.table_hbm, bf16[8,16]{1,0:T(8,128)(2,1)} %bitcast.70, ...), custom_call_target="tpu_custom_call" | custom-call | flops 3489660928 | bytes 12582912 | tf_op jit(solution)/shard_map/attend/pallas_call | solution.py:248
  10.9 3.3 %collective-permute-start.2 = (f32[8,4096]{1,0:T(8,128)S(1)}, f32[8,4096]{1,0:T(8,128)S(1)}, u32[]{:S(2)}, u32[]{:S(2)}) collective-permute-start(f32[8,4096]{1,0:T(8,128)S(1)} %get-tuple-element.20), channel_id=1, source_target_pairs={{0,1},{1,0},{2,3},{3,2},{4,5},{5,4},{6,7},{7,6},{8,9},{9,8},{10,11... | collective-permute-start | bytes 393224 | tf_op jit(solution)/shard_map/ppermute | solution.py:293
  14.8 0.5 collective-permute-done.2
  15.9 2.9 %collective-permute-start.3 = (bf16[1,8,4096]{2,1,0:T(8,128)(2,1)S(1)}, bf16[1,8,4096]{2,1,0:T(8,128)(2,1)S(1)}, u32[]{:S(2)}, u32[]{:S(2)}) collective-permute-start(bf16[1,8,4096]{2,1,0:T(8,128)(2,1)S(1)} %get-tuple-element.18), channel_id=1, source_target_pairs={{0,64},{1,5},{2,66},{3,7},{4,68},{5,1},{6,70},{7,3},{8,72},{9,13},... | collective-permute-start | bytes 196616 | tf_op jit(solution)/shard_map/ppermute | solution.py:316
  18.8 1.7 %collective-permute-start.6 = (bf16[256,128]{1,0:T(8,128)(2,1)S(1)}, bf16[256,128]{1,0:T(8,128)(2,1)S(1)}, u32[]{:S(2)}, u32[]{:S(2)}) collective-permute-start(bf16[256,128]{1,0:T(8,128)(2,1)S(1)} %slice.31), channel_id=1, source_target_pairs={{0,8},{1,33},{2,10},{3,35},{4,12},{5,37},{6,14},{7,39},{8,16},{9,4... | collective-permute-start | bytes 196616 | tf_op jit(solution)/shard_map/ppermute | solution.py:316
  20.9 2.4 %collective-permute-start.8 = (bf16[1,8,4096]{2,1,0:T(8,128)(2,1)S(1)}, bf16[1,8,4096]{2,1,0:T(8,128)(2,1)S(1)}, u32[]{:S(2)}, u32[]{:S(2)}) collective-permute-start(bf16[1,8,4096]{2,1,0:T(8,128)(2,1)S(1)} %get-tuple-element.18), channel_id=1, source_target_pairs={{0,96},{1,7},{2,98},{3,1},{4,100},{5,3},{6,102},{7,5},{8,104},{9,1... | collective-permute-start | bytes 196616 | tf_op jit(solution)/shard_map/ppermute | solution.py:316
  23.3 2.3 %collective-permute-start.13 = (bf16[2048,128]{1,0:T(8,128)(2,1)S(1)}, bf16[2048,128]{1,0:T(8,128)(2,1)S(1)}, u32[]{:S(2)}, u32[]{:S(2)}) collective-permute-start(bf16[2048,128]{1,0:T(8,128)(2,1)S(1)} %slice.36), channel_id=1, source_target_pairs={{0,24},{1,97},{2,26},{3,99},{4,28},{5,101},{6,30},{7,103},{8,0},{9... | collective-permute-start | bytes 1572872 | tf_op jit(solution)/shard_map/ppermute | solution.py:316
  25.7 1.8 %collective-permute-start.9 = (bf16[4,8,4096]{2,1,0:T(8,128)(2,1)S(1)}, bf16[4,8,4096]{2,1,0:T(8,128)(2,1)S(1)}, u32[]{:S(2)}, u32[]{:S(2)}) collective-permute-start(bf16[4,8,4096]{2,1,0:T(8,128)(2,1)S(1)} %pad_maximum_fusion), channel_id=1, source_target_pairs={{0,4},{1,17},{2,6},{3,19},{4,0},{5,21},{6,2},{7,23},{8,12},{9,25},... | collective-permute-start | bytes 786440 | tf_op jit(solution)/shard_map/ppermute | solution.py:316
  27.4 0.6 %collective-permute-start.10 = (bf16[4,8,4096]{2,1,0:T(8,128)(2,1)S(1)}, bf16[4,8,4096]{2,1,0:T(8,128)(2,1)S(1)}, u32[]{:S(2)}, u32[]{:S(2)}) collective-permute-start(bf16[4,8,4096]{2,1,0:T(8,128)(2,1)S(1)} %pad_maximum_fusion), channel_id=1, source_target_pairs={{0,2},{1,9},{2,4},{3,11},{4,6},{5,13},{6,0},{7,15},{8,10},{9,17},{... | collective-permute-start | bytes 786440 | tf_op jit(solution)/shard_map/ppermute | solution.py:316
  28.1 2.1 %collective-permute-start.11 = (bf16[4,8,4096]{2,1,0:T(8,128)(2,1)S(1)}, bf16[4,8,4096]{2,1,0:T(8,128)(2,1)S(1)}, u32[]{:S(2)}, u32[]{:S(2)}) collective-permute-start(bf16[4,8,4096]{2,1,0:T(8,128)(2,1)S(1)} %pad_maximum_fusion), channel_id=1, source_target_pairs={{0,6},{1,25},{2,0},{3,27},{4,2},{5,29},{6,4},{7,31},{8,14},{9,1},{... | collective-permute-start | bytes 786440 | tf_op jit(solution)/shard_map/ppermute | solution.py:316
  30.2 4.9 %collective-permute-done.9 = bf16[4,8,4096]{2,1,0:T(8,128)(2,1)S(1)} collective-permute-done((bf16[4,8,4096]{2,1,0:T(8,128)(2,1)S(1)}, bf16[4,8,4096]{2,1,0:T(8,128)(2,1)S(1)}, u32[]{:S(2)}, u32[]{:S(2)}) %collective-permute-start.9) | collective-permute-done | bytes 262176 | tf_op jit(solution)/shard_map/ppermute | solution.py:316
  35.1 3.9 %collective-permute-done.10 = bf16[4,8,4096]{2,1,0:T(8,128)(2,1)S(1)} collective-permute-done((bf16[4,8,4096]{2,1,0:T(8,128)(2,1)S(1)}, bf16[4,8,4096]{2,1,0:T(8,128)(2,1)S(1)}, u32[]{:S(2)}, u32[]{:S(2)}) %collective-permute-start.10) | collective-permute-done | bytes 262176 | tf_op jit(solution)/shard_map/ppermute | solution.py:316
  39.0 0.4 fusion.17
  39.5 2.9 %collective-permute-start.15 = (f32[128,128]{1,0:T(8,128)S(1)}, f32[128,128]{1,0:T(8,128)S(1)}, u32[]{:S(2)}, u32[]{:S(2)}) collective-permute-start(f32[128,128]{1,0:T(8,128)S(1)} %fusion.17), channel_id=1, source_target_pairs={{0,24},{1,97},{2,26},{3,99},{4,28},{5,101},{6,30},{7,103},{8,0},{9... | collective-permute-start | bytes 196616 | tf_op jit(solution)/shard_map/ppermute | solution.py:316
  42.4 0.4 fusion.15
  43.7 1.4 %collective-permute-start.14 = (f32[128,128]{1,0:T(8,128)S(1)}, f32[128,128]{1,0:T(8,128)S(1)}, u32[]{:S(2)}, u32[]{:S(2)}) collective-permute-start(f32[128,128]{1,0:T(8,128)S(1)} %fusion), channel_id=1, source_target_pairs={{0,16},{1,65},{2,18},{3,67},{4,20},{5,69},{6,22},{7,71},{8,24},{9,... | collective-permute-start | bytes 196616 | tf_op jit(solution)/shard_map/ppermute | solution.py:316
  45.1 0.4 fusion.19.refs_0_
  45.6 0.5 collective-permute-start.19
  46.1 1.1 %collective-permute-done.16.refs_3_ = f32[128,128]{1,0:T(8,128)S(1)} collective-permute-done((f32[128,128]{1,0:T(8,128)S(1)}, f32[128,128]{1,0:T(8,128)S(1)}, u32[]{:S(2)}, u32[]{:S(2)}) %collective-permute-start.16) | collective-permute-done | bytes 65568 | tf_op jit(solution)/shard_map/ppermute | solution.py:316
  47.7 0.7 %collective-permute-done.14.refs_1_ = f32[128,128]{1,0:T(8,128)S(1)} collective-permute-done((f32[128,128]{1,0:T(8,128)S(1)}, f32[128,128]{1,0:T(8,128)S(1)}, u32[]{:S(2)}, u32[]{:S(2)}) %collective-permute-start.14) | collective-permute-done | bytes 65568 | tf_op jit(solution)/shard_map/ppermute | solution.py:316
  48.8 0.9 %collective-permute-done.18.refs_5_ = f32[128,128]{1,0:T(8,128)S(1)} collective-permute-done((f32[128,128]{1,0:T(8,128)S(1)}, f32[128,128]{1,0:T(8,128)S(1)}, u32[]{:S(2)}, u32[]{:S(2)}) %collective-permute-start.18) | collective-permute-done | bytes 65568 | tf_op jit(solution)/shard_map/ppermute | solution.py:293
  49.7 0.9 %assemble.1 = f32[256,128]{1,0:T(8,128)} custom-call(f32[128,128]{1,0:T(8,128)S(1)} %fusion.19.refs_0_, f32[128,128]{1,0:T(8,128)S(1)} %collective-permute-done.14.refs_1_, f32[128,128]{1,0:T(8,128)S(1)} %collective-permute-done.15.refs_2_, f32[128,128]{1,0:T(8,128)S(1)} %collective-permute-done.16.refs_3_, f32[128,128]{1,0:T(8,128)S(1)} %collective-permute-done.17.refs_4_, ...), custom_call_target="tpu_custom_call" | custom-call | tf_op jit(solution)/shard_map/assemble/pallas_call | solution.py:354
  (40 shorter events, 3.4 us)
Async XLA Ops:
  0.0 18.8 %collective-permute-start.4 = (bf16[4096,128]{1,0:T(8,128)(2,1)}, bf16[4096,128]{1,0:T(8,128)(2,1)S(1)}, u32[]{:S(2)}, u32[]{:S(2)}) collective-permute-start(bf16[4096,128]{1,0:T(8,128)(2,1)} %param.18), channel_id=1, source_target_pairs={{0,8},{1,33},{2,10},{3,35},{4,12},{5,37},{6,14},{7,39},{8,16},{9,4... | collective-permute-start | bytes 3145736 | tf_op jit(solution)/shard_map/ppermute | solution.py:316
  2.5 16.4 %collective-permute-start.5 = (bf16[4096,128]{1,0:T(8,128)(2,1)}, bf16[4096,128]{1,0:T(8,128)(2,1)S(1)}, u32[]{:S(2)}, u32[]{:S(2)}) collective-permute-start(bf16[4096,128]{1,0:T(8,128)(2,1)} %param.18), channel_id=1, source_target_pairs={{0,24},{1,97},{2,26},{3,99},{4,28},{5,101},{6,30},{7,103},{8,0},{9... | collective-permute-start | bytes 3145736 | tf_op jit(solution)/shard_map/ppermute | solution.py:316
  10.9 4.3 %collective-permute-start.2 = (f32[8,4096]{1,0:T(8,128)S(1)}, f32[8,4096]{1,0:T(8,128)S(1)}, u32[]{:S(2)}, u32[]{:S(2)}) collective-permute-start(f32[8,4096]{1,0:T(8,128)S(1)} %get-tuple-element.20), channel_id=1, source_target_pairs={{0,1},{1,0},{2,3},{3,2},{4,5},{5,4},{6,7},{7,6},{8,9},{9,8},{10,11... | collective-permute-start | bytes 393224 | tf_op jit(solution)/shard_map/ppermute | solution.py:293
  14.3 1.3 %collective-permute-start.1 = (f32[8,4096]{1,0:T(8,128)S(1)}, f32[8,4096]{1,0:T(8,128)S(1)}, u32[]{:S(2)}, u32[]{:S(2)}) collective-permute-start(f32[8,4096]{1,0:T(8,128)S(1)} %get-tuple-element.21), channel_id=1, source_target_pairs={{0,1},{1,0},{2,3},{3,2},{4,5},{5,4},{6,7},{7,6},{8,9},{9,8},{10,11... | collective-permute-start | bytes 393224 | tf_op jit(solution)/shard_map/ppermute | solution.py:293
  14.4 1.4 %collective-permute-start = (f32[8,4096]{1,0:T(8,128)S(1)}, f32[8,4096]{1,0:T(8,128)S(1)}, u32[]{:S(2)}, u32[]{:S(2)}) collective-permute-start(f32[8,4096]{1,0:T(8,128)S(1)} %get-tuple-element.19), channel_id=1, source_target_pairs={{0,1},{1,0},{2,3},{3,2},{4,5},{5,4},{6,7},{7,6},{8,9},{9,8},{10,11... | collective-permute-start | bytes 393224 | tf_op jit(solution)/shard_map/ppermute | solution.py:293
  15.9 9.7 %collective-permute-start.3 = (bf16[1,8,4096]{2,1,0:T(8,128)(2,1)S(1)}, bf16[1,8,4096]{2,1,0:T(8,128)(2,1)S(1)}, u32[]{:S(2)}, u32[]{:S(2)}) collective-permute-start(bf16[1,8,4096]{2,1,0:T(8,128)(2,1)S(1)} %get-tuple-element.18), channel_id=1, source_target_pairs={{0,64},{1,5},{2,66},{3,7},{4,68},{5,1},{6,70},{7,3},{8,72},{9,13},... | collective-permute-start | bytes 196616 | tf_op jit(solution)/shard_map/ppermute | solution.py:316
  18.8 6.7 %collective-permute-start.6 = (bf16[256,128]{1,0:T(8,128)(2,1)S(1)}, bf16[256,128]{1,0:T(8,128)(2,1)S(1)}, u32[]{:S(2)}, u32[]{:S(2)}) collective-permute-start(bf16[256,128]{1,0:T(8,128)(2,1)S(1)} %slice.31), channel_id=1, source_target_pairs={{0,8},{1,33},{2,10},{3,35},{4,12},{5,37},{6,14},{7,39},{8,16},{9,4... | collective-permute-start | bytes 196616 | tf_op jit(solution)/shard_map/ppermute | solution.py:316
  20.6 5.0 %collective-permute-start.7 = (bf16[1,8,4096]{2,1,0:T(8,128)(2,1)S(1)}, bf16[1,8,4096]{2,1,0:T(8,128)(2,1)S(1)}, u32[]{:S(2)}, u32[]{:S(2)}) collective-permute-start(bf16[1,8,4096]{2,1,0:T(8,128)(2,1)S(1)} %get-tuple-element.18), channel_id=1, source_target_pairs={{0,32},{1,3},{2,34},{3,5},{4,36},{5,7},{6,38},{7,1},{8,40},{9,11},... | collective-permute-start | bytes 196616 | tf_op jit(solution)/shard_map/ppermute | solution.py:316
  20.9 4.7 %collective-permute-start.8 = (bf16[1,8,4096]{2,1,0:T(8,128)(2,1)S(1)}, bf16[1,8,4096]{2,1,0:T(8,128)(2,1)S(1)}, u32[]{:S(2)}, u32[]{:S(2)}) collective-permute-start(bf16[1,8,4096]{2,1,0:T(8,128)(2,1)S(1)} %get-tuple-element.18), channel_id=1, source_target_pairs={{0,96},{1,7},{2,98},{3,1},{4,100},{5,3},{6,102},{7,5},{8,104},{9,1... | collective-permute-start | bytes 196616 | tf_op jit(solution)/shard_map/ppermute | solution.py:316
  23.3 19.9 %collective-permute-start.13 = (bf16[2048,128]{1,0:T(8,128)(2,1)S(1)}, bf16[2048,128]{1,0:T(8,128)(2,1)S(1)}, u32[]{:S(2)}, u32[]{:S(2)}) collective-permute-start(bf16[2048,128]{1,0:T(8,128)(2,1)S(1)} %slice.36), channel_id=1, source_target_pairs={{0,24},{1,97},{2,26},{3,99},{4,28},{5,101},{6,30},{7,103},{8,0},{9... | collective-permute-start | bytes 1572872 | tf_op jit(solution)/shard_map/ppermute | solution.py:316
  25.6 17.3 %collective-permute-start.12 = (bf16[1792,128]{1,0:T(8,128)(2,1)S(1)}, bf16[1792,128]{1,0:T(8,128)(2,1)S(1)}, u32[]{:S(2)}, u32[]{:S(2)}) collective-permute-start(bf16[1792,128]{1,0:T(8,128)(2,1)S(1)} %slice.34), channel_id=1, source_target_pairs={{0,8},{1,33},{2,10},{3,35},{4,12},{5,37},{6,14},{7,39},{8,16},{9,4... | collective-permute-start | bytes 1376264 | tf_op jit(solution)/shard_map/ppermute | solution.py:316
  25.7 9.4 %collective-permute-start.9 = (bf16[4,8,4096]{2,1,0:T(8,128)(2,1)S(1)}, bf16[4,8,4096]{2,1,0:T(8,128)(2,1)S(1)}, u32[]{:S(2)}, u32[]{:S(2)}) collective-permute-start(bf16[4,8,4096]{2,1,0:T(8,128)(2,1)S(1)} %pad_maximum_fusion), channel_id=1, source_target_pairs={{0,4},{1,17},{2,6},{3,19},{4,0},{5,21},{6,2},{7,23},{8,12},{9,25},... | collective-permute-start | bytes 786440 | tf_op jit(solution)/shard_map/ppermute | solution.py:316
  27.4 11.5 %collective-permute-start.10 = (bf16[4,8,4096]{2,1,0:T(8,128)(2,1)S(1)}, bf16[4,8,4096]{2,1,0:T(8,128)(2,1)S(1)}, u32[]{:S(2)}, u32[]{:S(2)}) collective-permute-start(bf16[4,8,4096]{2,1,0:T(8,128)(2,1)S(1)} %pad_maximum_fusion), channel_id=1, source_target_pairs={{0,2},{1,9},{2,4},{3,11},{4,6},{5,13},{6,0},{7,15},{8,10},{9,17},{... | collective-permute-start | bytes 786440 | tf_op jit(solution)/shard_map/ppermute | solution.py:316
  28.1 10.9 %collective-permute-start.11 = (bf16[4,8,4096]{2,1,0:T(8,128)(2,1)S(1)}, bf16[4,8,4096]{2,1,0:T(8,128)(2,1)S(1)}, u32[]{:S(2)}, u32[]{:S(2)}) collective-permute-start(bf16[4,8,4096]{2,1,0:T(8,128)(2,1)S(1)} %pad_maximum_fusion), channel_id=1, source_target_pairs={{0,6},{1,25},{2,0},{3,27},{4,2},{5,29},{6,4},{7,31},{8,14},{9,1},{... | collective-permute-start | bytes 786440 | tf_op jit(solution)/shard_map/ppermute | solution.py:316
  30.2 15.0 %copy-start = (bf16[4096,128]{1,0:T(8,128)(2,1)S(1)}, bf16[4096,128]{1,0:T(8,128)(2,1)}, u32[]{:S(2)}) copy-start(bf16[4096,128]{1,0:T(8,128)(2,1)} %param.18) | copy-start | bytes 3145732
  39.5 6.2 %collective-permute-start.15 = (f32[128,128]{1,0:T(8,128)S(1)}, f32[128,128]{1,0:T(8,128)S(1)}, u32[]{:S(2)}, u32[]{:S(2)}) collective-permute-start(f32[128,128]{1,0:T(8,128)S(1)} %fusion.17), channel_id=1, source_target_pairs={{0,24},{1,97},{2,26},{3,99},{4,28},{5,101},{6,30},{7,103},{8,0},{9... | collective-permute-start | bytes 196616 | tf_op jit(solution)/shard_map/ppermute | solution.py:316
  42.8 4.4 %collective-permute-start.16 = (f32[128,128]{1,0:T(8,128)S(1)}, f32[128,128]{1,0:T(8,128)S(1)}, u32[]{:S(2)}, u32[]{:S(2)}) collective-permute-start(f32[128,128]{1,0:T(8,128)S(1)} %fusion.15), channel_id=1, source_target_pairs={{0,8},{1,33},{2,10},{3,35},{4,12},{5,37},{6,14},{7,39},{8,16},{9,4... | collective-permute-start | bytes 196616 | tf_op jit(solution)/shard_map/ppermute | solution.py:316
  43.7 4.7 %collective-permute-start.14 = (f32[128,128]{1,0:T(8,128)S(1)}, f32[128,128]{1,0:T(8,128)S(1)}, u32[]{:S(2)}, u32[]{:S(2)}) collective-permute-start(f32[128,128]{1,0:T(8,128)S(1)} %fusion), channel_id=1, source_target_pairs={{0,16},{1,65},{2,18},{3,67},{4,20},{5,69},{6,22},{7,71},{8,24},{9,... | collective-permute-start | bytes 196616 | tf_op jit(solution)/shard_map/ppermute | solution.py:316
  45.5 3.3 %collective-permute-start.17 = (f32[128,128]{1,0:T(8,128)S(1)}, f32[128,128]{1,0:T(8,128)S(1)}, u32[]{:S(2)}, u32[]{:S(2)}) collective-permute-start(f32[128,128]{1,0:T(8,128)S(1)} %fusion.19.refs_0_), channel_id=1, source_target_pairs={{0,1},{1,0},{2,3},{3,2},{4,5},{5,4},{6,7},{7,6},{8,9},{9,8},{10,11... | collective-permute-start | bytes 196616 | tf_op jit(solution)/shard_map/ppermute | solution.py:293
  45.6 3.2 %collective-permute-start.19 = (f32[128,128]{1,0:T(8,128)S(1)}, f32[128,128]{1,0:T(8,128)S(1)}, u32[]{:S(2)}, u32[]{:S(2)}) collective-permute-start(f32[128,128]{1,0:T(8,128)S(1)} %collective-permute-done.15.refs_2_), channel_id=1, source_target_pairs={{0,1},{1,0},{2,3},{3,2},{4,5},{5,4},{6,7},{7,6},{8,9},{9,8},{10,11... | collective-permute-start | bytes 196616 | tf_op jit(solution)/shard_map/ppermute | solution.py:293
  47.3 1.5 %collective-permute-start.20 = (f32[128,128]{1,0:T(8,128)S(1)}, f32[128,128]{1,0:T(8,128)S(1)}, u32[]{:S(2)}, u32[]{:S(2)}) collective-permute-start(f32[128,128]{1,0:T(8,128)S(1)} %collective-permute-done.16.refs_3_), channel_id=1, source_target_pairs={{0,1},{1,0},{2,3},{3,2},{4,5},{5,4},{6,7},{7,6},{8,9},{9,8},{10,11... | collective-permute-start | bytes 196616 | tf_op jit(solution)/shard_map/ppermute | solution.py:293
  48.4 1.3 %collective-permute-start.18 = (f32[128,128]{1,0:T(8,128)S(1)}, f32[128,128]{1,0:T(8,128)S(1)}, u32[]{:S(2)}, u32[]{:S(2)}) collective-permute-start(f32[128,128]{1,0:T(8,128)S(1)} %collective-permute-done.14.refs_1_), channel_id=1, source_target_pairs={{0,1},{1,0},{2,3},{3,2},{4,5},{5,4},{6,7},{7,6},{8,9},{9,8},{10,11... | collective-permute-start | bytes 196616 | tf_op jit(solution)/shard_map/ppermute | solution.py:293

commit v7 on v6

--- a/solution.py
+++ b/solution.py
@@ -373,8 +373,8 @@
     half = out_weight.shape[0] // 2
     far = [
         shifted(before[:cut], WEIGHT_AXIS, 1),
-        shifted(before[cut:half], WEIGHT_AXIS, 1),
-        shifted(after[half:], WEIGHT_AXIS, -1),
+        shifted(after[cut:half], WEIGHT_AXIS, -1),
+        shifted(before[half:], WEIGHT_AXIS, 1),
     ]
     blocks = [attended[None]] + [shifted(attended[None], FIRST_AXIS, shift) for shift in FIRST_SHIFTS]
     blocks[1], far[0] = lax.optimization_barrier((blocks[1], far[0]))

time: 50.7 us -> 50.2 us (level)
  starting transfers between devices: 28.3 us -> 27.5 us
    ppermute x14, starting transfers between devices: 23.1 us -> 21.9 us  [shifted(): return lax.ppermute(x, ('group', 'kv'), moves)]
where the time goes in v7:
time: 50.2 us; the launch traced here: 50.1 us
  starting transfers between devices  27.5 us (55%)
  waiting for transfers between devices  12.8 us (25%)
  Pallas kernels  6.57 us (13%)
  matrix products  2.01 us (4%)
  between operations  0.81 us (2%)
    ppermute x14, starting transfers between devices, shifted(): return lax.ppermute(x, ('group', 'kv'), moves)  21.9 us
    ppermute x14, waiting for transfers between devices, shifted(): return lax.ppermute(x, ('group', 'kv'), moves)  10.9 us
    pallas_call x1, Pallas kernels, attend(): pl.pallas_call(attend_kernel, out_shape=(shape, shape), in_specs=[pl.Bloc...  5.66 us
    ppermute x7, starting transfers between devices, other_core(): return lax.ppermute(x, 'kv', [(0, 1), (1, 0)])  5.63 us
    dot_general x6, matrix products, dot(): return jnp.dot(a, b, preferred_element_type=jnp.float32)  2.01 us
    ppermute x7, waiting for transfers between devices, other_core(): return lax.ppermute(x, 'kv', [(0, 1), (1, 0)])  1.92 us
  transfers between devices with their start and end apart: 21, of which 8 were waited for; matrix products, arithmetic and copies ran while one was open for 5% of the time, Pallas kernels for 11%

profile of v7, /device:TPU:1, one launch (start us, length us, event | category | flops | bytes accessed | tf_op | source)
XLA Modules:
  0.0 50.1 jit_solution(4454596205962498387)
XLA Ops:
  0.0 2.5 %collective-permute-start.4 = (bf16[4096,128]{1,0:T(8,128)(2,1)}, bf16[4096,128]{1,0:T(8,128)(2,1)S(1)}, u32[]{:S(2)}, u32[]{:S(2)}) collective-permute-start(bf16[4096,128]{1,0:T(8,128)(2,1)} %param.18), channel_id=1, source_target_pairs={{0,8},{1,33},{2,10},{3,35},{4,12},{5,37},{6,14},{7,39},{8,16},{9,4... | collective-permute-start | bytes 3145736 | tf_op jit(solution)/shard_map/ppermute | solution.py:316
  2.5 2.1 %collective-permute-start.5 = (bf16[4096,128]{1,0:T(8,128)(2,1)}, bf16[4096,128]{1,0:T(8,128)(2,1)S(1)}, u32[]{:S(2)}, u32[]{:S(2)}) collective-permute-start(bf16[4096,128]{1,0:T(8,128)(2,1)} %param.18), channel_id=1, source_target_pairs={{0,24},{1,97},{2,26},{3,99},{4,28},{5,101},{6,30},{7,103},{8,0},{9... | collective-permute-start | bytes 3145736 | tf_op jit(solution)/shard_map/ppermute | solution.py:316
  5.2 5.7 %attend.1 = (f32[3,8,4096]{2,1,0:T(8,128)S(1)}, f32[3,8,4096]{2,1,0:T(8,128)S(1)}) custom-call(s32[1]{0:T(128)S(6)} %copy.17.length_ref, bf16[160,4096]{1,0:T(8,128)(2,1)} %bitcast.66, bf16[4096,1024]{1,0:T(8,128)(2,1)} %bitcast.65, f32[2,2,64,4096]{3,2,1,0:T(8,128)} %constant.7.clone.table_hbm, bf16[8,16]{1,0:T(8,128)(2,1)} %bitcast.70, ...), custom_call_target="tpu_custom_call" | custom-call | flops 3489660928 | bytes 12582912 | tf_op jit(solution)/shard_map/attend/pallas_call | solution.py:248
  10.9 3.3 %collective-permute-start.2 = (f32[8,4096]{1,0:T(8,128)S(1)}, f32[8,4096]{1,0:T(8,128)S(1)}, u32[]{:S(2)}, u32[]{:S(2)}) collective-permute-start(f32[8,4096]{1,0:T(8,128)S(1)} %get-tuple-element.20), channel_id=1, source_target_pairs={{0,1},{1,0},{2,3},{3,2},{4,5},{5,4},{6,7},{7,6},{8,9},{9,8},{10,11... | collective-permute-start | bytes 393224 | tf_op jit(solution)/shard_map/ppermute | solution.py:293
  14.8 0.5 collective-permute-done.2
  15.9 2.9 %collective-permute-start.3 = (bf16[1,8,4096]{2,1,0:T(8,128)(2,1)S(1)}, bf16[1,8,4096]{2,1,0:T(8,128)(2,1)S(1)}, u32[]{:S(2)}, u32[]{:S(2)}) collective-permute-start(bf16[1,8,4096]{2,1,0:T(8,128)(2,1)S(1)} %get-tuple-element.18), channel_id=1, source_target_pairs={{0,64},{1,5},{2,66},{3,7},{4,68},{5,1},{6,70},{7,3},{8,72},{9,13},... | collective-permute-start | bytes 196616 | tf_op jit(solution)/shard_map/ppermute | solution.py:316
  18.8 1.7 %collective-permute-start.6 = (bf16[256,128]{1,0:T(8,128)(2,1)S(1)}, bf16[256,128]{1,0:T(8,128)(2,1)S(1)}, u32[]{:S(2)}, u32[]{:S(2)}) collective-permute-start(bf16[256,128]{1,0:T(8,128)(2,1)S(1)} %slice.31), channel_id=1, source_target_pairs={{0,8},{1,33},{2,10},{3,35},{4,12},{5,37},{6,14},{7,39},{8,16},{9,4... | collective-permute-start | bytes 196616 | tf_op jit(solution)/shard_map/ppermute | solution.py:316
  20.9 2.4 %collective-permute-start.8 = (bf16[1,8,4096]{2,1,0:T(8,128)(2,1)S(1)}, bf16[1,8,4096]{2,1,0:T(8,128)(2,1)S(1)}, u32[]{:S(2)}, u32[]{:S(2)}) collective-permute-start(bf16[1,8,4096]{2,1,0:T(8,128)(2,1)S(1)} %get-tuple-element.18), channel_id=1, source_target_pairs={{0,96},{1,7},{2,98},{3,1},{4,100},{5,3},{6,102},{7,5},{8,104},{9,1... | collective-permute-start | bytes 196616 | tf_op jit(solution)/shard_map/ppermute | solution.py:316
  23.3 1.7 %collective-permute-start.13 = (bf16[2048,128]{1,0:T(8,128)(2,1)S(1)}, bf16[2048,128]{1,0:T(8,128)(2,1)S(1)}, u32[]{:S(2)}, u32[]{:S(2)}) collective-permute-start(bf16[2048,128]{1,0:T(8,128)(2,1)S(1)} %slice.36), channel_id=1, source_target_pairs={{0,8},{1,33},{2,10},{3,35},{4,12},{5,37},{6,14},{7,39},{8,16},{9,4... | collective-permute-start | bytes 1572872 | tf_op jit(solution)/shard_map/ppermute | solution.py:316
  25.0 1.1 %collective-permute-start.12 = (bf16[1792,128]{1,0:T(8,128)(2,1)S(1)}, bf16[1792,128]{1,0:T(8,128)(2,1)S(1)}, u32[]{:S(2)}, u32[]{:S(2)}) collective-permute-start(bf16[1792,128]{1,0:T(8,128)(2,1)S(1)} %slice.34), channel_id=1, source_target_pairs={{0,24},{1,97},{2,26},{3,99},{4,28},{5,101},{6,30},{7,103},{8,0},{9... | collective-permute-start | bytes 1376264 | tf_op jit(solution)/shard_map/ppermute | solution.py:316
  26.2 1.8 %collective-permute-start.9 = (bf16[4,8,4096]{2,1,0:T(8,128)(2,1)S(1)}, bf16[4,8,4096]{2,1,0:T(8,128)(2,1)S(1)}, u32[]{:S(2)}, u32[]{:S(2)}) collective-permute-start(bf16[4,8,4096]{2,1,0:T(8,128)(2,1)S(1)} %pad_maximum_fusion), channel_id=1, source_target_pairs={{0,4},{1,17},{2,6},{3,19},{4,0},{5,21},{6,2},{7,23},{8,12},{9,25},... | collective-permute-start | bytes 786440 | tf_op jit(solution)/shard_map/ppermute | solution.py:316
  28.4 2.3 %collective-permute-start.11 = (bf16[4,8,4096]{2,1,0:T(8,128)(2,1)S(1)}, bf16[4,8,4096]{2,1,0:T(8,128)(2,1)S(1)}, u32[]{:S(2)}, u32[]{:S(2)}) collective-permute-start(bf16[4,8,4096]{2,1,0:T(8,128)(2,1)S(1)} %pad_maximum_fusion), channel_id=1, source_target_pairs={{0,6},{1,25},{2,0},{3,27},{4,2},{5,29},{6,4},{7,31},{8,14},{9,1},{... | collective-permute-start | bytes 786440 | tf_op jit(solution)/shard_map/ppermute | solution.py:316
  30.7 5.1 %collective-permute-done.9 = bf16[4,8,4096]{2,1,0:T(8,128)(2,1)S(1)} collective-permute-done((bf16[4,8,4096]{2,1,0:T(8,128)(2,1)S(1)}, bf16[4,8,4096]{2,1,0:T(8,128)(2,1)S(1)}, u32[]{:S(2)}, u32[]{:S(2)}) %collective-permute-start.9) | collective-permute-done | bytes 262176 | tf_op jit(solution)/shard_map/ppermute | solution.py:316
  35.8 3.9 %collective-permute-done.10 = bf16[4,8,4096]{2,1,0:T(8,128)(2,1)S(1)} collective-permute-done((bf16[4,8,4096]{2,1,0:T(8,128)(2,1)S(1)}, bf16[4,8,4096]{2,1,0:T(8,128)(2,1)S(1)}, u32[]{:S(2)}, u32[]{:S(2)}) %collective-permute-start.10) | collective-permute-done | bytes 262176 | tf_op jit(solution)/shard_map/ppermute | solution.py:316
  39.7 0.4 fusion.17
  40.2 1.1 %collective-permute-start.15 = (f32[128,128]{1,0:T(8,128)S(1)}, f32[128,128]{1,0:T(8,128)S(1)}, u32[]{:S(2)}, u32[]{:S(2)}) collective-permute-start(f32[128,128]{1,0:T(8,128)S(1)} %fusion.17), channel_id=1, source_target_pairs={{0,24},{1,97},{2,26},{3,99},{4,28},{5,101},{6,30},{7,103},{8,0},{9... | collective-permute-start | bytes 196616 | tf_op jit(solution)/shard_map/ppermute | solution.py:316
  41.7 0.5 %collective-permute-start.16 = (f32[128,128]{1,0:T(8,128)S(1)}, f32[128,128]{1,0:T(8,128)S(1)}, u32[]{:S(2)}, u32[]{:S(2)}) collective-permute-start(f32[128,128]{1,0:T(8,128)S(1)} %fusion.15), channel_id=1, source_target_pairs={{0,8},{1,33},{2,10},{3,35},{4,12},{5,37},{6,14},{7,39},{8,16},{9,4... | collective-permute-start | bytes 196616 | tf_op jit(solution)/shard_map/ppermute | solution.py:316
  43.0 1.1 %collective-permute-start.14 = (f32[128,128]{1,0:T(8,128)S(1)}, f32[128,128]{1,0:T(8,128)S(1)}, u32[]{:S(2)}, u32[]{:S(2)}) collective-permute-start(f32[128,128]{1,0:T(8,128)S(1)} %fusion), channel_id=1, source_target_pairs={{0,16},{1,65},{2,18},{3,67},{4,20},{5,69},{6,22},{7,71},{8,24},{9,... | collective-permute-start | bytes 196616 | tf_op jit(solution)/shard_map/ppermute | solution.py:316
  44.5 0.6 %collective-permute-start.17 = (f32[128,128]{1,0:T(8,128)S(1)}, f32[128,128]{1,0:T(8,128)S(1)}, u32[]{:S(2)}, u32[]{:S(2)}) collective-permute-start(f32[128,128]{1,0:T(8,128)S(1)} %fusion.19.refs_0_), channel_id=1, source_target_pairs={{0,1},{1,0},{2,3},{3,2},{4,5},{5,4},{6,7},{7,6},{8,9},{9,8},{10,11... | collective-permute-start | bytes 196616 | tf_op jit(solution)/shard_map/ppermute | solution.py:293
  45.2 1.2 %collective-permute-done.16.refs_3_ = f32[128,128]{1,0:T(8,128)S(1)} collective-permute-done((f32[128,128]{1,0:T(8,128)S(1)}, f32[128,128]{1,0:T(8,128)S(1)}, u32[]{:S(2)}, u32[]{:S(2)}) %collective-permute-start.16) | collective-permute-done | bytes 65568 | tf_op jit(solution)/shard_map/ppermute | solution.py:316
  46.4 0.7 %collective-permute-start.20 = (f32[128,128]{1,0:T(8,128)S(1)}, f32[128,128]{1,0:T(8,128)S(1)}, u32[]{:S(2)}, u32[]{:S(2)}) collective-permute-start(f32[128,128]{1,0:T(8,128)S(1)} %collective-permute-done.16.refs_3_), channel_id=1, source_target_pairs={{0,1},{1,0},{2,3},{3,2},{4,5},{5,4},{6,7},{7,6},{8,9},{9,8},{10,11... | collective-permute-start | bytes 196616 | tf_op jit(solution)/shard_map/ppermute | solution.py:293
  47.1 0.7 %collective-permute-done.14.refs_1_ = f32[128,128]{1,0:T(8,128)S(1)} collective-permute-done((f32[128,128]{1,0:T(8,128)S(1)}, f32[128,128]{1,0:T(8,128)S(1)}, u32[]{:S(2)}, u32[]{:S(2)}) %collective-permute-start.14) | collective-permute-done | bytes 65568 | tf_op jit(solution)/shard_map/ppermute | solution.py:316
  48.3 0.9 %collective-permute-done.18.refs_5_ = f32[128,128]{1,0:T(8,128)S(1)} collective-permute-done((f32[128,128]{1,0:T(8,128)S(1)}, f32[128,128]{1,0:T(8,128)S(1)}, u32[]{:S(2)}, u32[]{:S(2)}) %collective-permute-start.18) | collective-permute-done | bytes 65568 | tf_op jit(solution)/shard_map/ppermute | solution.py:293
  49.2 0.9 %assemble.1 = f32[256,128]{1,0:T(8,128)} custom-call(f32[128,128]{1,0:T(8,128)S(1)} %fusion.19.refs_0_, f32[128,128]{1,0:T(8,128)S(1)} %collective-permute-done.14.refs_1_, f32[128,128]{1,0:T(8,128)S(1)} %collective-permute-done.15.refs_2_, f32[128,128]{1,0:T(8,128)S(1)} %collective-permute-done.16.refs_3_, f32[128,128]{1,0:T(8,128)S(1)} %collective-permute-done.17.refs_4_, ...), custom_call_target="tpu_custom_call" | custom-call | tf_op jit(solution)/shard_map/assemble/pallas_call | solution.py:354
  (40 shorter events, 4.2 us)
Async XLA Ops:
  0.0 18.8 %collective-permute-start.4 = (bf16[4096,128]{1,0:T(8,128)(2,1)}, bf16[4096,128]{1,0:T(8,128)(2,1)S(1)}, u32[]{:S(2)}, u32[]{:S(2)}) collective-permute-start(bf16[4096,128]{1,0:T(8,128)(2,1)} %param.18), channel_id=1, source_target_pairs={{0,8},{1,33},{2,10},{3,35},{4,12},{5,37},{6,14},{7,39},{8,16},{9,4... | collective-permute-start | bytes 3145736 | tf_op jit(solution)/shard_map/ppermute | solution.py:316
  2.5 16.4 %collective-permute-start.5 = (bf16[4096,128]{1,0:T(8,128)(2,1)}, bf16[4096,128]{1,0:T(8,128)(2,1)S(1)}, u32[]{:S(2)}, u32[]{:S(2)}) collective-permute-start(bf16[4096,128]{1,0:T(8,128)(2,1)} %param.18), channel_id=1, source_target_pairs={{0,24},{1,97},{2,26},{3,99},{4,28},{5,101},{6,30},{7,103},{8,0},{9... | collective-permute-start | bytes 3145736 | tf_op jit(solution)/shard_map/ppermute | solution.py:316
  10.9 4.3 %collective-permute-start.2 = (f32[8,4096]{1,0:T(8,128)S(1)}, f32[8,4096]{1,0:T(8,128)S(1)}, u32[]{:S(2)}, u32[]{:S(2)}) collective-permute-start(f32[8,4096]{1,0:T(8,128)S(1)} %get-tuple-element.20), channel_id=1, source_target_pairs={{0,1},{1,0},{2,3},{3,2},{4,5},{5,4},{6,7},{7,6},{8,9},{9,8},{10,11... | collective-permute-start | bytes 393224 | tf_op jit(solution)/shard_map/ppermute | solution.py:293
  14.3 1.3 %collective-permute-start.1 = (f32[8,4096]{1,0:T(8,128)S(1)}, f32[8,4096]{1,0:T(8,128)S(1)}, u32[]{:S(2)}, u32[]{:S(2)}) collective-permute-start(f32[8,4096]{1,0:T(8,128)S(1)} %get-tuple-element.21), channel_id=1, source_target_pairs={{0,1},{1,0},{2,3},{3,2},{4,5},{5,4},{6,7},{7,6},{8,9},{9,8},{10,11... | collective-permute-start | bytes 393224 | tf_op jit(solution)/shard_map/ppermute | solution.py:293
  14.4 1.4 %collective-permute-start = (f32[8,4096]{1,0:T(8,128)S(1)}, f32[8,4096]{1,0:T(8,128)S(1)}, u32[]{:S(2)}, u32[]{:S(2)}) collective-permute-start(f32[8,4096]{1,0:T(8,128)S(1)} %get-tuple-element.19), channel_id=1, source_target_pairs={{0,1},{1,0},{2,3},{3,2},{4,5},{5,4},{6,7},{7,6},{8,9},{9,8},{10,11... | collective-permute-start | bytes 393224 | tf_op jit(solution)/shard_map/ppermute | solution.py:293
  15.9 9.1 %collective-permute-start.3 = (bf16[1,8,4096]{2,1,0:T(8,128)(2,1)S(1)}, bf16[1,8,4096]{2,1,0:T(8,128)(2,1)S(1)}, u32[]{:S(2)}, u32[]{:S(2)}) collective-permute-start(bf16[1,8,4096]{2,1,0:T(8,128)(2,1)S(1)} %get-tuple-element.18), channel_id=1, source_target_pairs={{0,64},{1,5},{2,66},{3,7},{4,68},{5,1},{6,70},{7,3},{8,72},{9,13},... | collective-permute-start | bytes 196616 | tf_op jit(solution)/shard_map/ppermute | solution.py:316
  18.8 7.3 %collective-permute-start.6 = (bf16[256,128]{1,0:T(8,128)(2,1)S(1)}, bf16[256,128]{1,0:T(8,128)(2,1)S(1)}, u32[]{:S(2)}, u32[]{:S(2)}) collective-permute-start(bf16[256,128]{1,0:T(8,128)(2,1)S(1)} %slice.31), channel_id=1, source_target_pairs={{0,8},{1,33},{2,10},{3,35},{4,12},{5,37},{6,14},{7,39},{8,16},{9,4... | collective-permute-start | bytes 196616 | tf_op jit(solution)/shard_map/ppermute | solution.py:316
  20.6 5.6 %collective-permute-start.7 = (bf16[1,8,4096]{2,1,0:T(8,128)(2,1)S(1)}, bf16[1,8,4096]{2,1,0:T(8,128)(2,1)S(1)}, u32[]{:S(2)}, u32[]{:S(2)}) collective-permute-start(bf16[1,8,4096]{2,1,0:T(8,128)(2,1)S(1)} %get-tuple-element.18), channel_id=1, source_target_pairs={{0,32},{1,3},{2,34},{3,5},{4,36},{5,7},{6,38},{7,1},{8,40},{9,11},... | collective-permute-start | bytes 196616 | tf_op jit(solution)/shard_map/ppermute | solution.py:316
  20.9 5.3 %collective-permute-start.8 = (bf16[1,8,4096]{2,1,0:T(8,128)(2,1)S(1)}, bf16[1,8,4096]{2,1,0:T(8,128)(2,1)S(1)}, u32[]{:S(2)}, u32[]{:S(2)}) collective-permute-start(bf16[1,8,4096]{2,1,0:T(8,128)(2,1)S(1)} %get-tuple-element.18), channel_id=1, source_target_pairs={{0,96},{1,7},{2,98},{3,1},{4,100},{5,3},{6,102},{7,5},{8,104},{9,1... | collective-permute-start | bytes 196616 | tf_op jit(solution)/shard_map/ppermute | solution.py:316
  23.3 19.2 %collective-permute-start.13 = (bf16[2048,128]{1,0:T(8,128)(2,1)S(1)}, bf16[2048,128]{1,0:T(8,128)(2,1)S(1)}, u32[]{:S(2)}, u32[]{:S(2)}) collective-permute-start(bf16[2048,128]{1,0:T(8,128)(2,1)S(1)} %slice.36), channel_id=1, source_target_pairs={{0,8},{1,33},{2,10},{3,35},{4,12},{5,37},{6,14},{7,39},{8,16},{9,4... | collective-permute-start | bytes 1572872 | tf_op jit(solution)/shard_map/ppermute | solution.py:316
  25.0 17.2 %collective-permute-start.12 = (bf16[1792,128]{1,0:T(8,128)(2,1)S(1)}, bf16[1792,128]{1,0:T(8,128)(2,1)S(1)}, u32[]{:S(2)}, u32[]{:S(2)}) collective-permute-start(bf16[1792,128]{1,0:T(8,128)(2,1)S(1)} %slice.34), channel_id=1, source_target_pairs={{0,24},{1,97},{2,26},{3,99},{4,28},{5,101},{6,30},{7,103},{8,0},{9... | collective-permute-start | bytes 1376264 | tf_op jit(solution)/shard_map/ppermute | solution.py:316
  26.2 9.6 %collective-permute-start.9 = (bf16[4,8,4096]{2,1,0:T(8,128)(2,1)S(1)}, bf16[4,8,4096]{2,1,0:T(8,128)(2,1)S(1)}, u32[]{:S(2)}, u32[]{:S(2)}) collective-permute-start(bf16[4,8,4096]{2,1,0:T(8,128)(2,1)S(1)} %pad_maximum_fusion), channel_id=1, source_target_pairs={{0,4},{1,17},{2,6},{3,19},{4,0},{5,21},{6,2},{7,23},{8,12},{9,25},... | collective-permute-start | bytes 786440 | tf_op jit(solution)/shard_map/ppermute | solution.py:316
  28.0 11.7 %collective-permute-start.10 = (bf16[4,8,4096]{2,1,0:T(8,128)(2,1)S(1)}, bf16[4,8,4096]{2,1,0:T(8,128)(2,1)S(1)}, u32[]{:S(2)}, u32[]{:S(2)}) collective-permute-start(bf16[4,8,4096]{2,1,0:T(8,128)(2,1)S(1)} %pad_maximum_fusion), channel_id=1, source_target_pairs={{0,2},{1,9},{2,4},{3,11},{4,6},{5,13},{6,0},{7,15},{8,10},{9,17},{... | collective-permute-start | bytes 786440 | tf_op jit(solution)/shard_map/ppermute | solution.py:316
  28.4 11.3 %collective-permute-start.11 = (bf16[4,8,4096]{2,1,0:T(8,128)(2,1)S(1)}, bf16[4,8,4096]{2,1,0:T(8,128)(2,1)S(1)}, u32[]{:S(2)}, u32[]{:S(2)}) collective-permute-start(bf16[4,8,4096]{2,1,0:T(8,128)(2,1)S(1)} %pad_maximum_fusion), channel_id=1, source_target_pairs={{0,6},{1,25},{2,0},{3,27},{4,2},{5,29},{6,4},{7,31},{8,14},{9,1},{... | collective-permute-start | bytes 786440 | tf_op jit(solution)/shard_map/ppermute | solution.py:316
  30.7 13.4 %copy-start = (bf16[4096,128]{1,0:T(8,128)(2,1)S(1)}, bf16[4096,128]{1,0:T(8,128)(2,1)}, u32[]{:S(2)}) copy-start(bf16[4096,128]{1,0:T(8,128)(2,1)} %param.18) | copy-start | bytes 3145732
  40.2 4.9 %collective-permute-start.15 = (f32[128,128]{1,0:T(8,128)S(1)}, f32[128,128]{1,0:T(8,128)S(1)}, u32[]{:S(2)}, u32[]{:S(2)}) collective-permute-start(f32[128,128]{1,0:T(8,128)S(1)} %fusion.17), channel_id=1, source_target_pairs={{0,24},{1,97},{2,26},{3,99},{4,28},{5,101},{6,30},{7,103},{8,0},{9... | collective-permute-start | bytes 196616 | tf_op jit(solution)/shard_map/ppermute | solution.py:316
  41.7 4.7 %collective-permute-start.16 = (f32[128,128]{1,0:T(8,128)S(1)}, f32[128,128]{1,0:T(8,128)S(1)}, u32[]{:S(2)}, u32[]{:S(2)}) collective-permute-start(f32[128,128]{1,0:T(8,128)S(1)} %fusion.15), channel_id=1, source_target_pairs={{0,8},{1,33},{2,10},{3,35},{4,12},{5,37},{6,14},{7,39},{8,16},{9,4... | collective-permute-start | bytes 196616 | tf_op jit(solution)/shard_map/ppermute | solution.py:316
  43.0 4.9 %collective-permute-start.14 = (f32[128,128]{1,0:T(8,128)S(1)}, f32[128,128]{1,0:T(8,128)S(1)}, u32[]{:S(2)}, u32[]{:S(2)}) collective-permute-start(f32[128,128]{1,0:T(8,128)S(1)} %fusion), channel_id=1, source_target_pairs={{0,16},{1,65},{2,18},{3,67},{4,20},{5,69},{6,22},{7,71},{8,24},{9,... | collective-permute-start | bytes 196616 | tf_op jit(solution)/shard_map/ppermute | solution.py:316
  44.5 3.7 %collective-permute-start.17 = (f32[128,128]{1,0:T(8,128)S(1)}, f32[128,128]{1,0:T(8,128)S(1)}, u32[]{:S(2)}, u32[]{:S(2)}) collective-permute-start(f32[128,128]{1,0:T(8,128)S(1)} %fusion.19.refs_0_), channel_id=1, source_target_pairs={{0,1},{1,0},{2,3},{3,2},{4,5},{5,4},{6,7},{7,6},{8,9},{9,8},{10,11... | collective-permute-start | bytes 196616 | tf_op jit(solution)/shard_map/ppermute | solution.py:293
  45.1 3.1 %collective-permute-start.19 = (f32[128,128]{1,0:T(8,128)S(1)}, f32[128,128]{1,0:T(8,128)S(1)}, u32[]{:S(2)}, u32[]{:S(2)}) collective-permute-start(f32[128,128]{1,0:T(8,128)S(1)} %collective-permute-done.15.refs_2_), channel_id=1, source_target_pairs={{0,1},{1,0},{2,3},{3,2},{4,5},{5,4},{6,7},{7,6},{8,9},{9,8},{10,11... | collective-permute-start | bytes 196616 | tf_op jit(solution)/shard_map/ppermute | solution.py:293
  46.4 1.8 %collective-permute-start.20 = (f32[128,128]{1,0:T(8,128)S(1)}, f32[128,128]{1,0:T(8,128)S(1)}, u32[]{:S(2)}, u32[]{:S(2)}) collective-permute-start(f32[128,128]{1,0:T(8,128)S(1)} %collective-permute-done.16.refs_3_), channel_id=1, source_target_pairs={{0,1},{1,0},{2,3},{3,2},{4,5},{5,4},{6,7},{7,6},{8,9},{9,8},{10,11... | collective-permute-start | bytes 196616 | tf_op jit(solution)/shard_map/ppermute | solution.py:293
  47.9 1.3 %collective-permute-start.18 = (f32[128,128]{1,0:T(8,128)S(1)}, f32[128,128]{1,0:T(8,128)S(1)}, u32[]{:S(2)}, u32[]{:S(2)}) collective-permute-start(f32[128,128]{1,0:T(8,128)S(1)} %collective-permute-done.14.refs_1_), channel_id=1, source_target_pairs={{0,1},{1,0},{2,3},{3,2},{4,5},{5,4},{6,7},{7,6},{8,9},{9,8},{10,11... | collective-permute-start | bytes 196616 | tf_op jit(solution)/shard_map/ppermute | solution.py:293

commit v8 on v7

--- a/solution.py
+++ b/solution.py
@@ -382,9 +382,9 @@
     rows = jnp.concatenate([near] + [shifted(near, SECOND_AXIS, shift) for shift in SECOND_SHIFTS], axis=0)
     rows = rows.reshape(SIDE * SIDE * Q_TOK, HEADS // 2 * HEAD_DIM)
     distant = dot(rows[:, :cut], far[0]) + dot(rows[:, cut:half], far[1]) + dot(rows[:, half:], far[2])
-    distant = shifted(distant, WEIGHT_AXIS, -2)
-    pieces = [shifted(dot(rows, w), WEIGHT_AXIS, -shift) for w, shift in zip((before, after), SHIFTS)]
-    pieces = [dot(rows, out_weight), distant, *pieces]
+    distant = shifted(distant.astype(jnp.bfloat16), WEIGHT_AXIS, -2)
+    pieces = [shifted(dot(rows, w).astype(jnp.bfloat16), WEIGHT_AXIS, -shift) for w, shift in zip((before, after), SHIFTS)]
+    pieces = [dot(rows, out_weight)] + [p.astype(jnp.float32) for p in (distant, *pieces)]
     return assemble(pieces, [other_core(p) for p in pieces])
 
 

time: 50.2 us -> 49.9 us (level)
  waiting for transfers between devices: 12.8 us -> 11 us
  starting transfers between devices: 27.5 us -> 29.1 us
    ppermute x14, waiting for transfers between devices: 10.9 us -> 9.07 us  [shifted(): return lax.ppermute(x, ('group', 'kv'), moves)]
    ppermute x7, starting transfers between devices: 5.63 us -> 6.76 us  [other_core(): return lax.ppermute(x, 'kv', [(0, 1), (1, 0)])]
  transfers between devices with their start and end apart: 21 -> 21, of which waited for: 8 -> 7; matrix products, arithmetic and copies ran while one was open for 5% -> 5% of each run, Pallas kernels for 11% -> 11%
where the time goes in v8:
time: 49.9 us; the launch traced here: 49.8 us
  starting transfers between devices  29.1 us (58%)
  waiting for transfers between devices  11 us (22%)
  Pallas kernels  6.57 us (13%)
  matrix products  2 us (4%)
  between operations  0.82 us (2%)
    ppermute x14, starting transfers between devices, shifted(): return lax.ppermute(x, ('group', 'kv'), moves)  22.3 us
    ppermute x14, waiting for transfers between devices, shifted(): return lax.ppermute(x, ('group', 'kv'), moves)  9.07 us
    ppermute x7, starting transfers between devices, other_core(): return lax.ppermute(x, 'kv', [(0, 1), (1, 0)])  6.76 us
    pallas_call x1, Pallas kernels, attend(): pl.pallas_call(attend_kernel, out_shape=(shape, shape), in_specs=[pl.Bloc...  5.66 us
    dot_general x6, matrix products, dot(): return jnp.dot(a, b, preferred_element_type=jnp.float32)  2 us
    ppermute x7, waiting for transfers between devices, other_core(): return lax.ppermute(x, 'kv', [(0, 1), (1, 0)])  1.92 us
  transfers between devices with their start and end apart: 21, of which 7 were waited for; matrix products, arithmetic and copies ran while one was open for 5% of the time, Pallas kernels for 11%

profile of v8, /device:TPU:1, one launch (start us, length us, event | category | flops | bytes accessed | tf_op | source)
XLA Modules:
  0.0 49.8 jit_solution(9250671307068100340)
XLA Ops:
  0.0 2.5 %collective-permute-start.4 = (bf16[4096,128]{1,0:T(8,128)(2,1)}, bf16[4096,128]{1,0:T(8,128)(2,1)S(1)}, u32[]{:S(2)}, u32[]{:S(2)}) collective-permute-start(bf16[4096,128]{1,0:T(8,128)(2,1)} %param.18), channel_id=1, source_target_pairs={{0,8},{1,33},{2,10},{3,35},{4,12},{5,37},{6,14},{7,39},{8,16},{9,4... | collective-permute-start | bytes 3145736 | tf_op jit(solution)/shard_map/ppermute | solution.py:316
  2.5 2.1 %collective-permute-start.5 = (bf16[4096,128]{1,0:T(8,128)(2,1)}, bf16[4096,128]{1,0:T(8,128)(2,1)S(1)}, u32[]{:S(2)}, u32[]{:S(2)}) collective-permute-start(bf16[4096,128]{1,0:T(8,128)(2,1)} %param.18), channel_id=1, source_target_pairs={{0,24},{1,97},{2,26},{3,99},{4,28},{5,101},{6,30},{7,103},{8,0},{9... | collective-permute-start | bytes 3145736 | tf_op jit(solution)/shard_map/ppermute | solution.py:316
  5.2 5.7 %attend.1 = (f32[3,8,4096]{2,1,0:T(8,128)S(1)}, f32[3,8,4096]{2,1,0:T(8,128)S(1)}) custom-call(s32[1]{0:T(128)S(6)} %copy.17.length_ref, bf16[160,4096]{1,0:T(8,128)(2,1)} %bitcast.66, bf16[4096,1024]{1,0:T(8,128)(2,1)} %bitcast.65, f32[2,2,64,4096]{3,2,1,0:T(8,128)} %constant.7.clone.table_hbm, bf16[8,16]{1,0:T(8,128)(2,1)} %bitcast.70, ...), custom_call_target="tpu_custom_call" | custom-call | flops 3489660928 | bytes 12582912 | tf_op jit(solution)/shard_map/attend/pallas_call | solution.py:248
  10.9 3.3 %collective-permute-start.2 = (f32[8,4096]{1,0:T(8,128)S(1)}, f32[8,4096]{1,0:T(8,128)S(1)}, u32[]{:S(2)}, u32[]{:S(2)}) collective-permute-start(f32[8,4096]{1,0:T(8,128)S(1)} %get-tuple-element.20), channel_id=1, source_target_pairs={{0,1},{1,0},{2,3},{3,2},{4,5},{5,4},{6,7},{7,6},{8,9},{9,8},{10,11... | collective-permute-start | bytes 393224 | tf_op jit(solution)/shard_map/ppermute | solution.py:293
  14.8 0.5 collective-permute-done.2
  15.9 2.9 %collective-permute-start.3 = (bf16[1,8,4096]{2,1,0:T(8,128)(2,1)S(1)}, bf16[1,8,4096]{2,1,0:T(8,128)(2,1)S(1)}, u32[]{:S(2)}, u32[]{:S(2)}) collective-permute-start(bf16[1,8,4096]{2,1,0:T(8,128)(2,1)S(1)} %get-tuple-element.18), channel_id=1, source_target_pairs={{0,64},{1,5},{2,66},{3,7},{4,68},{5,1},{6,70},{7,3},{8,72},{9,13},... | collective-permute-start | bytes 196616 | tf_op jit(solution)/shard_map/ppermute | solution.py:316
  18.8 1.7 %collective-permute-start.6 = (bf16[256,128]{1,0:T(8,128)(2,1)S(1)}, bf16[256,128]{1,0:T(8,128)(2,1)S(1)}, u32[]{:S(2)}, u32[]{:S(2)}) collective-permute-start(bf16[256,128]{1,0:T(8,128)(2,1)S(1)} %slice.31), channel_id=1, source_target_pairs={{0,8},{1,33},{2,10},{3,35},{4,12},{5,37},{6,14},{7,39},{8,16},{9,4... | collective-permute-start | bytes 196616 | tf_op jit(solution)/shard_map/ppermute | solution.py:316
  20.9 2.4 %collective-permute-start.8 = (bf16[1,8,4096]{2,1,0:T(8,128)(2,1)S(1)}, bf16[1,8,4096]{2,1,0:T(8,128)(2,1)S(1)}, u32[]{:S(2)}, u32[]{:S(2)}) collective-permute-start(bf16[1,8,4096]{2,1,0:T(8,128)(2,1)S(1)} %get-tuple-element.18), channel_id=1, source_target_pairs={{0,96},{1,7},{2,98},{3,1},{4,100},{5,3},{6,102},{7,5},{8,104},{9,1... | collective-permute-start | bytes 196616 | tf_op jit(solution)/shard_map/ppermute | solution.py:316
  23.3 1.7 %collective-permute-start.13 = (bf16[2048,128]{1,0:T(8,128)(2,1)S(1)}, bf16[2048,128]{1,0:T(8,128)(2,1)S(1)}, u32[]{:S(2)}, u32[]{:S(2)}) collective-permute-start(bf16[2048,128]{1,0:T(8,128)(2,1)S(1)} %slice.36), channel_id=1, source_target_pairs={{0,8},{1,33},{2,10},{3,35},{4,12},{5,37},{6,14},{7,39},{8,16},{9,4... | collective-permute-start | bytes 1572872 | tf_op jit(solution)/shard_map/ppermute | solution.py:316
  25.0 1.1 %collective-permute-start.12 = (bf16[1792,128]{1,0:T(8,128)(2,1)S(1)}, bf16[1792,128]{1,0:T(8,128)(2,1)S(1)}, u32[]{:S(2)}, u32[]{:S(2)}) collective-permute-start(bf16[1792,128]{1,0:T(8,128)(2,1)S(1)} %slice.34), channel_id=1, source_target_pairs={{0,24},{1,97},{2,26},{3,99},{4,28},{5,101},{6,30},{7,103},{8,0},{9... | collective-permute-start | bytes 1376264 | tf_op jit(solution)/shard_map/ppermute | solution.py:316
  26.2 1.8 %collective-permute-start.9 = (bf16[4,8,4096]{2,1,0:T(8,128)(2,1)S(1)}, bf16[4,8,4096]{2,1,0:T(8,128)(2,1)S(1)}, u32[]{:S(2)}, u32[]{:S(2)}) collective-permute-start(bf16[4,8,4096]{2,1,0:T(8,128)(2,1)S(1)} %pad_maximum_fusion), channel_id=1, source_target_pairs={{0,4},{1,17},{2,6},{3,19},{4,0},{5,21},{6,2},{7,23},{8,12},{9,25},... | collective-permute-start | bytes 786440 | tf_op jit(solution)/shard_map/ppermute | solution.py:316
  28.4 2.3 %collective-permute-start.11 = (bf16[4,8,4096]{2,1,0:T(8,128)(2,1)S(1)}, bf16[4,8,4096]{2,1,0:T(8,128)(2,1)S(1)}, u32[]{:S(2)}, u32[]{:S(2)}) collective-permute-start(bf16[4,8,4096]{2,1,0:T(8,128)(2,1)S(1)} %pad_maximum_fusion), channel_id=1, source_target_pairs={{0,6},{1,25},{2,0},{3,27},{4,2},{5,29},{6,4},{7,31},{8,14},{9,1},{... | collective-permute-start | bytes 786440 | tf_op jit(solution)/shard_map/ppermute | solution.py:316
  30.7 5.1 %collective-permute-done.9 = bf16[4,8,4096]{2,1,0:T(8,128)(2,1)S(1)} collective-permute-done((bf16[4,8,4096]{2,1,0:T(8,128)(2,1)S(1)}, bf16[4,8,4096]{2,1,0:T(8,128)(2,1)S(1)}, u32[]{:S(2)}, u32[]{:S(2)}) %collective-permute-start.9) | collective-permute-done | bytes 262176 | tf_op jit(solution)/shard_map/ppermute | solution.py:316
  35.8 3.4 %collective-permute-done.10 = bf16[4,8,4096]{2,1,0:T(8,128)(2,1)S(1)} collective-permute-done((bf16[4,8,4096]{2,1,0:T(8,128)(2,1)S(1)}, bf16[4,8,4096]{2,1,0:T(8,128)(2,1)S(1)}, u32[]{:S(2)}, u32[]{:S(2)}) %collective-permute-start.10) | collective-permute-done | bytes 262176 | tf_op jit(solution)/shard_map/ppermute | solution.py:316
  39.3 0.4 convolution_convert_fusion.1
  39.7 1.6 %collective-permute-start.15 = (bf16[128,128]{1,0:T(8,128)(2,1)S(1)}, bf16[128,128]{1,0:T(8,128)(2,1)S(1)}, u32[]{:S(2)}, u32[]{:S(2)}) collective-permute-start(bf16[128,128]{1,0:T(8,128)(2,1)S(1)} %convolution_convert_fusion.1), channel_id=1, source_target_pairs={{0,24},{1,97},{2,26},{3,99},{4,28},{5,101},{6,30},{7,103},{8,0},{9... | collective-permute-start | bytes 98312 | tf_op jit(solution)/shard_map/ppermute | solution.py:316
  41.3 0.4 convolution_convert_fusion
  42.5 1.6 %collective-permute-start.14 = (bf16[128,128]{1,0:T(8,128)(2,1)S(1)}, bf16[128,128]{1,0:T(8,128)(2,1)S(1)}, u32[]{:S(2)}, u32[]{:S(2)}) collective-permute-start(bf16[128,128]{1,0:T(8,128)(2,1)S(1)} %fusion.1), channel_id=1, source_target_pairs={{0,16},{1,65},{2,18},{3,67},{4,20},{5,69},{6,22},{7,71},{8,24},{9,... | collective-permute-start | bytes 98312 | tf_op jit(solution)/shard_map/ppermute | solution.py:316
  44.5 0.6 %collective-permute-start.17 = (f32[128,128]{1,0:T(8,128)S(1)}, f32[128,128]{1,0:T(8,128)S(1)}, u32[]{:S(2)}, u32[]{:S(2)}) collective-permute-start(f32[128,128]{1,0:T(8,128)S(1)} %fusion.18.refs_0_), channel_id=1, source_target_pairs={{0,1},{1,0},{2,3},{3,2},{4,5},{5,4},{6,7},{7,6},{8,9},{9,8},{10,11... | collective-permute-start | bytes 196616 | tf_op jit(solution)/shard_map/ppermute | solution.py:293
  45.2 0.5 %collective-permute-done.16 = bf16[128,128]{1,0:T(8,128)(2,1)S(1)} collective-permute-done((bf16[128,128]{1,0:T(8,128)(2,1)S(1)}, bf16[128,128]{1,0:T(8,128)(2,1)S(1)}, u32[]{:S(2)}, u32[]{:S(2)}) %collective-permute-start.16) | collective-permute-done | bytes 32800 | tf_op jit(solution)/shard_map/ppermute | solution.py:316
  45.8 1.1 %collective-permute-start.20 = (f32[128,128]{1,0:T(8,128)S(1)}, f32[128,128]{1,0:T(8,128)S(1)}, u32[]{:S(2)}, u32[]{:S(2)}) collective-permute-start(f32[128,128]{1,0:T(8,128)S(1)} %convert_element_type.27.refs_3_), channel_id=1, source_target_pairs={{0,1},{1,0},{2,3},{3,2},{4,5},{5,4},{6,7},{7,6},{8,9},{9,8},{10,11... | collective-permute-start | bytes 196616 | tf_op jit(solution)/shard_map/ppermute | solution.py:293
  46.9 1.1 %collective-permute-start.18 = (f32[128,128]{1,0:T(8,128)S(1)}, f32[128,128]{1,0:T(8,128)S(1)}, u32[]{:S(2)}, u32[]{:S(2)}) collective-permute-start(f32[128,128]{1,0:T(8,128)S(1)} %convert_element_type.23.refs_1_), channel_id=1, source_target_pairs={{0,1},{1,0},{2,3},{3,2},{4,5},{5,4},{6,7},{7,6},{8,9},{9,8},{10,11... | collective-permute-start | bytes 196616 | tf_op jit(solution)/shard_map/ppermute | solution.py:293
  48.0 0.9 %collective-permute-done.18.refs_5_ = f32[128,128]{1,0:T(8,128)S(1)} collective-permute-done((f32[128,128]{1,0:T(8,128)S(1)}, f32[128,128]{1,0:T(8,128)S(1)}, u32[]{:S(2)}, u32[]{:S(2)}) %collective-permute-start.18) | collective-permute-done | bytes 65568 | tf_op jit(solution)/shard_map/ppermute | solution.py:293
  48.9 0.9 %assemble.1 = f32[256,128]{1,0:T(8,128)} custom-call(f32[128,128]{1,0:T(8,128)S(1)} %fusion.18.refs_0_, f32[128,128]{1,0:T(8,128)S(1)} %convert_element_type.23.refs_1_, f32[128,128]{1,0:T(8,128)S(1)} %convert_element_type.25.refs_2_, f32[128,128]{1,0:T(8,128)S(1)} %convert_element_type.27.refs_3_, f32[128,128]{1,0:T(8,128)S(1)} %collective-permute-done.17.refs_4_, ...), custom_call_target="tpu_custom_call" | custom-call | tf_op jit(solution)/shard_map/assemble/pallas_call | solution.py:354
  (43 shorter events, 3.4 us)
Async XLA Ops:
  0.0 18.8 %collective-permute-start.4 = (bf16[4096,128]{1,0:T(8,128)(2,1)}, bf16[4096,128]{1,0:T(8,128)(2,1)S(1)}, u32[]{:S(2)}, u32[]{:S(2)}) collective-permute-start(bf16[4096,128]{1,0:T(8,128)(2,1)} %param.18), channel_id=1, source_target_pairs={{0,8},{1,33},{2,10},{3,35},{4,12},{5,37},{6,14},{7,39},{8,16},{9,4... | collective-permute-start | bytes 3145736 | tf_op jit(solution)/shard_map/ppermute | solution.py:316
  2.5 16.4 %collective-permute-start.5 = (bf16[4096,128]{1,0:T(8,128)(2,1)}, bf16[4096,128]{1,0:T(8,128)(2,1)S(1)}, u32[]{:S(2)}, u32[]{:S(2)}) collective-permute-start(bf16[4096,128]{1,0:T(8,128)(2,1)} %param.18), channel_id=1, source_target_pairs={{0,24},{1,97},{2,26},{3,99},{4,28},{5,101},{6,30},{7,103},{8,0},{9... | collective-permute-start | bytes 3145736 | tf_op jit(solution)/shard_map/ppermute | solution.py:316
  10.9 4.3 %collective-permute-start.2 = (f32[8,4096]{1,0:T(8,128)S(1)}, f32[8,4096]{1,0:T(8,128)S(1)}, u32[]{:S(2)}, u32[]{:S(2)}) collective-permute-start(f32[8,4096]{1,0:T(8,128)S(1)} %get-tuple-element.20), channel_id=1, source_target_pairs={{0,1},{1,0},{2,3},{3,2},{4,5},{5,4},{6,7},{7,6},{8,9},{9,8},{10,11... | collective-permute-start | bytes 393224 | tf_op jit(solution)/shard_map/ppermute | solution.py:293
  14.3 1.3 %collective-permute-start.1 = (f32[8,4096]{1,0:T(8,128)S(1)}, f32[8,4096]{1,0:T(8,128)S(1)}, u32[]{:S(2)}, u32[]{:S(2)}) collective-permute-start(f32[8,4096]{1,0:T(8,128)S(1)} %get-tuple-element.21), channel_id=1, source_target_pairs={{0,1},{1,0},{2,3},{3,2},{4,5},{5,4},{6,7},{7,6},{8,9},{9,8},{10,11... | collective-permute-start | bytes 393224 | tf_op jit(solution)/shard_map/ppermute | solution.py:293
  14.4 1.4 %collective-permute-start = (f32[8,4096]{1,0:T(8,128)S(1)}, f32[8,4096]{1,0:T(8,128)S(1)}, u32[]{:S(2)}, u32[]{:S(2)}) collective-permute-start(f32[8,4096]{1,0:T(8,128)S(1)} %get-tuple-element.19), channel_id=1, source_target_pairs={{0,1},{1,0},{2,3},{3,2},{4,5},{5,4},{6,7},{7,6},{8,9},{9,8},{10,11... | collective-permute-start | bytes 393224 | tf_op jit(solution)/shard_map/ppermute | solution.py:293
  15.9 9.1 %collective-permute-start.3 = (bf16[1,8,4096]{2,1,0:T(8,128)(2,1)S(1)}, bf16[1,8,4096]{2,1,0:T(8,128)(2,1)S(1)}, u32[]{:S(2)}, u32[]{:S(2)}) collective-permute-start(bf16[1,8,4096]{2,1,0:T(8,128)(2,1)S(1)} %get-tuple-element.18), channel_id=1, source_target_pairs={{0,64},{1,5},{2,66},{3,7},{4,68},{5,1},{6,70},{7,3},{8,72},{9,13},... | collective-permute-start | bytes 196616 | tf_op jit(solution)/shard_map/ppermute | solution.py:316
  18.8 7.3 %collective-permute-start.6 = (bf16[256,128]{1,0:T(8,128)(2,1)S(1)}, bf16[256,128]{1,0:T(8,128)(2,1)S(1)}, u32[]{:S(2)}, u32[]{:S(2)}) collective-permute-start(bf16[256,128]{1,0:T(8,128)(2,1)S(1)} %slice.31), channel_id=1, source_target_pairs={{0,8},{1,33},{2,10},{3,35},{4,12},{5,37},{6,14},{7,39},{8,16},{9,4... | collective-permute-start | bytes 196616 | tf_op jit(solution)/shard_map/ppermute | solution.py:316
  20.6 5.6 %collective-permute-start.7 = (bf16[1,8,4096]{2,1,0:T(8,128)(2,1)S(1)}, bf16[1,8,4096]{2,1,0:T(8,128)(2,1)S(1)}, u32[]{:S(2)}, u32[]{:S(2)}) collective-permute-start(bf16[1,8,4096]{2,1,0:T(8,128)(2,1)S(1)} %get-tuple-element.18), channel_id=1, source_target_pairs={{0,32},{1,3},{2,34},{3,5},{4,36},{5,7},{6,38},{7,1},{8,40},{9,11},... | collective-permute-start | bytes 196616 | tf_op jit(solution)/shard_map/ppermute | solution.py:316
  20.9 5.3 %collective-permute-start.8 = (bf16[1,8,4096]{2,1,0:T(8,128)(2,1)S(1)}, bf16[1,8,4096]{2,1,0:T(8,128)(2,1)S(1)}, u32[]{:S(2)}, u32[]{:S(2)}) collective-permute-start(bf16[1,8,4096]{2,1,0:T(8,128)(2,1)S(1)} %get-tuple-element.18), channel_id=1, source_target_pairs={{0,96},{1,7},{2,98},{3,1},{4,100},{5,3},{6,102},{7,5},{8,104},{9,1... | collective-permute-start | bytes 196616 | tf_op jit(solution)/shard_map/ppermute | solution.py:316
  23.3 18.8 %collective-permute-start.13 = (bf16[2048,128]{1,0:T(8,128)(2,1)S(1)}, bf16[2048,128]{1,0:T(8,128)(2,1)S(1)}, u32[]{:S(2)}, u32[]{:S(2)}) collective-permute-start(bf16[2048,128]{1,0:T(8,128)(2,1)S(1)} %slice.36), channel_id=1, source_target_pairs={{0,8},{1,33},{2,10},{3,35},{4,12},{5,37},{6,14},{7,39},{8,16},{9,4... | collective-permute-start | bytes 1572872 | tf_op jit(solution)/shard_map/ppermute | solution.py:316
  25.0 16.8 %collective-permute-start.12 = (bf16[1792,128]{1,0:T(8,128)(2,1)S(1)}, bf16[1792,128]{1,0:T(8,128)(2,1)S(1)}, u32[]{:S(2)}, u32[]{:S(2)}) collective-permute-start(bf16[1792,128]{1,0:T(8,128)(2,1)S(1)} %slice.34), channel_id=1, source_target_pairs={{0,24},{1,97},{2,26},{3,99},{4,28},{5,101},{6,30},{7,103},{8,0},{9... | collective-permute-start | bytes 1376264 | tf_op jit(solution)/shard_map/ppermute | solution.py:316
  26.2 9.6 %collective-permute-start.9 = (bf16[4,8,4096]{2,1,0:T(8,128)(2,1)S(1)}, bf16[4,8,4096]{2,1,0:T(8,128)(2,1)S(1)}, u32[]{:S(2)}, u32[]{:S(2)}) collective-permute-start(bf16[4,8,4096]{2,1,0:T(8,128)(2,1)S(1)} %pad_maximum_fusion), channel_id=1, source_target_pairs={{0,4},{1,17},{2,6},{3,19},{4,0},{5,21},{6,2},{7,23},{8,12},{9,25},... | collective-permute-start | bytes 786440 | tf_op jit(solution)/shard_map/ppermute | solution.py:316
  28.0 11.2 %collective-permute-start.10 = (bf16[4,8,4096]{2,1,0:T(8,128)(2,1)S(1)}, bf16[4,8,4096]{2,1,0:T(8,128)(2,1)S(1)}, u32[]{:S(2)}, u32[]{:S(2)}) collective-permute-start(bf16[4,8,4096]{2,1,0:T(8,128)(2,1)S(1)} %pad_maximum_fusion), channel_id=1, source_target_pairs={{0,2},{1,9},{2,4},{3,11},{4,6},{5,13},{6,0},{7,15},{8,10},{9,17},{... | collective-permute-start | bytes 786440 | tf_op jit(solution)/shard_map/ppermute | solution.py:316
  28.4 10.9 %collective-permute-start.11 = (bf16[4,8,4096]{2,1,0:T(8,128)(2,1)S(1)}, bf16[4,8,4096]{2,1,0:T(8,128)(2,1)S(1)}, u32[]{:S(2)}, u32[]{:S(2)}) collective-permute-start(bf16[4,8,4096]{2,1,0:T(8,128)(2,1)S(1)} %pad_maximum_fusion), channel_id=1, source_target_pairs={{0,6},{1,25},{2,0},{3,27},{4,2},{5,29},{6,4},{7,31},{8,14},{9,1},{... | collective-permute-start | bytes 786440 | tf_op jit(solution)/shard_map/ppermute | solution.py:316
  30.7 13.4 %copy-start = (bf16[4096,128]{1,0:T(8,128)(2,1)S(1)}, bf16[4096,128]{1,0:T(8,128)(2,1)}, u32[]{:S(2)}) copy-start(bf16[4096,128]{1,0:T(8,128)(2,1)} %param.18) | copy-start | bytes 3145732
  39.7 5.4 %collective-permute-start.15 = (bf16[128,128]{1,0:T(8,128)(2,1)S(1)}, bf16[128,128]{1,0:T(8,128)(2,1)S(1)}, u32[]{:S(2)}, u32[]{:S(2)}) collective-permute-start(bf16[128,128]{1,0:T(8,128)(2,1)S(1)} %convolution_convert_fusion.1), channel_id=1, source_target_pairs={{0,24},{1,97},{2,26},{3,99},{4,28},{5,101},{6,30},{7,103},{8,0},{9... | collective-permute-start | bytes 98312 | tf_op jit(solution)/shard_map/ppermute | solution.py:316
  41.7 4.0 %collective-permute-start.16 = (bf16[128,128]{1,0:T(8,128)(2,1)S(1)}, bf16[128,128]{1,0:T(8,128)(2,1)S(1)}, u32[]{:S(2)}, u32[]{:S(2)}) collective-permute-start(bf16[128,128]{1,0:T(8,128)(2,1)S(1)} %convolution_convert_fusion), channel_id=1, source_target_pairs={{0,8},{1,33},{2,10},{3,35},{4,12},{5,37},{6,14},{7,39},{8,16},{9,4... | collective-permute-start | bytes 98312 | tf_op jit(solution)/shard_map/ppermute | solution.py:316
  42.5 4.3 %collective-permute-start.14 = (bf16[128,128]{1,0:T(8,128)(2,1)S(1)}, bf16[128,128]{1,0:T(8,128)(2,1)S(1)}, u32[]{:S(2)}, u32[]{:S(2)}) collective-permute-start(bf16[128,128]{1,0:T(8,128)(2,1)S(1)} %fusion.1), channel_id=1, source_target_pairs={{0,16},{1,65},{2,18},{3,67},{4,20},{5,69},{6,22},{7,71},{8,24},{9,... | collective-permute-start | bytes 98312 | tf_op jit(solution)/shard_map/ppermute | solution.py:316
  44.5 3.5 %collective-permute-start.17 = (f32[128,128]{1,0:T(8,128)S(1)}, f32[128,128]{1,0:T(8,128)S(1)}, u32[]{:S(2)}, u32[]{:S(2)}) collective-permute-start(f32[128,128]{1,0:T(8,128)S(1)} %fusion.18.refs_0_), channel_id=1, source_target_pairs={{0,1},{1,0},{2,3},{3,2},{4,5},{5,4},{6,7},{7,6},{8,9},{9,8},{10,11... | collective-permute-start | bytes 196616 | tf_op jit(solution)/shard_map/ppermute | solution.py:293
  45.1 2.9 %collective-permute-start.19 = (f32[128,128]{1,0:T(8,128)S(1)}, f32[128,128]{1,0:T(8,128)S(1)}, u32[]{:S(2)}, u32[]{:S(2)}) collective-permute-start(f32[128,128]{1,0:T(8,128)S(1)} %convert_element_type.25.refs_2_), channel_id=1, source_target_pairs={{0,1},{1,0},{2,3},{3,2},{4,5},{5,4},{6,7},{7,6},{8,9},{9,8},{10,11... | collective-permute-start | bytes 196616 | tf_op jit(solution)/shard_map/ppermute | solution.py:293
  45.8 2.3 %collective-permute-start.20 = (f32[128,128]{1,0:T(8,128)S(1)}, f32[128,128]{1,0:T(8,128)S(1)}, u32[]{:S(2)}, u32[]{:S(2)}) collective-permute-start(f32[128,128]{1,0:T(8,128)S(1)} %convert_element_type.27.refs_3_), channel_id=1, source_target_pairs={{0,1},{1,0},{2,3},{3,2},{4,5},{5,4},{6,7},{7,6},{8,9},{9,8},{10,11... | collective-permute-start | bytes 196616 | tf_op jit(solution)/shard_map/ppermute | solution.py:293
  46.9 2.0 %collective-permute-start.18 = (f32[128,128]{1,0:T(8,128)S(1)}, f32[128,128]{1,0:T(8,128)S(1)}, u32[]{:S(2)}, u32[]{:S(2)}) collective-permute-start(f32[128,128]{1,0:T(8,128)S(1)} %convert_element_type.23.refs_1_), channel_id=1, source_target_pairs={{0,1},{1,0},{2,3},{3,2},{4,5},{5,4},{6,7},{7,6},{8,9},{9,8},{10,11... | collective-permute-start | bytes 196616 | tf_op jit(solution)/shard_map/ppermute | solution.py:293
